TPU v7x, 32 devices: a whole 2x2x4 slice. The times are simulated.
32 devices in a mesh: ctx: 16 (over z, x, core), wsh: 2 (over y).
Axes of the slice: x: 2, y: 2, z: 4, core: 2. Of those that a mesh axis runs over, the one named last changes fastest.
Arguments:
- tokens: bfloat16 [2, 2048, 1024], P('wsh', 'ctx'), may hold values from -6 to 6
- out_cotangent: bfloat16 [2, 2048, 1024], P('wsh', 'ctx'), may hold values from -6 to 6
- norm_gains: float32 [2, 1024], replicated, may hold values from 0.5 to 1.5
- norm_biases: float32 [2, 1024], replicated, may hold values from -2 to 2
- qkv_weight: bfloat16 [1024, 3072], P('wsh'), may hold values from -0.1875 to 0.1875
- out_weight: bfloat16 [1024, 1024], P('wsh'), may hold values from -0.75 to 0.75
- up_weight: bfloat16 [1024, 4096], P('wsh'), may hold values from -0.1875 to 0.1875
- down_weight: bfloat16 [4096, 1024], P('wsh'), may hold values from -0.09375 to 0.09375
- proj_biases: float32 [9216], replicated, may hold values from -2 to 2
- adapters: float32 [8, 16, 16384], P(None, None, ('ctx', 'wsh')), may hold values from -0.12 to 0.12
- first_moment: float32 [8, 16, 16384], P(None, None, ('ctx', 'wsh')), may hold values from -64 to 64
- second_moment: float32 [8, 16, 16384], P(None, None, ('ctx', 'wsh')), may hold values from 6400 to 102400
- doc_starts: int32 [2, 1], P('wsh'), may hold values from 0 to 0, as said below
- doc_adapter: int32 [2, 1, 8], P('wsh'), may hold values from 0 to 1, as said below
- block_order: int32 [2, 32], P('wsh'), may hold values from 0 to 31, each once within a row
Outputs:
- block_out: bfloat16 [2, 2048, 1024], P('wsh', 'ctx')
- tokens_grad: float32 [2, 2048, 1024], P('wsh', 'ctx')
- adapter_grad: float32 [8, 16, 16384], P(None, None, ('ctx', 'wsh'))
- new_adapters: float32 [8, 16, 16384], P(None, None, ('ctx', 'wsh'))
- new_first: float32 [8, 16, 16384], P(None, None, ('ctx', 'wsh'))
- new_second: float32 [8, 16, 16384], P(None, None, ('ctx', 'wsh'))
- adapters_low: bfloat16 [8, 16, 16384], P(None, None, ('ctx', 'wsh'))
Inputs may be any that keep to these rules, and one draw needn't show every extreme that they name: `doc_starts`: per stream: ascending and starting at 0; a document runs from its start to the next start (the last to 2048) and has 1024 to 2048 tokens; one has exactly 2048; where a stream has several documents, the last has exactly 1024. `doc_adapter`: each document's row is one-hot. Each stream's row is a permutation; the device of ctx index c holds the stream's blocks block_order[2c] and block_order[2c + 1] of 64 tokens, in this order.
All inputs are finite; a program needn't handle non-finite values.
Results may differ from a plain program's by a relative error of at most 0.014.
Values may be sent and summed in bfloat16 or wider, within the bound.
No kernel may reach another device: no remote copies, remote signals or barrier semaphores. Data moves between devices by JAX's collectives and lax.ppermute only.
A program may use at most 384 MiB of HBM per device.

v0:
```python
import jax
import jax.numpy as jnp
from jax import lax
from jax.sharding import PartitionSpec as P

D = 1024
HEADS = 16
FF = 4096
HEAD_DIM = 64
ROT = 16
ADAPTERS = 8
RANK = 16
KEY_BLOCK = 512
STEP = 8


epsilon = 1e-05
adapter_scale = 8.0
rope_base = 10000.0
learn_rate = 0.02
beta_first = 0.5
beta_second = 0.5
weight_decay = 0.01
adam_epsilon = 1e-08
masked_value = -1e30


def layer_norm(values, gain_row, shift_row):
    center = values - jnp.mean(values, axis=-1, keepdims=True)
    spread = jnp.mean(center * center, axis=-1, keepdims=True)
    return center * lax.rsqrt(spread + epsilon) * gain_row + shift_row


def rotate_half(values):
    half_size = values.shape[-1] // 2
    return jnp.concatenate([-values[..., half_size:], values[..., :half_size]], axis=-1)


def rotary(values, cosine_table, sine_table):
    turned = values[..., :ROT]
    turned = turned * cosine_table[:, None, :] + rotate_half(turned) * sine_table[:, None, :]
    return jnp.concatenate([turned, values[..., ROT:]], axis=-1)


def rope_tables(place_rows):
    frequency = rope_base ** (-jnp.arange(0, ROT, 2, dtype=jnp.float32) / ROT)
    angles = place_rows.astype(jnp.float32)[:, None] * frequency[None, :]
    angles = jnp.concatenate([angles, angles], axis=1)
    return (jnp.cos(angles), jnp.sin(angles))


def token_layout(order_row, starts_row, adapter_rows, held_rows, total_rows, tok_dev):
    half_dev = tok_dev // 2
    owner_dev = held_rows // tok_dev
    within = held_rows % tok_dev
    slot_index = 2 * owner_dev + within // half_dev
    picked = (
        slot_index[:, None] == jnp.arange(order_row.shape[0], dtype=jnp.int32)[None, :]
    ).astype(jnp.int32)
    block_id = jnp.sum(picked * order_row[None, :], axis=1)
    stream_pos = block_id * half_dev + within % half_dev
    finish = jnp.concatenate([starts_row[1:], jnp.full((1,), total_rows, jnp.int32)])
    inside = (
        (stream_pos[:, None] >= starts_row[None, :]) & (stream_pos[:, None] < finish[None, :])
    ).astype(jnp.int32)
    doc_index = jnp.sum(inside * jnp.arange(starts_row.shape[0], dtype=jnp.int32)[None, :], axis=1)
    doc_place = stream_pos - jnp.sum(inside * starts_row[None, :], axis=1)
    chosen = jnp.sum(inside[:, :, None] * adapter_rows[None, :, :], axis=1)
    return (stream_pos, doc_index, doc_place, chosen)


def adapter_pair(low_adapters, in_start, in_width, out_start, out_width):
    down_part = low_adapters[:, :, in_start : in_start + in_width]
    up_term = low_adapters[:, :, out_start : out_start + out_width].reshape(
        ADAPTERS * RANK, out_width
    )
    return (down_part, up_term)


def frozen_forward(inputs_low, weight):
    return jnp.dot(inputs_low, weight, preferred_element_type=jnp.float32)


def frozen_backward(grad_low, weight):
    return jnp.einsum("to,io->ti", grad_low, weight, preferred_element_type=jnp.float32)


def project(inputs_low, weight, bias_vector, pair, column_mask):
    down_part, up_term = pair
    frozen_term = frozen_forward(inputs_low, weight)
    inner_product_rows = jnp.einsum(
        "ti,ari->tar", inputs_low, down_part, preferred_element_type=jnp.float32
    )
    inner_reduced = (
        inner_product_rows.reshape(inputs_low.shape[0], ADAPTERS * RANK) * column_mask
    ).astype(jnp.bfloat16)
    result = (
        frozen_term
        + bias_vector
        + adapter_scale * jnp.dot(inner_reduced, up_term, preferred_element_type=jnp.float32)
    )
    return (result, inner_reduced)


def project_back(inputs_low, weight, pair, column_mask, inner_reduced, grad_low):
    down_part, up_term = pair
    row_total = inputs_low.shape[0]
    grad_inputs = frozen_backward(grad_low, weight)
    inner_gradient = adapter_scale * jnp.einsum(
        "to,ko->tk", grad_low, up_term, preferred_element_type=jnp.float32
    )
    grad_split = (
        (inner_gradient * column_mask).astype(jnp.bfloat16).reshape(row_total, ADAPTERS, RANK)
    )
    grad_inputs = grad_inputs + jnp.einsum(
        "tar,ari->ti", grad_split, down_part, preferred_element_type=jnp.float32
    )
    grad_down = jnp.einsum(
        "ti,tar->ari", inputs_low, grad_split, preferred_element_type=jnp.float32
    )
    up_gradient = adapter_scale * jnp.einsum(
        "tk,to->ko", inner_reduced, grad_low, preferred_element_type=jnp.float32
    )
    return (grad_inputs, grad_down, up_gradient.reshape(ADAPTERS, RANK, -1))


def masked_scores(query_blk, key_blk, query_pos, query_doc, key_pos, key_doc):
    scores = jnp.einsum(
        "qhd,khd->qhk", query_blk, key_blk, preferred_element_type=jnp.float32
    ) * HEAD_DIM ** (-0.5)
    allowed = (query_doc[:, None] == key_doc[None, :]) & (key_pos[None, :] <= query_pos[:, None])
    return jnp.where(allowed[:, None, :], scores, masked_value)


def on_device(
    tokens,
    out_cotangent,
    norm_gains,
    norm_biases,
    qkv_weight,
    out_weight,
    up_weight,
    down_weight,
    proj_biases,
    adapters,
    first_moment,
    second_moment,
    doc_starts,
    doc_adapter,
    block_order,
):
    ctx_count = lax.axis_size("ctx")
    tok_dev = tokens.shape[1]
    total_rows = tok_dev * ctx_count
    first_row = lax.axis_index("ctx") * tok_dev
    score_scale = HEAD_DIM ** (-0.5)
    low_adapters = lax.all_gather(adapters.astype(jnp.bfloat16), ("ctx", "wsh"), axis=2, tiled=True)
    w_qkv, w_out, w_up, w_down = (
        lax.all_gather(qkv_weight, "wsh", axis=0, tiled=True),
        lax.all_gather(out_weight, "wsh", axis=0, tiled=True),
        lax.all_gather(up_weight, "wsh", axis=0, tiled=True),
        lax.all_gather(down_weight, "wsh", axis=0, tiled=True),
    )
    every_row = jnp.arange(total_rows, dtype=jnp.int32)
    all_layout = token_layout(
        block_order[0], doc_starts[0], doc_adapter[0], every_row, total_rows, tok_dev
    )
    all_pos = all_layout[0]
    all_doc = all_layout[1]
    my_rows = first_row + jnp.arange(tok_dev, dtype=jnp.int32)
    my_pos, my_doc, my_place, my_chosen = token_layout(
        block_order[0], doc_starts[0], doc_adapter[0], my_rows, total_rows, tok_dev
    )
    column_mask = jnp.repeat(my_chosen.astype(jnp.float32), RANK, axis=1)
    qkv_pair = adapter_pair(low_adapters, 0, D, 3 * D + FF, 3 * D)
    out_pair = adapter_pair(low_adapters, D, D, 6 * D + FF, D)
    up_pair = adapter_pair(low_adapters, 2 * D, D, 7 * D + FF, FF)
    down_pair = adapter_pair(low_adapters, 3 * D, FF, 7 * D + 2 * FF, D)
    inputs = tokens[0].astype(jnp.float32)
    norm_attn, norm_attn_back = jax.vjp(
        lambda values: layer_norm(values, norm_gains[0], norm_biases[0]), inputs
    )
    h_attn = norm_attn.astype(jnp.bfloat16)
    qkv_full, inner_qkv = project(h_attn, w_qkv, proj_biases[0 : 3 * D], qkv_pair, column_mask)
    cosine_table, sine_table = rope_tables(my_place)
    queries = rotary(
        qkv_full[:, 0:D].reshape(tok_dev, HEADS, HEAD_DIM), cosine_table, sine_table
    ).astype(jnp.bfloat16)
    keys_mine = rotary(
        qkv_full[:, D : 2 * D].reshape(tok_dev, HEADS, HEAD_DIM), cosine_table, sine_table
    ).astype(jnp.bfloat16)
    values_mine = qkv_full[:, 2 * D : 3 * D].astype(jnp.bfloat16)
    keys_all, values_all = (
        lax.all_gather(keys_mine.reshape(tok_dev, D), "ctx", axis=0, tiled=True),
        lax.all_gather(values_mine, "ctx", axis=0, tiled=True),
    )
    norm_mlp, norm_mlp_back = jax.vjp(
        lambda values: layer_norm(values, norm_gains[1], norm_biases[1]), inputs
    )
    h_mlp = norm_mlp.astype(jnp.bfloat16)
    up_full, inner_up = project(h_mlp, w_up, proj_biases[4 * D : 4 * D + FF], up_pair, column_mask)
    gelu_out, gelu_back = jax.vjp(lambda values: jax.nn.gelu(values, approximate=False), up_full)
    hidden_low = gelu_out.astype(jnp.bfloat16)
    mlp_out, inner_down = project(
        hidden_low, w_down, proj_biases[4 * D + FF : 5 * D + FF], down_pair, column_mask
    )
    key_count = total_rows // KEY_BLOCK
    key_stack = keys_all.reshape(key_count, KEY_BLOCK, HEADS, HEAD_DIM)
    value_stack = values_all.reshape(key_count, KEY_BLOCK, HEADS, HEAD_DIM)
    pos_stack = all_pos.reshape(key_count, KEY_BLOCK)
    doc_stack = all_doc.reshape(key_count, KEY_BLOCK)

    def lse_step(running, block_item):
        running_top, running_sum = running
        key_blk, key_pos, key_doc = block_item
        scores = masked_scores(queries, key_blk, my_pos, my_doc, key_pos, key_doc)
        new_top = jnp.maximum(running_top, jnp.max(scores, axis=-1))
        running_sum = running_sum * jnp.exp(running_top - new_top) + jnp.sum(
            jnp.exp(scores - new_top[..., None]), axis=-1
        )
        return ((new_top, running_sum), None)

    lse_start = (
        jnp.full((tok_dev, HEADS), masked_value, jnp.float32),
        jnp.zeros((tok_dev, HEADS), jnp.float32),
    )
    lse_state = lax.scan(lse_step, lse_start, (key_stack, pos_stack, doc_stack))[0]
    log_total = lse_state[0] + jnp.log(lse_state[1])

    def out_step(running, block_item):
        key_blk, value_blk, key_pos, key_doc = block_item
        scores = masked_scores(queries, key_blk, my_pos, my_doc, key_pos, key_doc)
        weights_low = jnp.exp(scores - log_total[..., None]).astype(jnp.bfloat16)
        return (
            running
            + jnp.einsum(
                "qhk,khd->qhd", weights_low, value_blk, preferred_element_type=jnp.float32
            ),
            None,
        )

    zero_heads = jnp.zeros((tok_dev, HEADS, HEAD_DIM), jnp.float32)
    attended = lax.scan(out_step, zero_heads, (key_stack, value_stack, pos_stack, doc_stack))[0]
    attended_low = attended.astype(jnp.bfloat16).reshape(tok_dev, D)
    attn_out, inner_out = project(
        attended_low, w_out, proj_biases[3 * D : 4 * D], out_pair, column_mask
    )
    block_out = (inputs + attn_out + mlp_out).astype(jnp.bfloat16)
    grad_low = out_cotangent[0]
    grad_hidden, down_grad_a, down_grad_b = project_back(
        hidden_low, w_down, down_pair, column_mask, inner_down, grad_low
    )
    grad_up_low = gelu_back(grad_hidden)[0].astype(jnp.bfloat16)
    grad_h_mlp, up_grad_a, up_grad_b = project_back(
        h_mlp, w_up, up_pair, column_mask, inner_up, grad_up_low
    )
    grad_attended, out_grad_a, out_grad_b = project_back(
        attended_low, w_out, out_pair, column_mask, inner_out, grad_low
    )
    grad_att_low = grad_attended.astype(jnp.bfloat16).reshape(tok_dev, HEADS, HEAD_DIM)
    row_delta = jnp.sum(grad_att_low.astype(jnp.float32) * attended, axis=-1)

    def query_grad_step(running, block_item):
        key_blk, value_blk, key_pos, key_doc = block_item
        scores = masked_scores(queries, key_blk, my_pos, my_doc, key_pos, key_doc)
        weights_exp = jnp.exp(scores - log_total[..., None])
        grad_weights = jnp.einsum(
            "qhd,khd->qhk", grad_att_low, value_blk, preferred_element_type=jnp.float32
        )
        grad_scores = (weights_exp * (grad_weights - row_delta[..., None])).astype(jnp.bfloat16)
        return (
            running
            + jnp.einsum("qhk,khd->qhd", grad_scores, key_blk, preferred_element_type=jnp.float32),
            None,
        )

    grad_query_sum = lax.scan(
        query_grad_step, zero_heads, (key_stack, value_stack, pos_stack, doc_stack)
    )[0]
    size_sub = KEY_BLOCK

    def one_block(offset):
        key_blk = lax.dynamic_slice_in_dim(keys_all, offset, size_sub).reshape(
            size_sub, HEADS, HEAD_DIM
        )
        value_blk = lax.dynamic_slice_in_dim(values_all, offset, size_sub).reshape(
            size_sub, HEADS, HEAD_DIM
        )
        key_pos = lax.dynamic_slice_in_dim(all_pos, offset, size_sub)
        key_doc = lax.dynamic_slice_in_dim(all_doc, offset, size_sub)
        scores = masked_scores(queries, key_blk, my_pos, my_doc, key_pos, key_doc)
        weights_exp = jnp.exp(scores - log_total[..., None])
        grad_weights = jnp.einsum(
            "qhd,khd->qhk", grad_att_low, value_blk, preferred_element_type=jnp.float32
        )
        grad_scores = (weights_exp * (grad_weights - row_delta[..., None])).astype(jnp.bfloat16)
        grad_values = jnp.einsum(
            "qhk,qhd->khd",
            weights_exp.astype(jnp.bfloat16),
            grad_att_low,
            preferred_element_type=jnp.float32,
        )
        grad_keys = (
            jnp.einsum("qhk,qhd->khd", grad_scores, queries, preferred_element_type=jnp.float32)
            * score_scale
        )
        return jnp.concatenate(
            [grad_keys.reshape(size_sub, D), grad_values.reshape(size_sub, D)], axis=1
        )

    offsets = jnp.arange(tok_dev * lax.axis_size("ctx") // size_sub, dtype=jnp.int32) * size_sub
    key_sums = lax.psum_scatter(
        lax.map(one_block, offsets).reshape(tok_dev * lax.axis_size("ctx"), 2 * D),
        "ctx",
        scatter_dimension=0,
        tiled=True,
    )
    grad_key_sum = key_sums[:, 0:D].reshape(tok_dev, HEADS, HEAD_DIM)
    grad_value_sum = key_sums[:, D : 2 * D].reshape(tok_dev, HEADS, HEAD_DIM)
    grad_queries = (grad_query_sum * score_scale).astype(jnp.bfloat16).astype(jnp.float32)
    grad_keys_low = grad_key_sum.astype(jnp.bfloat16).astype(jnp.float32)
    grad_qkv = jnp.concatenate(
        [
            rotary(grad_queries, cosine_table, -sine_table).reshape(tok_dev, D),
            rotary(grad_keys_low, cosine_table, -sine_table).reshape(tok_dev, D),
            grad_value_sum.reshape(tok_dev, D),
        ],
        axis=1,
    ).astype(jnp.bfloat16)
    grad_h_attn, qkv_grad_a, qkv_grad_b = project_back(
        h_attn, w_qkv, qkv_pair, column_mask, inner_qkv, grad_qkv
    )
    tokens_grad = (
        grad_low.astype(jnp.float32) + norm_attn_back(grad_h_attn)[0] + norm_mlp_back(grad_h_mlp)[0]
    )
    flat_grad = jnp.concatenate(
        [
            qkv_grad_a,
            out_grad_a,
            up_grad_a,
            down_grad_a,
            qkv_grad_b,
            out_grad_b,
            up_grad_b,
            down_grad_b,
        ],
        axis=2,
    )
    summed = lax.psum_scatter(flat_grad, ("ctx", "wsh"), scatter_dimension=2, tiled=True)
    new_first = beta_first * first_moment + (1.0 - beta_first) * summed
    new_second = beta_second * second_moment + (1.0 - beta_second) * summed * summed
    first_hat = new_first / (1.0 - beta_first**STEP)
    second_hat = new_second / (1.0 - beta_second**STEP)
    new_adapters = adapters - learn_rate * (
        first_hat / (jnp.sqrt(second_hat) + adam_epsilon) + weight_decay * adapters
    )
    return (
        block_out[None],
        tokens_grad[None],
        summed,
        new_adapters,
        new_first,
        new_second,
        new_adapters.astype(jnp.bfloat16),
    )


def solution(mesh):
    in_specs = (
        P("wsh", "ctx", None),
        P("wsh", "ctx", None),
        P(),
        P(),
        P("wsh", None),
        P("wsh", None),
        P("wsh", None),
        P("wsh", None),
        P(),
        P(None, None, ("ctx", "wsh")),
        P(None, None, ("ctx", "wsh")),
        P(None, None, ("ctx", "wsh")),
        P("wsh", None),
        P("wsh", None, None),
        P("wsh", None),
    )
    out_specs = (
        P("wsh", "ctx", None),
        P("wsh", "ctx", None),
        P(None, None, ("ctx", "wsh")),
        P(None, None, ("ctx", "wsh")),
        P(None, None, ("ctx", "wsh")),
        P(None, None, ("ctx", "wsh")),
        P(None, None, ("ctx", "wsh")),
    )
    return jax.shard_map(
        on_device, mesh=mesh, in_specs=in_specs, out_specs=out_specs, check_vma=False
    )
```

profile of v0, /device:TPU:1, one launch (start us, length us, event | category | flops | bytes accessed | tf_op | source)
XLA Modules:
  0.0 902.4 jit_solution(16261884112844090415)
XLA Ops:
  13.0 79.2 %all-gather.8.cloned.1.call-done = bf16[1024,3072]{1,0:T(8,128)(2,1)} async-done(((bf16[512,3072]{1,0:T(8,128)(2,1)}), bf16[1024,3072]{1,0:T(8,128)(2,1)}) %all-gather.8.cloned.1.call-update) | async-done | bytes 6291472 | tf_op jit(solution)/shard_map/all_gather | solution.py:159
  96.0 64.0 %all-gather.10.cloned.1.call-done = bf16[8,16,16384]{2,1,0:T(8,128)(2,1)} async-done(((bf16[8,16,512]{2,1,0:T(8,128)(2,1)}), bf16[8,16,16384]{2,1,0:T(8,128)(2,1)}) %all-gather.10.cloned.1.call-update) | async-done | bytes 4194320 | tf_op jit(solution)/shard_map/all_gather | solution.py:157
  172.6 19.9 %all-gather.16.cloned.1.call-done = bf16[1024,1024]{1,0:T(8,128)(2,1)} async-done(((bf16[512,1024]{1,0:T(8,128)(2,1)}), bf16[1024,1024]{1,0:T(8,128)(2,1)}) %all-gather.16.cloned.1.call-update) | async-done | bytes 2097168 | tf_op jit(solution)/shard_map/all_gather | solution.py:160
  195.2 53.7 %all-gather.14.cloned.1.call-done = bf16[2048,1024]{0,1:T(8,128)(2,1)} async-done(((bf16[128,1024]{0,1:T(8,128)(2,1)}), bf16[2048,1024]{0,1:T(8,128)(2,1)}) %all-gather.14.cloned.1.call-update) | async-done | bytes 4194320 | tf_op jit(solution)/shard_map/all_gather | solution.py:194
  248.8 7.8 reshape.684
  261.9 32.9 %while.50 = (s32[]{:T(128)}, f32[128,16]{0,1:T(8,128)S(1)}, f32[128,16]{0,1:T(8,128)S(1)}, s32[4,512]{1,0:T(4,128)}, s32[128]{0:T(128)S(1)}, /*index=5*/bf16[4,5...) while((s32[]{:T(128)}, f32[128,16]{0,1:T(8,128)S(1)}, ...), condition=%wide.region_7.8_spmd.clone, body=%wide.region_4.7_spmd.clone.sunk | while | flops 141633536 | bytes 10009708 | solution.py:227
  294.8 5.5 all-gather.12.cloned.1.call-done
  300.3 6.5 copy.81
  306.8 8.2 reshape.682
  315.1 5.5 copy.85
  320.6 16.6 %while.51 = (s32[]{:T(128)}, f32[128,16,64]{0,2,1:T(8,128)S(1)}, bf16[4,512,16,64]{1,3,2,0:T(8,128)(2,1)}, s32[4,512]{1,0:T(4,128)}, s32[128]{0:T(128)S(1)}, /*i...) while((s32[]{:T(128)}, f32[128,16,64]{0,2,1:T(8,128)S(1)}, ...), condition=%wide.region_9.10_spmd.clone, body=%wide.region_8.9_spmd.clone.sunk | while | flops 272957440 | bytes 3554931 | solution.py:243
  338.0 120.5 %while.49 = (s32[]{:T(128)}, f32[4,512,2048]{2,1,0:T(8,128)}, s32[4]{0:T(128)S(1)}, s32[2048]{0:T(1024)S(1)}, s32[128]{0:T(128)S(1)}, /*index=5*/bf16[2048,1024]...) while((s32[]{:T(128)}, f32[4,512,2048]{2,1,0:T(8,128)}, ...), condition=%wide.region_14.15_spmd, body=%wide.region_13.14_spmd.sunk | while | flops 548995072 | bytes 49577384 | solution.py:313
  418.1 5.7 copy.114
  466.8 6.5 multiply_convert_fusion
  476.5 32.9 %all-gather.20.cloned.1.call-done = bf16[4096,1024]{1,0:T(8,128)(2,1)} async-done(((bf16[2048,1024]{1,0:T(8,128)(2,1)}), bf16[4096,1024]{1,0:T(8,128)(2,1)}) %all-gather.20.cloned.1.call-update) | async-done | bytes 8388624 | tf_op jit(solution)/shard_map/all_gather | solution.py:162
  509.4 6.4 fusion.126
  521.3 45.3 %while.52 = (s32[]{:T(128)}, f32[128,16,64]{0,2,1:T(8,128)}, bf16[4,512,16,64]{1,3,2,0:T(8,128)(2,1)}, s32[4,512]{1,0:T(4,128)}, s32[128]{0:T(128)S(1)}, /*index...) while((s32[]{:T(128)}, f32[128,16,64]{0,2,1:T(8,128)}, ...), condition=%wide.region_12.13_spmd.clone, body=%wide.region_11.12_spmd.clone.sunk | while | flops 409272320 | bytes 13262979 | solution.py:277
  526.5 6.6 fusion.292
  538.5 6.3 fusion.292
  549.6 6.3 fusion.292
  560.7 5.6 fusion.292
  572.0 120.1 %reduce-scatter.3.cloned.1.call-done = f32[128,2048]{1,0:T(8,128)} async-done(((f32[2048,2048]{1,0:T(8,128)}), f32[128,2048]{1,0:T(8,128)}) %reduce-scatter.3.cloned.1.call-update) | async-done | bytes 1048592 | tf_op jit(solution)/shard_map/reduce_scatter | solution.py:312
  718.6 6.3 fusion.195
  733.0 160.4 %reduce-scatter.5.cloned.1.call-done = f32[8,16,512]{2,1,0:T(8,128)} async-done(((f32[8,16,16384]{2,1,0:T(8,128)}), f32[8,16,512]{2,1,0:T(8,128)}) %reduce-scatter.5.cloned.1.call-update) | async-done | bytes 262160 | tf_op jit(solution)/shard_map/reduce_scatter | solution.py:349
  (387 shorter events, 264.2 us)
Async XLA Ops:
  7.2 84.9 %slice-start.2 = ((f32[9216]{0:T(1024)}), f32[3072]{0:T(1024)S(1)}, s32[]{:S(2)}) async-start(f32[9216]{0:T(1024)} %param.31), calls=%async_computation.13 | async-start | bytes 24576 | tf_op jit(solution)/shard_map/slice | solution.py:184
  7.2 84.9 %all-gather.8.cloned.1.call-start = ((), (), s32[]{:S(2)}) async-start(), calls=%async_computation.2 | async-start | bytes 9437184 | tf_op jit(solution)/shard_map/all_gather | solution.py:159
  8.0 152.1 %all-gather.10.cloned.1.call-start = ((), (), s32[]{:S(2)}) async-start(), calls=%async_computation.3 | async-start | bytes 4325376 | tf_op jit(solution)/shard_map/all_gather | solution.py:157
  8.8 183.7 %all-gather.16.cloned.1.call-start = ((), (), s32[]{:S(2)}) async-start(), calls=%async_computation.6 | async-start | bytes 3145728 | tf_op jit(solution)/shard_map/all_gather | solution.py:160
  9.6 239.3 %all-gather.14.cloned.1.call-start = ((), (), s32[]{:S(2)}) async-start(), calls=%async_computation.5 | async-start | bytes 4456448 | tf_op jit(solution)/shard_map/all_gather | solution.py:194
  10.6 153.1 %copy-start.30 = (f32[128,128]{1,0:T(8,128)}, f32[128,128]{1,0:T(8,128)S(1)}, u32[]{:S(2)}) copy-start(f32[128,128]{1,0:T(8,128)S(1)} %copy.80) | copy-start | bytes 196612
  10.8 153.0 %copy-start.46 = (f32[128]{0:T(128)}, f32[128]{0:T(128)S(1)}, u32[]{:S(2)}) copy-start(f32[128]{0:T(128)S(1)} %broadcast_multiply_fusion.2) | copy-start | bytes 1540
  11.6 152.1 %copy-start.55 = (f32[128]{0:T(128)}, f32[128]{0:T(128)S(1)}, u32[]{:S(2)}) copy-start(f32[128]{0:T(128)S(1)} %fusion.171) | copy-start | bytes 1540
  11.7 152.1 %copy-start.32 = (f32[1,1024]{1,0:T(1,128)}, f32[1,1024]{1,0:T(1,128)S(1)}, u32[]{:S(2)}) copy-start(f32[1,1024]{1,0:T(1,128)S(1)} %get-tuple-element.642) | copy-start | bytes 12292
  12.3 151.5 %copy-start.41 = (f32[1,1024]{1,0:T(1,128)}, f32[1,1024]{1,0:T(1,128)S(1)}, u32[]{:S(2)}) copy-start(f32[1,1024]{1,0:T(1,128)S(1)} %get-tuple-element.644) | copy-start | bytes 12292
  13.0 153.2 %copy-start.43 = (f32[128,16]{0,1:T(8,128)}, f32[128,16]{0,1:T(8,128)S(1)}, u32[]{:S(2)}) copy-start(f32[128,16]{0,1:T(8,128)S(1)} %get-tuple-element.648) | copy-start | bytes 24580
  167.0 133.3 %all-gather.12.cloned.1.call-start = ((), (), s32[]{:S(2)}) async-start(), calls=%async_computation.4 | async-start | bytes 4456448 | tf_op jit(solution)/shard_map/all_gather | solution.py:195
  168.9 293.1 %all-gather.18.cloned.1.call-start = ((), (), s32[]{:S(2)}) async-start(), calls=%async_computation.7 | async-start | bytes 12582912 | tf_op jit(solution)/shard_map/all_gather | solution.py:161
  169.5 339.9 %all-gather.20.cloned.1.call-start = ((), (), s32[]{:S(2)}) async-start(), calls=%async_computation.8 | async-start | bytes 12582912 | tf_op jit(solution)/shard_map/all_gather | solution.py:162
  170.3 521.9 %reduce-scatter.3.cloned.1.call-start = ((), (), s32[]{:S(2)}) async-start(), calls=%async_computation.9 | async-start | bytes 17825792 | tf_op jit(solution)/shard_map/reduce_scatter | solution.py:312
  171.4 23.7 %copy-start.22 = (bf16[128,128]{0,1:T(8,128)(2,1)}, bf16[128,128]{0,1:T(8,128)(2,1)S(1)}, u32[]{:S(2)}) copy-start(bf16[128,128]{0,1:T(8,128)(2,1)S(1)} %fusion.84) | copy-start | bytes 98308
  458.5 434.9 %reduce-scatter.5.cloned.1.call-start = ((), (), s32[]{:S(2)}) async-start(), calls=%async_computation.10 | async-start | bytes 8650752 | tf_op jit(solution)/shard_map/reduce_scatter | solution.py:349
  476.5 39.3 %copy-start.37 = (bf16[128,128]{0,1:T(8,128)(2,1)S(1)}, bf16[128,128]{0,1:T(8,128)(2,1)}, u32[]{:S(2)}) copy-start(bf16[128,128]{0,1:T(8,128)(2,1)} %fusion.83) | copy-start | bytes 98308
  570.9 123.5 %copy-start.25 = (bf16[128,128]{1,0:T(8,128)(2,1)}, bf16[128,128]{1,0:T(8,128)(2,1)S(1)}, u32[]{:S(2)}) copy-start(bf16[128,128]{1,0:T(8,128)(2,1)S(1)} %fusion.89) | copy-start | bytes 98308
  572.0 123.2 %copy-start.44 = (f32[128,16]{0,1:T(8,128)S(1)}, f32[128,16]{0,1:T(8,128)}, u32[]{:S(2)}) copy-start(f32[128,16]{0,1:T(8,128)} %copy-done.43) | copy-start | bytes 24580
  712.4 15.4 %slice-start = ((s8[6291456]{0:T(1024)(128)(4,1)}), s8[4194304]{0:T(1024)(128)(4,1)S(1)}, s32[]{:S(2)}) async-start(s8[6291456]{0:T(1024)(128)(4,1)} %bitcast.388), calls=%async_computation.11 | async-start | bytes 8388608
  731.4 162.0 %copy-start.14 = (f32[8,16,512]{2,1,0:T(8,128)S(1)}, f32[8,16,512]{2,1,0:T(8,128)}, u32[]{:S(2)}) copy-start(f32[8,16,512]{2,1,0:T(8,128)} %param.32) | copy-start | bytes 786436
  731.4 162.0 %copy-start.27 = (f32[8,16,512]{2,1,0:T(8,128)S(1)}, f32[8,16,512]{2,1,0:T(8,128)}, u32[]{:S(2)}) copy-start(f32[8,16,512]{2,1,0:T(8,128)} %param.33) | copy-start | bytes 786436
  731.4 162.0 %copy-start.28 = (f32[8,16,512]{2,1,0:T(8,128)S(1)}, f32[8,16,512]{2,1,0:T(8,128)}, u32[]{:S(2)}) copy-start(f32[8,16,512]{2,1,0:T(8,128)} %param.34) | copy-start | bytes 786436
  (72 other events, 268.3 us)
Sparse Core Ops, SparseCore 0:
  9.6 82.4 all-gather.7
  95.6 64.4 all-gather.9
  161.6 30.8 all-gather.15
  195.1 53.6 all-gather.13
  251.4 48.8 all-gather.11
  301.7 102.0 all-gather.17
  405.4 103.9 all-gather.19
  513.5 178.5 reduce-scatter.2
  711.8 181.5 reduce-scatter.4
where the time goes:
time: 915 us; the launch traced here: 902 us
  waiting for transfers between devices  538 us (59%)
  matrix products  179 us (20%)
  local copies, waits for them, and re-layouts  121 us (13%)
  other arithmetic  38.9 us (4%)
  between operations  16.1 us (2%)
    reduce_scatter x1, waiting for transfers between devices, on_device(): lax.psum_scatter(flat_grad, ('ctx', 'wsh'), scatter_dimension=2, tiled=True)  160 us
    reduce_scatter x1, waiting for transfers between devices, on_device(): lax.psum_scatter(lax.map(one_block, offsets).reshape(tok_dev * lax.axis_s...  120 us
    all_gather x1, waiting for transfers between devices, on_device(): lax.all_gather(qkv_weight, 'wsh', axis=0, tiled=True)  79.2 us
    all_gather x1, waiting for transfers between devices, on_device(): lax.all_gather(adapters.astype(jnp.bfloat16), ('ctx', 'wsh'), axis=2, til...  64 us
    all_gather x1, waiting for transfers between devices, on_device(): lax.all_gather(keys_mine.reshape(tok_dev, D), 'ctx', axis=0, tiled=True)  53.7 us
    dot_general x12, matrix products, masked_scores(): jnp.einsum('qhd,khd->qhk', query_blk, key_blk, preferred_element_type=jnp...  44.3 us
    dynamic_update_slice x8, local copies, waits for them, and re-layouts, on_device(): lax.map(one_block, offsets).reshape(tok_dev * lax.axis_size('ctx'), 2 * D)  41.2 us
    all_gather x1, waiting for transfers between devices, on_device(): lax.all_gather(down_weight, 'wsh', axis=0, tiled=True)  32.9 us
  transfers between devices with their start and end apart: 9, of which 8 were waited for; matrix products, arithmetic and copies ran while one was open for 35% of the time, Pallas kernels for 0%

commit v1 on v0

v1 whole, which is shorter than its diff:
```python
from types import SimpleNamespace

import jax
import jax.numpy as jnp
from jax import lax
from jax.experimental import pallas as pl
from jax.experimental.pallas import tpu as pltpu
from jax.sharding import PartitionSpec as P

D = 1024
HEADS = 16
FF = 4096
HEAD_DIM = 64
ROT = 16
ADAPTERS = 8
RANK = 16
STEP = 8
COLS = 8 * D + 2 * FF
CB = 512
NB = COLS // CB
WIDE = 512
UP_CUT = 1024
DOWN_CUT = 384
TILE = 256

A_QKV, A_OUT, A_UP, A_DOWN = 0, 1, 2, 3
B_QKV, B_OUT, B_UP, B_DOWN = 7, 10, 11, 15

epsilon = 1e-05
adapter_scale = 8.0
rope_base = 10000.0
learn_rate = 0.02
beta_first = 0.5
beta_second = 0.5
weight_decay = 0.01
adam_epsilon = 1e-08
masked_value = -1e30

bf16 = jnp.bfloat16
f32 = jnp.float32

HBM = pl.BlockSpec(memory_space=pltpu.HBM)


def dot_nn(a, b):
    return jnp.dot(a, b, preferred_element_type=f32)


def dot_nt(a, b):
    return lax.dot_general(a, b, (((1,), (1,)), ((), ())), preferred_element_type=f32)


def dot_tn(a, b):
    return lax.dot_general(a, b, (((0,), (0,)), ((), ())), preferred_element_type=f32)


def shape(dims, dtype=bf16):
    return jax.ShapeDtypeStruct(tuple(dims), dtype)


def cut(index, width=D):
    return slice(index * width, (index + 1) * width)


class Stage:
    def __init__(self, loads, scalar, raw, out, targets):
        self.loads = loads
        self.scalar = scalar
        self.raw = raw
        self.out = out
        self.targets = targets
        self.waited = set()
        self.pending = []

    def __getattr__(self, name):
        buffer, copy = self.loads[name]
        if name not in self.waited:
            self.waited.add(name)
            copy.wait()
        return buffer

    def start(self, *ends):
        copy = pltpu.make_async_copy(*ends)
        copy.start()
        self.pending.append(copy)

    def store(self, buffer, at=None, into=None):
        target, sems = self.targets[id(buffer)]
        if into is not None:
            self.start(buffer, target.at[into], sems.at[0])
        elif at is None:
            self.start(buffer, target, sems.at[0])
        else:
            self.start(buffer.at[at], target.at[at], sems.at[at])


def staged(body, loads, results, raws=None, scalars=None, scratch=(), parts=None, micros=2, inside=None, alias=None):
    raws, scalars, parts, inside, alias = raws or {}, scalars or {}, parts or {}, inside or {}, alias or {}
    raw_list, raw_tree = jax.tree.flatten(raws)

    def kernel(*refs):
        refs = list(refs)

        def take(count):
            head = refs[:count]
            del refs[:count]
            return head

        scalar_from, load_from = take(len(scalars)), take(len(loads))
        raw = jax.tree.unflatten(raw_tree, take(len(raw_list)))
        targets = take(len(results))
        scalar_to, load_to, out = take(len(scalars)), take(len(loads)), take(len(results))
        (sems,) = take(1)
        out_sems = take(len(results))
        moves = [
            pltpu.make_async_copy(source, buffer, sems.at[i])
            for i, (source, buffer) in enumerate(zip(scalar_from + load_from, scalar_to + load_to))
        ]
        for move in moves:
            move.start()
        for move in moves[: len(scalars)]:
            move.wait()
        stage = Stage(
            dict(zip(loads, zip(load_to, moves[len(scalars) :]))),
            SimpleNamespace(**dict(zip(scalars, scalar_to))),
            SimpleNamespace(**raw),
            SimpleNamespace(**dict(zip(results, out))),
            {id(buffer): ends for buffer, ends in zip(out, zip(targets, out_sems))},
        )
        body(stage, *refs)
        for name in loads:
            getattr(stage, name)
        for copy in stage.pending:
            copy.wait()

    raw_names = list(raws)
    made = pl.pallas_call(
        kernel,
        out_shape=tuple(results.values()),
        in_specs=[HBM] * (len(scalars) + len(loads) + len(raw_list)),
        out_specs=(HBM,) * len(results),
        scratch_shapes=[pltpu.SMEM(a.shape, a.dtype) for a in scalars.values()]
        + [pltpu.VMEM(a.shape, a.dtype) for a in loads.values()]
        + [pltpu.VMEM(inside.get(n, s.shape), s.dtype) for n, s in results.items()]
        + [pltpu.SemaphoreType.DMA((len(loads) + len(scalars) + 1,))]
        + [pltpu.SemaphoreType.DMA((parts.get(n, 1),)) for n in results]
        + list(scratch),
        compiler_params=pltpu.CompilerParams(vmem_limit_bytes=56 * 1024 * 1024),
        input_output_aliases={
            len(scalars) + len(loads) + raw_names.index(a): list(results).index(b) for a, b in alias.items()
        },
        cost_estimate=pl.CostEstimate(flops=int(micros * 1.15e9), bytes_accessed=1024, transcendentals=0),
        name=body.__name__,
    )(*scalars.values(), *loads.values(), *raw_list)
    return SimpleNamespace(**dict(zip(results, made)))


def normalize(values):
    center = values - jnp.mean(values, axis=-1, keepdims=True)
    spread = jnp.mean(center * center, axis=-1, keepdims=True)
    scale = lax.rsqrt(spread + epsilon)
    return center * scale, scale


def give_adapters(stage):
    give = stage.out.give
    for a in range(ADAPTERS):
        give[cut(a, RANK), :] = stage.adapters[a].astype(bf16)
    row = lax.broadcasted_iota(jnp.int32, (RANK, give.shape[1]), 0)
    lane = lax.broadcasted_iota(jnp.int32, (RANK, give.shape[1]), 1)
    choice = jnp.zeros((RANK, give.shape[1]), f32)
    for j in range(stage.scalar.chosen.shape[1]):
        for a in range(ADAPTERS):
            choice = jnp.where((row == j) & (lane == a), stage.scalar.chosen[0, j, a].astype(f32), choice)
    give[ADAPTERS * RANK :, :] = choice.astype(bf16)
    stage.store(give)


def layer_norms(stage, sems):
    raw, out = stage.raw, stage.out
    copies = [
        pltpu.make_async_copy(raw.out.at[own_part(raw.out, 4), :], out.o, sems.at[0]),
        pltpu.make_async_copy(raw.up.at[own_part(raw.up, 4), :UP_CUT], out.t, sems.at[1]),
    ]
    for copy in copies:
        copy.start()
    normed, _ = normalize(stage.tok[...].astype(f32))
    gain, shift = stage.gain, stage.shift
    attn = stage.out.attn
    attn[...] = (normed * gain[0:1, :] + shift[0:1, :]).astype(bf16)
    half = pl.multiple_of((1 - lax.axis_index("wsh")) * (D // 2), D // 2)
    stage.out.give[...] = attn[:, pl.ds(half, D // 2)]
    stage.store(stage.out.give)
    stage.store(attn)
    for copy, buffer in zip(copies, (out.o, out.t)):
        copy.wait()
        stage.store(buffer)
    stage.out.mlp[...] = (normed * gain[1:2, :] + shift[1:2, :]).astype(bf16)
    stage.store(stage.out.mlp)


def choose_adapters(stage):
    adapters, given = stage.adapters, stage.given
    rows = stage.out.rows
    target, sems = stage.targets[id(rows)]
    columns = adapters.shape[2]
    wsh = lax.axis_index("wsh")
    for j in range(rows.shape[0] // RANK):
        index = 0
        for a in range(1, ADAPTERS):
            index = index + a * stage.scalar.chosen[0, j, a]
        start = pl.multiple_of(index * RANK, RANK)
        own_at = pl.multiple_of(wsh * columns, 128)
        other_at = pl.multiple_of((1 - wsh) * columns, 128)
        rows[cut(j, RANK), pl.ds(own_at, columns)] = adapters[index].astype(bf16)
        rows[cut(j, RANK), pl.ds(other_at, columns)] = given[pl.ds(start, RANK), :]
    for i in range(target.shape[0]):
        stage.start(rows, target.at[i], sems.at[i])


def part_orders(share):
    ctx = lax.axis_index("ctx")
    if share == 2:
        return ctx % 2, 1 - ctx % 2
    mine = ctx % 2 * 2 + ctx // 2 % 2
    return mine, mine ^ 1, mine ^ 2, mine ^ 3


def rows_at(first, count):
    return pl.ds(pl.multiple_of(first, count), count)


def own_part(weight, share):
    rows = weight.shape[0] // share
    return rows_at(part_orders(share)[0] * rows, rows)


def cut_parts(stage, sems):
    raw, out = stage.raw, stage.out
    plan = [
        (out.u, raw.up, own_part(raw.up, 4), UP_CUT, FF, 0),
        (out.d, raw.down, own_part(raw.down, 4), 0, DOWN_CUT, 0),
        (out.e, raw.down, own_part(raw.down, 2), DOWN_CUT, D, 0),
        (out.w, raw.qkv, own_part(raw.qkv, 2), 0, 3 * D, 0),
    ]
    copies = []
    for i, (buffer, source, rows, first, last, at) in enumerate(plan):
        copies.append(
            pltpu.make_async_copy(source.at[rows, first:last], buffer.at[:, at : at + last - first], sems.at[i])
        )
        copies[-1].start()
    for i, (buffer, *_) in enumerate(plan):
        copies[i].wait()
        if i + 1 == len(plan) or plan[i + 1][0] is not buffer:
            stage.store(buffer)


def place_weights(own, chunks, target, sems, first):
    half = own.shape[0]
    own_half = lax.axis_index("wsh")
    copies = [pltpu.make_async_copy(own, target.at[rows_at(own_half * half, half), :], sems.at[first])]
    for column, source_column, width, parts in chunks:
        rows = half // len(parts)
        for order, part in zip(part_orders(len(parts)), parts):
            copies.append(
                pltpu.make_async_copy(
                    part.at[:, source_column : source_column + width],
                    target.at[rows_at((1 - own_half) * half + order * rows, rows), column : column + width],
                    sems.at[first + len(copies)],
                )
            )
    for copy in copies:
        copy.start()
    return copies


def turn(values, tab, sign):
    left = pltpu.roll(values, 120, 1)
    right = pltpu.roll(values, 8, 1)
    return values * tab[0] + sign * (left * tab[1] + right * tab[2])


def swap_halves(first, second):
    low = lax.broadcasted_iota(jnp.int32, first.shape, 1) < HEAD_DIM
    one = jnp.where(low, first, pltpu.roll(second, HEAD_DIM, 1))
    two = jnp.where(low, pltpu.roll(first, HEAD_DIM, 1), second)
    return one, two


def both_streams(stage):
    half = pl.multiple_of(lax.axis_index("wsh") * (D // 2), D // 2)
    return jnp.concatenate([stage.h[:, pl.ds(half, D // 2)], stage.given[...]], axis=0)


def weight_columns(source, first, weights, sems):
    copies = []
    for n in range(weights.shape[0]):
        copies.append(
            pltpu.make_async_copy(source.at[:, first + n * WIDE : first + (n + 1) * WIDE], weights.at[n], sems.at[n])
        )
        copies[-1].start()
    return copies


def partial_qk(stage, weights, sems):
    copies = weight_columns(stage.raw.qkv, 0, weights, sems)
    both = both_streams(stage)
    rows = both.shape[0] // 2
    for n, copy in enumerate(copies):
        copy.wait()
        part = dot_nn(both, weights[n])
        stage.out.give[:, cut(n, WIDE)] = part[rows:].astype(bf16)
        stage.out.kept[n] = part[:rows]
    stage.store(stage.out.give)
    stage.store(stage.out.kept)


def partial_v(stage, weights, sems):
    copies = weight_columns(stage.raw.qkv, 2 * D, weights, sems)
    both = both_streams(stage)
    rows = both.shape[0] // 2
    for n, copy in enumerate(copies):
        copy.wait()
        part = dot_nn(both, weights[n])
        stage.out.give[:, cut(n, WIDE)] = part[rows:].astype(bf16)
        stage.out.kept[n] = part[:rows]
    stage.store(stage.out.give)
    stage.store(stage.out.kept)


def queries_keys(stage, wo, sems):
    copies = place_weights(stage.raw.out, [(0, 0, D, stage.raw.o)], wo, sems, 0)
    low, mask, bias, tab, kept, given = stage.low, stage.mask[...], stage.bias, stage.tab, stage.kept, stage.given
    inner = (dot_nt(stage.h[...], low[A_QKV]) * mask).astype(bf16)
    stage.out.inner[...] = inner
    stage.store(stage.out.inner)
    grad_inner = (adapter_scale * dot_nt(stage.grad[...], low[B_OUT]) * mask).astype(bf16)
    stage.out.grad_inner[...] = grad_inner
    stage.store(stage.out.grad_inner)
    steps = D // WIDE
    for n in range(steps):
        sides = []
        for kind in range(2):
            at = cut(kind * steps + n, WIDE)
            part = kept[kind * steps + n] + given[:, at].astype(f32) + bias[:, at]
            sides.append(part + adapter_scale * dot_nn(inner, low[B_QKV + kind][:, cut(n, WIDE)]))
        for pair in range(WIDE // 128):
            query = turn(sides[0][:, cut(pair, 128)], tab, 1.0) * HEAD_DIM**-0.5
            key = turn(sides[1][:, cut(pair, 128)], tab, 1.0)
            head = n * WIDE // HEAD_DIM + 2 * pair
            for i, both in enumerate(swap_halves(query, key)):
                stage.out.send[head + i] = both.astype(bf16)
    stage.store(stage.out.send, into=(slice(None), 0))
    base, grad, kept = stage.out.base, stage.grad[...], stage.kept_v
    for n in range(steps):
        base[n] = kept[n] + bias[:, 2 * D + n * WIDE : 2 * D + (n + 1) * WIDE]
        base[n] += adapter_scale * dot_nn(inner, low[B_QKV + 2][:, cut(n, WIDE)])
    for copy in copies:
        copy.wait()
    for n in range(steps):
        base[steps + n] = dot_nt(grad, wo[cut(n, WIDE), :]) + dot_nn(grad_inner, low[A_OUT][:, cut(n, WIDE)])
    stage.store(base)


def values_grads(stage):
    base, given = stage.base, stage.given
    steps = D // WIDE
    for n in range(steps):
        value = base[n] + given[:, cut(n, WIDE)].astype(f32)
        grad = base[steps + n]
        for pair in range(WIDE // 128):
            head = n * WIDE // HEAD_DIM + 2 * pair
            for i, both in enumerate(swap_halves(value[:, cut(pair, 128)], grad[:, cut(pair, 128)])):
                stage.out.send[head + i] = both.astype(bf16)
    stage.store(stage.out.send, into=(slice(None), 1))


def attention(stage, xt, dks, dvs, ks, vs, aq, s_scr, e_scr):
    order = stage.scalar.order
    rows = aq.shape[0]
    count = rows // TILE
    blocks = order.shape[1]
    half = rows // blocks
    hd = HEAD_DIM
    x = stage.arrived
    per = x.shape[2] // half
    for i in range(blocks):
        start = pl.multiple_of(order[0, i] * half, half)
        for side in range(2):
            aq[pl.ds(start, half), cut(side, 2 * hd)] = x[i // per, side, cut(i % per, half), :]
    for t in range(count):
        part = aq[cut(t, TILE), :]
        ks[cut(t, TILE), :] = part[:, hd : 2 * hd]
        vs[cut(t, TILE), :] = part[:, 2 * hd : 3 * hd]
        xt[:, cut(t, TILE)] = part.T
    dks[...] = jnp.zeros_like(dks)
    dvs[...] = jnp.zeros_like(dvs)
    key_row = lax.broadcasted_iota(jnp.int32, (TILE, TILE), 0)
    query_col = lax.broadcasted_iota(jnp.int32, (TILE, TILE), 1)
    seen = key_row <= query_col
    for b in range(count):
        at = cut(b, TILE)
        q_t = xt[0:hd, at]
        g_t = xt[3 * hd : 4 * hd, at]
        top = jnp.full((8, TILE), masked_value, f32)
        for t in range(b + 1):
            s = dot_nn(ks[cut(t, TILE), :], q_t)
            if t == b:
                s = jnp.where(seen, s, masked_value)
            s_scr[cut(t, TILE), :] = s
            top = jnp.maximum(top, jnp.max(s.reshape(TILE // 8, 8, TILE), axis=0))
        top = jnp.max(top, axis=0, keepdims=True)
        total = jnp.zeros((8, TILE), f32)
        att = jnp.zeros((hd, TILE), f32)
        for t in range(b + 1):
            e = jnp.exp(s_scr[cut(t, TILE), :] - top)
            total = total + jnp.sum(e.reshape(TILE // 8, 8, TILE), axis=0)
            e = e.astype(bf16)
            e_scr[cut(t, TILE), :] = e
            att = att + dot_nn(xt[2 * hd : 3 * hd, cut(t, TILE)], e)
        inverse = 1.0 / jnp.sum(total, axis=0, keepdims=True)
        att = att * inverse
        g_f = g_t.astype(f32)
        delta = jnp.sum(g_f * att, axis=0, keepdims=True) * inverse
        g_n = (g_f * inverse).astype(bf16)
        dq = jnp.zeros((hd, TILE), f32)
        for t in range(b + 1):
            e = e_scr[cut(t, TILE), :]
            dp = dot_nn(vs[cut(t, TILE), :], g_n)
            ds = (e.astype(f32) * (dp - delta)).astype(bf16)
            dq = dq + dot_nn(xt[hd : 2 * hd, cut(t, TILE)], ds)
            dks[cut(t, TILE), :] += dot_nt(ds, q_t)
            dvs[cut(t, TILE), :] += dot_nt(e, g_n)
        both = jnp.concatenate([att, dq * hd**-0.5], axis=0)
        aq[at, 0 : 2 * hd] = both.T.astype(bf16)
    for t in range(count):
        aq[cut(t, TILE), 2 * hd : 3 * hd] = dks[cut(t, TILE), :].astype(bf16)
        aq[cut(t, TILE), 3 * hd :] = dvs[cut(t, TILE), :].astype(bf16)
    for i in range(blocks):
        start = pl.multiple_of(order[0, i] * half, half)
        stage.out.back[cut(i, half), :] = aq[pl.ds(start, half), :]
    stage.store(stage.out.back)


def attention_one_document(order, arrived):
    rows = arrived.shape[0] * arrived.shape[2]
    hd = HEAD_DIM
    return staged(
        attention,
        dict(arrived=arrived),
        dict(back=shape((rows, 4 * hd))),
        scalars=dict(order=order),
        scratch=[
            pltpu.VMEM((4 * hd, rows), bf16),
            pltpu.VMEM((rows, hd), f32),
            pltpu.VMEM((rows, hd), f32),
            pltpu.VMEM((rows, hd), bf16),
            pltpu.VMEM((rows, hd), bf16),
            pltpu.VMEM((rows, 4 * hd), bf16),
            pltpu.VMEM((rows, TILE), f32),
            pltpu.VMEM((rows, TILE), bf16),
        ],
        micros=17,
    ).back


def attention_documents(arrived, pos, doc, groups, first_row):
    rows = arrived.shape[0] * arrived.shape[2]
    hd = HEAD_DIM
    qk, vg = (arrived[:, side].reshape(rows, 2 * hd) for side in range(2))
    q, k, v, g = qk[:, :hd], qk[:, hd:], vg[:, :hd], vg[:, hd:]
    if groups is not None:
        both = lax.all_gather(jnp.concatenate([k, v], 1), "ctx", axis=0, tiled=True, axis_index_groups=groups)
        k, v = both[:, :hd], both[:, hd:]
    step = 512
    my_pos = lax.dynamic_slice_in_dim(pos, first_row, rows)
    my_doc = lax.dynamic_slice_in_dim(doc, first_row, rows)

    def one(sums, item):
        q_b, g_b, pos_b, doc_b = item
        scores = dot_nt(q_b, k)
        allowed = (doc_b[:, None] == doc[None, :]) & (pos[None, :] <= pos_b[:, None])
        scores = jnp.where(allowed, scores, masked_value)
        top = jnp.max(scores, axis=1, keepdims=True)
        weights = jnp.exp(scores - top)
        weights = weights / jnp.sum(weights, axis=1, keepdims=True)
        weights_low = weights.astype(bf16)
        att = dot_nn(weights_low, v)
        delta = jnp.sum(g_b.astype(f32) * att, axis=1, keepdims=True)
        ds = (weights * (dot_nt(g_b, v) - delta)).astype(bf16)
        dq = dot_nn(ds, k) * hd**-0.5
        sums = (sums[0] + dot_tn(ds, q_b), sums[1] + dot_tn(weights_low, g_b))
        return sums, jnp.concatenate([att, dq], 1).astype(bf16)

    zero = jnp.zeros((k.shape[0], hd), f32)
    split = lambda a: a.reshape((rows // step, step) + a.shape[1:])
    sums, att_dq = lax.scan(one, (zero, zero), tuple(map(split, (q, g, my_pos, my_doc))))
    sums = jnp.concatenate(sums, 1)
    if groups is not None:
        sums = lax.psum_scatter(sums, "ctx", scatter_dimension=0, tiled=True, axis_index_groups=groups)
    return jnp.concatenate([att_dq.reshape(rows, 2 * hd), sums.astype(bf16)], axis=1)


def mlp_both_ways(stage, wu, wd, sems):
    raw = stage.raw
    copies = place_weights(raw.up, [(0, 0, UP_CUT, raw.t), (UP_CUT, 0, FF - UP_CUT, raw.u)], wu, sems, 0)
    copies += place_weights(raw.down, [(0, 0, DOWN_CUT, raw.d), (DOWN_CUT, 0, D - DOWN_CUT, raw.e)], wd, sems, 9)
    h, grad, low, mask, bias = stage.h[...], stage.grad[...], stage.low, stage.mask[...], stage.bias
    rows, rank = mask.shape
    out, back, grads = stage.out.out, stage.out.back, stage.out.grads
    inner_up = (dot_nt(h, low[A_UP]) * mask).astype(bf16)
    gi_down = (adapter_scale * dot_nt(grad, low[B_DOWN]) * mask).astype(bf16)
    for copy in copies:
        copy.wait()
    inner_down = jnp.zeros((rows, rank), f32)
    gi_up = jnp.zeros((rows, rank), f32)
    out[...] = jnp.zeros_like(out)
    back[...] = jnp.zeros_like(back)
    for f in range(FF // CB):
        big, small = divmod(f * CB, D)
        a_down = low[A_DOWN + big][:, small : small + CB]
        b_up = low[B_UP + big][:, small : small + CB]
        up = dot_nn(h, wu[:, cut(f, CB)]) + bias[:, 4 * D + f * CB : 4 * D + (f + 1) * CB]
        up = up + adapter_scale * dot_nn(inner_up, b_up)
        spread = 0.5 * (1.0 + lax.erf(up * (0.5**0.5)))
        hidden = (up * spread).astype(bf16)
        slope = spread + up * (jnp.exp(-0.5 * up * up) * (0.5 / jnp.pi) ** 0.5)
        down_rows = wd[cut(f, CB), :]
        out[...] += dot_nn(hidden, down_rows)
        inner_down = inner_down + dot_nt(hidden, a_down)
        grad_hidden = dot_nt(grad, down_rows) + dot_nn(gi_down, a_down)
        grad_up = (grad_hidden * slope).astype(bf16)
        back[...] += dot_nt(grad_up, wu[:, cut(f, CB)])
        gi_up = gi_up + dot_nt(grad_up, b_up)
        grads[2 + f] = dot_tn(gi_down, hidden).astype(bf16)
        grads[10 + f] = (adapter_scale * dot_tn(inner_up, grad_up)).astype(bf16)
    inner_down = (inner_down * mask).astype(bf16)
    gi_up = (adapter_scale * gi_up * mask).astype(bf16)
    for i in range(2):
        at = cut(i, CB)
        grads[i] = dot_tn(gi_up, h[:, at]).astype(bf16)
        grads[18 + i] = (adapter_scale * dot_tn(inner_down, grad[:, at])).astype(bf16)
    stage.store(grads)
    out[...] += bias[:, 4 * D + FF : 5 * D + FF] + adapter_scale * dot_nn(inner_down, low[B_DOWN])
    stage.store(out)
    back[...] += dot_nn(gi_up, low[A_UP])
    stage.store(back)


def adapter_gradients(stage):
    arrived, tab = stage.arrived, stage.tab
    att, gq, flat = stage.out.att, stage.out.gq, stage.out.flat
    for pair in range(HEADS // 2):
        at = cut(pair, 128)
        one, two = arrived[2 * pair].astype(f32), arrived[2 * pair + 1].astype(f32)
        attended, query = swap_halves(one[:, :128], two[:, :128])
        key, value = swap_halves(one[:, 128:], two[:, 128:])
        att[:, at] = attended.astype(bf16)
        for kind, part in enumerate((turn(query, tab, -1.0), turn(key, tab, -1.0), value)):
            gq[:, kind * D + pair * 128 : kind * D + (pair + 1) * 128] = part.astype(bf16)
    stage.store(att)
    stage.store(gq)
    low, mask, h, grad = stage.low, stage.mask[...], stage.h, stage.grad
    inner_out = (dot_nt(att[...], low[A_OUT]) * mask).astype(bf16)
    stage.out.inner_out[...] = inner_out
    stage.store(stage.out.inner_out)
    gi = sum(dot_nt(gq[:, cut(i)], low[B_QKV + i]) for i in range(3))
    gi = (adapter_scale * gi * mask).astype(bf16)
    stage.out.gi[...] = gi
    stage.store(stage.out.gi)
    per = D // CB

    def put(block, value):
        for i in range(per):
            flat[block * per + i] = value[:, cut(i, CB)].astype(bf16)

    put(A_QKV, dot_tn(gi, h[...]))
    put(A_OUT, dot_tn(stage.grad_inner[...], att[...]))
    put(B_OUT, adapter_scale * dot_tn(inner_out, grad[...]))
    for i in range(3):
        put(B_QKV + i, adapter_scale * dot_tn(stage.inner[...], gq[:, cut(i)]))
    flat[A_UP * per : A_UP * per + 10] = stage.mlp[0:10]
    flat[B_UP * per : B_UP * per + 10] = stage.mlp[10:20]
    stage.store(flat)


def outputs(stage, wq, wo, sems):
    raw = stage.raw
    o_copies = place_weights(raw.out, [(0, 0, D, raw.o)], wo, sems, 0)
    q_copies = place_weights(raw.qkv, [(0, 0, 3 * D, raw.w)], wq, sems, 5)
    tok, grad, low, gain, bias = stage.tok, stage.grad, stage.low, stage.gain, stage.bias
    att, inner_out, mlp_out, back = stage.att[...], stage.inner_out[...], stage.mlp_out, stage.back
    block = stage.out.block
    for copy in o_copies:
        copy.wait()
    for n in range(D // WIDE):
        at = cut(n, WIDE)
        part = dot_nn(att, wo[:, at]) + bias[:, 3 * D + n * WIDE : 3 * D + (n + 1) * WIDE]
        part = part + adapter_scale * dot_nn(inner_out, low[B_OUT][:, at])
        block[:, at] = (part + tok[:, at].astype(f32) + mlp_out[:, at]).astype(bf16)
    stage.store(block)
    normed, scale = normalize(tok[...].astype(f32))
    for copy in q_copies:
        copy.wait()
    grad_h = dot_nt(stage.gq[...], wq[...]) + dot_nn(stage.gi[...], low[A_QKV])
    grad_n = grad_h * gain[0:1, :] + back[...] * gain[1:2, :]
    grad_v = grad_n - jnp.mean(grad_n, axis=-1, keepdims=True) - normed * jnp.mean(grad_n * normed, axis=-1, keepdims=True)
    stage.out.tokens[...] = grad[...].astype(f32) + scale * grad_v
    stage.store(stage.out.tokens)


def adamw(stage):
    chosen, parts, out = stage.scalar.chosen, stage.parts, stage.out
    sums = []
    for stream in range(2):
        total = parts[stream].astype(f32)
        for source in range(stream + 2, parts.shape[0], 2):
            total = total + parts[source].astype(f32)
        sums.append(total)
    ndoc = sums[0].shape[0] // RANK
    for a in range(ADAPTERS):
        grad = None
        for stream in range(2):
            for j in range(ndoc):
                pick = chosen[stream, j, a].astype(f32)
                term = pick * sums[stream][cut(j, RANK), :]
                grad = term if grad is None else grad + term
        new_first = beta_first * stage.first[a] + (1.0 - beta_first) * grad
        new_second = beta_second * stage.second[a] + (1.0 - beta_second) * grad * grad
        first_hat = new_first / (1.0 - beta_first**STEP)
        second_hat = new_second / (1.0 - beta_second**STEP)
        old = stage.adapters[a]
        new = old - learn_rate * (first_hat / (jnp.sqrt(second_hat) + adam_epsilon) + weight_decay * old)
        for buffer, value in (
            (out.grad, grad),
            (out.new, new),
            (out.first, new_first),
            (out.second, new_second),
            (out.low, new.astype(bf16)),
        ):
            buffer[a] = value
            stage.store(buffer, a)


def stream_layout(order_row, starts_row, rows, total_rows, half_dev):
    slot = rows // half_dev
    picked = (slot[:, None] == jnp.arange(order_row.shape[0], dtype=jnp.int32)[None, :]).astype(jnp.int32)
    pos = jnp.sum(picked * order_row[None, :], axis=1) * half_dev + rows % half_dev
    finish = jnp.concatenate([starts_row[1:], jnp.full((1,), total_rows, jnp.int32)])
    inside = ((pos[:, None] >= starts_row[None, :]) & (pos[:, None] < finish[None, :])).astype(jnp.int32)
    doc = jnp.sum(inside * jnp.arange(starts_row.shape[0], dtype=jnp.int32)[None, :], axis=1)
    place = pos - jnp.sum(inside * starts_row[None, :], axis=1)
    return pos, doc, place, inside


def turn_tables(place):
    frequency = rope_base ** (-jnp.arange(0, ROT, 2, dtype=f32) / ROT)
    lane = jnp.arange(128, dtype=jnp.int32) % HEAD_DIM
    angles = place.astype(f32)[:, None] * jnp.tile(frequency, 128 // (ROT // 2))[None, :]
    cosine = jnp.where(lane < ROT, jnp.cos(angles), 1.0)
    sine = jnp.sin(angles)
    left = jnp.where(lane < ROT // 2, -sine, 0.0)
    right = jnp.where((lane >= ROT // 2) & (lane < ROT), sine, 0.0)
    return jnp.stack([cosine, left, right])


def tie(first, *others):
    return lax.optimization_barrier((first,) + others)[0]


def on_device(
    tokens,
    out_cotangent,
    norm_gains,
    norm_biases,
    qkv_weight,
    out_weight,
    up_weight,
    down_weight,
    proj_biases,
    adapters,
    first_moment,
    second_moment,
    doc_starts,
    doc_adapter,
    block_order,
):
    n_ctx = lax.axis_size("ctx")
    n_dev = n_ctx * lax.axis_size("wsh")
    ctx = lax.axis_index("ctx")
    wsh = lax.axis_index("wsh")
    tok_dev = tokens.shape[1]
    half_dev = tok_dev // 2
    total_rows = tok_dev * n_ctx
    ndoc = doc_starts.shape[1]
    rank = ndoc * RANK
    columns = adapters.shape[2]
    tok, grad = tokens[0], out_cotangent[0]
    bias = proj_biases[None, :]

    def to_y(a, name):
        with jax.named_scope("y_" + name):
            return lax.ppermute(a, "wsh", [(0, 1), (1, 0)])

    def to_x(a, name):
        with jax.named_scope("x_" + name):
            return lax.ppermute(a, "ctx", [(i, i ^ 2) for i in range(n_ctx)])

    def to_core(a, name):
        with jax.named_scope("c_" + name):
            return lax.ppermute(a, "ctx", [(i, i ^ 1) for i in range(n_ctx)])

    give = staged(
        give_adapters,
        dict(adapters=adapters),
        dict(give=shape(((ADAPTERS + 1) * RANK, columns))),
        scalars=dict(chosen=doc_adapter),
    ).give
    adapters_given = to_y(give, "adapters")
    normed = staged(
        layer_norms,
        dict(tok=tie(tok, give), gain=norm_gains, shift=norm_biases),
        dict(
            attn=shape(tok.shape),
            mlp=shape(tok.shape),
            give=shape((tok_dev, D // 2)),
            o=shape((D // 8, D)),
            t=shape((D // 8, UP_CUT)),
        ),
        raws=dict(out=out_weight, up=up_weight),
        scratch=[pltpu.SemaphoreType.DMA((2,))],
    )
    h_attn, h_mlp = normed.attn, normed.mlp
    o_y = to_y(normed.o, "o")
    given = to_y(normed.give, "h")
    chosen_rows = staged(
        choose_adapters,
        dict(adapters=adapters, given=tie(adapters_given, h_attn)),
        dict(rows=shape((n_ctx, rank, 2 * columns))),
        scalars=dict(chosen=doc_adapter),
        parts=dict(rows=n_ctx),
        inside=dict(rows=(rank, 2 * columns)),
    ).rows
    low = lax.all_to_all(chosen_rows, "ctx", 0, 0, tiled=True)
    if n_ctx != HEADS:
        low = low.reshape(COLS // D, n_ctx // HEADS, rank, 2 * columns).transpose(0, 2, 1, 3).reshape(COLS // D, rank, D)

    t_y = to_y(tie(normed.t, o_y), "t")
    o_x = to_x(o_y, "o")
    both = staged(
        partial_qk,
        dict(h=h_attn, given=tie(given, chosen_rows)),
        dict(give=shape((tok_dev, 2 * D)), kept=shape((2 * D // WIDE, tok_dev, WIDE), f32)),
        raws=dict(qkv=qkv_weight),
        scratch=[pltpu.VMEM((2 * D // WIDE, D // 2, WIDE), bf16), pltpu.SemaphoreType.DMA((2 * D // WIDE,))],
        micros=3,
    )
    kept_qk, give_qk = both.kept, both.give
    given_qk = to_y(give_qk, "qk")
    both = staged(
        partial_v,
        dict(h=tie(h_attn, give_qk, t_y), given=given),
        dict(give=shape((tok_dev, D)), kept=shape((D // WIDE, tok_dev, WIDE), f32)),
        raws=dict(qkv=qkv_weight),
        scratch=[pltpu.VMEM((D // WIDE, D // 2, WIDE), bf16), pltpu.SemaphoreType.DMA((D // WIDE,))],
        micros=3,
    )
    given_v = to_y(both.give, "v")
    my_rows = ctx * tok_dev + jnp.arange(tok_dev, dtype=jnp.int32)
    _, _, place, inside = stream_layout(tie(block_order, both.give)[0], doc_starts[0], my_rows, total_rows, half_dev)
    mask = jnp.repeat(inside.astype(f32), RANK, axis=1)
    tab = turn_tables(place)
    t_x = to_x(t_y, "t")

    def quarters(y, x, name, *after):
        return [y, x, to_core(tie(y, *after), name + "y"), to_core(tie(x, *after), name + "x")]

    def halves(y, name, *after):
        return [y, to_core(tie(y, *after), name)]

    o_parts, t_parts = quarters(o_y, o_x, "o"), quarters(t_y, t_x, "t")
    cuts = staged(
        cut_parts,
        {},
        dict(
            u=shape((D // 8, FF - UP_CUT)),
            d=shape((FF // 8, DOWN_CUT)),
            e=shape((FF // 4, D - DOWN_CUT)),
            w=shape((D // 4, 3 * D)),
        ),
        raws=dict(up=tie(up_weight, both.give), down=down_weight, qkv=qkv_weight),
        scratch=[pltpu.SemaphoreType.DMA((4,))],
    )
    heads = shape((HEADS, 2, tok_dev, 2 * HEAD_DIM))
    one = (HEADS, tok_dev, 2 * HEAD_DIM)
    made = staged(
        queries_keys,
        dict(
            h=tie(h_attn, cuts.u),
            grad=grad,
            low=low,
            mask=mask,
            bias=bias,
            tab=tab,
            kept=kept_qk,
            given=given_qk,
            kept_v=both.kept,
        ),
        dict(
            inner=shape((tok_dev, rank)),
            grad_inner=shape((tok_dev, rank)),
            send=heads,
            base=shape((2 * D // WIDE, tok_dev, WIDE), f32),
        ),
        raws=dict(out=out_weight, o=o_parts),
        inside=dict(send=one),
        scratch=[pltpu.VMEM((D, D), bf16), pltpu.SemaphoreType.DMA((5,))],
        micros=4,
    )
    inner_qkv, grad_inner_out = made.inner, made.grad_inner
    made = staged(
        values_grads,
        dict(base=made.base, given=given_v),
        dict(send=heads),
        raws=dict(send=made.send),
        inside=dict(send=one),
        alias=dict(send="send"),
        micros=3,
    )
    parts = n_ctx // HEADS
    near = None if parts == 1 else [[g * HEADS + i for i in range(HEADS)] for g in range(parts)]

    def exchange(a):
        return lax.all_to_all(a, "ctx", 0, 0, tiled=True, axis_index_groups=near)

    u_y = to_y(cuts.u, "u")
    d_y = to_y(tie(cuts.d, u_y), "d")
    e_y = to_y(tie(cuts.e, u_y), "e")
    u_x = to_x(u_y, "u")

    other = adapters_given[ADAPTERS * RANK : ADAPTERS * RANK + ndoc, :ADAPTERS].astype(jnp.int32)[None]
    chosen = jnp.where(wsh == 0, jnp.concatenate([doc_adapter, other]), jnp.concatenate([other, doc_adapter]))

    arrived = tie(exchange(made.send), u_y, *t_parts, chosen)
    if parts == 1 and ndoc == 1:
        done = attention_one_document(block_order, arrived)
    else:
        all_pos, all_doc, _, _ = stream_layout(
            block_order[0], doc_starts[0], jnp.arange(total_rows, dtype=jnp.int32), total_rows, half_dev
        )
        far = None if parts == 1 else [[g * HEADS + i for g in range(parts)] for i in range(HEADS)]
        done = attention_documents(arrived, all_pos, all_doc, far, ctx // HEADS * HEADS * tok_dev)
    d_x = to_x(tie(d_y, done), "d")
    u_parts, d_parts = quarters(u_y, u_x, "u", done), quarters(d_y, d_x, "d", done)
    back = exchange(tie(done.reshape(HEADS, tok_dev, 4 * HEAD_DIM), *u_parts, *d_parts, e_y))

    w_y = to_y(tie(cuts.w, done), "w")
    mlp = staged(
        mlp_both_ways,
        dict(h=h_mlp, grad=grad, low=low, mask=mask, bias=bias),
        dict(out=shape((tok_dev, D), f32), back=shape((tok_dev, D), f32), grads=shape((20, rank, CB))),
        raws=dict(
            up=up_weight,
            down=down_weight,
            t=t_parts,
            u=u_parts,
            d=d_parts,
            e=halves(e_y, "e", done),
        ),
        scratch=[
            pltpu.VMEM((D, FF), bf16),
            pltpu.VMEM((FF, D), bf16),
            pltpu.SemaphoreType.DMA((18,)),
        ],
        micros=0.1,
    )
    tail = staged(
        adapter_gradients,
        dict(
            arrived=back,
            tab=tab,
            low=low,
            mask=mask,
            h=h_attn,
            grad=grad,
            inner=inner_qkv,
            grad_inner=grad_inner_out,
            mlp=mlp.grads,
        ),
        dict(
            att=shape((tok_dev, D)),
            gq=shape((tok_dev, 3 * D)),
            inner_out=shape((tok_dev, rank)),
            gi=shape((tok_dev, rank)),
            flat=shape((NB, rank, CB)),
        ),
        micros=5,
    )
    flat = tail.flat
    if columns != CB:
        flat = flat.reshape(NB, rank, CB // columns, columns).transpose(0, 2, 1, 3).reshape(n_dev, rank, columns)
    shares = lax.all_to_all(flat, ("ctx", "wsh"), 0, 0, tiled=True)
    ends = staged(
        outputs,
        dict(
            tok=tok,
            grad=grad,
            gain=norm_gains,
            att=tail.att,
            gq=tail.gq,
            inner_out=tail.inner_out,
            gi=tail.gi,
            low=low,
            bias=bias,
            mlp_out=mlp.out,
            back=mlp.back,
        ),
        dict(block=shape((tok_dev, D)), tokens=shape((tok_dev, D), f32)),
        raws=dict(qkv=qkv_weight, out=out_weight, o=o_parts, w=halves(w_y, "w", tail.flat)),
        scratch=[pltpu.VMEM((D, 3 * D), bf16), pltpu.VMEM((D, D), bf16), pltpu.SemaphoreType.DMA((10,))],
        micros=0.1,
    )
    full = shape(adapters.shape, f32)
    new = staged(
        adamw,
        dict(adapters=adapters, first=first_moment, second=second_moment, parts=tie(shares, ends.block)),
        dict(grad=full, new=full, first=full, second=full, low=shape(adapters.shape)),
        scalars=dict(chosen=chosen),
        parts=dict(grad=ADAPTERS, new=ADAPTERS, first=ADAPTERS, second=ADAPTERS, low=ADAPTERS),
    )
    return (ends.block[None], ends.tokens[None], new.grad, new.new, new.first, new.second, new.low)


def solution(mesh):
    spread = P(None, None, ("ctx", "wsh"))
    rows = P("wsh", "ctx", None)
    half = P("wsh", None)
    in_specs = (rows, rows, P(), P(), half, half, half, half, P(), spread, spread, spread, half, P("wsh", None, None), half)
    out_specs = (rows, rows, spread, spread, spread, spread, spread)
    return jax.shard_map(on_device, mesh=mesh, in_specs=in_specs, out_specs=out_specs, check_vma=False)
```

time: 915 us -> 185 us (0.20); the launches traced: 902 us -> 184 us
  waiting for transfers between devices: 538 us -> 49.2 us
  matrix products: 179 us -> 0 us
  local copies, waits for them, and re-layouts: 121 us -> 7.36 us
  Pallas kernels: 0 us -> 76.3 us
  starting transfers between devices: 0.36 us -> 46.8 us
  other arithmetic: 38.9 us -> 2.46 us
  between operations: 16.1 us -> 1.91 us
    reduce_scatter x2 -> x0, waiting for transfers between devices: 281 us -> none  [the longest x1 160 us: on_device(): lax.psum_scatter(flat_grad, ('ctx', 'wsh'), scatter_dimension=2, tiled=True)]
    all_gather x7 -> x0, waiting for transfers between devices: 255 us -> none  [the longest x1 79.2 us: on_device(): lax.all_gather(qkv_weight, 'wsh', axis=0, tiled=True)]
    dot_general x60 -> x0, matrix products: 179 us -> none  [the longest x12 44.3 us: masked_scores(): jnp.einsum('qhd,khd->qhk', query_blk, key_blk, preferred_element_type=jnp...]
    pallas_call x0 -> x13, Pallas kernels: none -> 76.3 us  [staged(): pl.pallas_call(kernel, out_shape=tuple(results.values()), in_specs=[HBM]...]
    ppermute x0 -> x24, waiting for transfers between devices: none -> 41.5 us  [the longest x4 26.7 us: to_x(): return lax.ppermute(a, 'ctx', [(i, i ^ 2) for i in range(n_ctx)])]
    dynamic_update_slice x8 -> x0, local copies, waits for them, and re-layouts: 41.2 us -> none  [on_device(): lax.map(one_block, offsets).reshape(tok_dev * lax.axis_size('ctx'), 2 * D)]
    dynamic_slice x24 -> x0, local copies, waits for them, and re-layouts: 26 us -> none  [the longest x4 14.8 us: one_block(): lax.dynamic_slice_in_dim(values_all, offset, size_sub)]
    all_to_all x0 -> x4, starting transfers between devices: none -> 25.9 us  [the longest x2 13.4 us: exchange(): return lax.all_to_all(a, 'ctx', 0, 0, tiled=True, axis_index_groups=near)]
  transfers between devices with their start and end apart: 9 -> 28, of which waited for: 8 -> 10; matrix products, arithmetic and copies ran while one was open for 35% -> 2% of each run, Pallas kernels for 0% -> 38%
where the time goes in v1:
time: 185 us; the launch traced here: 184 us
  Pallas kernels  76.3 us (41%)
  waiting for transfers between devices  49.2 us (27%)
  starting transfers between devices  46.8 us (25%)
  local copies, waits for them, and re-layouts  7.36 us (4%)
  other arithmetic  2.46 us (1%)
  between operations  1.91 us (1%)
    pallas_call x13, Pallas kernels, staged(): pl.pallas_call(kernel, out_shape=tuple(results.values()), in_specs=[HBM]...  76.3 us
    ppermute x4, waiting for transfers between devices, to_x(): return lax.ppermute(a, 'ctx', [(i, i ^ 2) for i in range(n_ctx)])  26.7 us
    all_to_all x2, starting transfers between devices, exchange(): return lax.all_to_all(a, 'ctx', 0, 0, tiled=True, axis_index_groups=near)  13.4 us
    ppermute x10, waiting for transfers between devices, to_y(): return lax.ppermute(a, 'wsh', [(0, 1), (1, 0)])  12.6 us
    ppermute x10, starting transfers between devices, to_y(): return lax.ppermute(a, 'wsh', [(0, 1), (1, 0)])  8.76 us
    all_to_all x1, starting transfers between devices, on_device(): low = lax.all_to_all(chosen_rows, 'ctx', 0, 0, tiled=True)  7.34 us
    all_to_all x1, waiting for transfers between devices, on_device(): shares = lax.all_to_all(flat, ('ctx', 'wsh'), 0, 0, tiled=True)  6.37 us
    unnamed x50, local copies, waits for them, and re-layouts  6.35 us
  transfers between devices with their start and end apart: 28, of which 10 were waited for; matrix products, arithmetic and copies ran while one was open for 2% of the time, Pallas kernels for 38%

profile of v1, /device:TPU:1, one launch (start us, length us, event | category | flops | bytes accessed | tf_op | source)
XLA Modules:
  0.0 184.1 jit_solution(6222412287397131463)
XLA Ops:
  2.3 2.1 %collective-permute-start.1 = (bf16[144,512]{1,0:T(8,128)(2,1)}, bf16[144,512]{1,0:T(8,128)(2,1)S(1)}, u32[]{:S(2)}, u32[]{:S(2)}) collective-permute-start(bf16[144,512]{1,0:T(8,128)(2,1)} %give_adapters.1), channel_id=1, source_target_pairs={{0,1},{1,0},{2,3},{3,2},{4,5},{5,4},{6,7},{7,6},{8,9},{9,8},{10,11... | collective-permute-start | bytes 442376 | tf_op jit(solution)/shard_map/y_adapters/ppermute | solution.py:703
  4.4 2.4 %layer_norms.1 = (bf16[128,1024]{1,0:T(8,128)(2,1)}, bf16[128,1024]{1,0:T(8,128)(2,1)}, bf16[128,512]{1,0:T(8,128)(2,1)}, bf16[128,1024]{1,0:T(8,128)(2,1)}, bf16[128,1024]{1,0:T(8,128)(2,1)}) custom-call(bf16[128,1024]{1,0:T(8,128)(2,1)} %bitcast.20, f32[2,1024]{1,0:T(2,128)} %refs_2_.9, f32[2,1024]{1,0:T(2,128)} %refs_2_.5, bf16[512,1024]{1,0:T(8,128)(2,1)} %refs_15_.1, ...), custom_call_target="tpu_custom_call" | custom-call | flops 2300000000 | bytes 1024 | tf_op jit(solution)/shard_map/layer_norms/pallas_call | solution.py:137
  9.8 2.0 %choose_adapters.1 = bf16[16,16,1024]{2,1,0:T(8,128)(2,1)} custom-call(s32[1,1,8]{2,1,0:T(1,128)} %refs_0_.5, f32[8,16,512]{2,1,0:T(8,128)} %refs_1_.9, bf16[144,512]{1,0:T(8,128)(2,1)} %copy-done.22), custom_call_target="tpu_custom_call" | custom-call | flops 2300000000 | bytes 1024 | tf_op jit(solution)/shard_map/choose_adapters/pallas_call | solution.py:137
  11.8 7.3 %all-to-all-start = ((bf16[16,16,1024]{2,1,0:T(8,128)(2,1)}), bf16[16,16,1024]{2,1,0:T(8,128)(2,1)S(1)}, u32[]{:S(2)}, u32[]{:S(2)}) async-start(bf16[16,16,1024]{2,1,0:T(8,128)(2,1)} %choose_adapters.1), calls=%async_computation | async-start | bytes 1048576 | tf_op jit(solution)/shard_map/all_to_all | solution.py:744
  19.9 3.9 %partial_qk.1 = (bf16[128,2048]{1,0:T(8,128)(2,1)}, f32[4,128,512]{2,1,0:T(8,128)}) custom-call(bf16[128,1024]{1,0:T(8,128)(2,1)} %get-tuple-element.72.refs_0_.refs_4_, bf16[128,512]{1,0:T(8,128)(2,1)} %copy-done.23, bf16[512,3072]{1,0:T(8,128)(2,1)} %refs_16_.1), custom_call_target="tpu_custom_call" | custom-call | flops 3449999872 | bytes 1024 | tf_op jit(solution)/shard_map/partial_qk/pallas_call | solution.py:137
  27.2 2.8 %partial_v.1 = (bf16[128,1024]{1,0:T(8,128)(2,1)}, f32[2,128,512]{2,1,0:T(8,128)}) custom-call(bf16[128,1024]{1,0:T(8,128)(2,1)} %get-tuple-element.72.refs_0_.refs_4_, bf16[128,512]{1,0:T(8,128)(2,1)} %copy-done.23, bf16[512,3072]{1,0:T(8,128)(2,1)} %refs_16_.1), custom_call_target="tpu_custom_call" | custom-call | flops 3449999872 | bytes 1024 | tf_op jit(solution)/shard_map/partial_v/pallas_call | solution.py:137
  30.6 5.0 %collective-permute-done.5.refs_10_.refs_12_ = bf16[128,1024]{1,0:T(8,128)(2,1)S(1)} collective-permute-done((bf16[128,1024]{1,0:T(8,128)(2,1)S(1)}, bf16[128,1024]{1,0:T(8,128)(2,1)S(1)}, u32[]{:S(2)}, u32[]{:S(2)}) %collective-permute-start.5) | collective-permute-done | bytes 262176 | tf_op jit(solution)/shard_map/x_o/ppermute | solution.py:707
  36.6 3.6 %cut_parts.1 = (bf16[128,3072]{1,0:T(8,128)(2,1)}, bf16[512,384]{1,0:T(8,128)(2,1)}, bf16[1024,640]{1,0:T(8,128)(2,1)}, bf16[256,3072]{1,0:T(8,128)(2,1)}) custom-call(bf16[2048,1024]{1,0:T(8,128)(2,1)} %refs_9_.1, bf16[512,3072]{1,0:T(8,128)(2,1)} %refs_16_.1, bf16[512,4096]{1,0:T(8,128)(2,1)} %refs_20_.1), custom_call_target="tpu_custom_call" | custom-call | flops 2300000000 | bytes 1024 | tf_op jit(solution)/shard_map/cut_parts/pallas_call | solution.py:137
  42.2 5.7 %queries_keys.1 = (bf16[128,16]{1,0:T(8,128)(2,1)}, bf16[128,16]{1,0:T(8,128)(2,1)}, bf16[16,2,128,128]{3,2,1,0:T(8,128)(2,1)}, f32[4,128,512]{2,1,0:T(8,128)}) custom-call(bf16[128,1024]{1,0:T(8,128)(2,1)} %get-tuple-element.72.refs_0_.refs_4_, bf16[128,1024]{1,0:T(8,128)(2,1)} %bitcast.15, bf16[16,16,1024]{2,1,0:T(8,128)(2,1)} %copy-done, ...), custom_call_target="tpu_custom_call" | custom-call | flops 4600000000 | bytes 1024 | tf_op jit(solution)/shard_map/queries_keys/pallas_call | solution.py:137
  48.7 2.3 %values_grads.1 = bf16[16,2,128,128]{3,2,1,0:T(8,128)(2,1)} custom-call(f32[4,128,512]{2,1,0:T(8,128)} %get-tuple-element.76.refs_0_, bf16[128,1024]{1,0:T(8,128)(2,1)} %copy-done.20, bf16[16,2,128,128]{3,2,1,0:T(8,128)(2,1)} %get-tuple-element.77.refs_2_), custom_call_target="tpu_custom_call", output_to_operand_aliasing={{}: (2, {})} | custom-call | flops 3449999872 | bytes 1024 | tf_op jit(solution)/shard_map/values_grads/pallas_call | solution.py:137
  51.0 5.8 %all-to-all-start.1 = ((bf16[16,2,128,128]{3,2,1,0:T(8,128)(2,1)}), bf16[16,2,128,128]{3,2,1,0:T(8,128)(2,1)S(1)}, u32[]{:S(2)}, u32[]{:S(2)}) async-start(bf16[16,2,128,128]{3,2,1,0:T(8,128)(2,1)} %values_grads.1), calls=%async_computation.1 | async-start | bytes 2097152 | tf_op jit(solution)/shard_map/all_to_all | solution.py:834
  59.9 13.5 %collective-permute-done.10.refs_13_ = bf16[128,1024]{1,0:T(8,128)(2,1)S(1)} collective-permute-done((bf16[128,1024]{1,0:T(8,128)(2,1)S(1)}, bf16[128,1024]{1,0:T(8,128)(2,1)S(1)}, u32[]{:S(2)}, u32[]{:S(2)}) %collective-permute-start.10) | collective-permute-done | bytes 262176 | tf_op jit(solution)/shard_map/x_t/ppermute | solution.py:707
  81.0 16.8 %attention.1 = bf16[2048,256]{1,0:T(8,128)(2,1)} custom-call(s32[1,32]{1,0:T(1,128)} %refs_0_.7, bf16[16,2,128,128]{3,2,1,0:T(8,128)(2,1)} %copy-done.5), custom_call_target="tpu_custom_call" | custom-call | flops 19549999104 | bytes 1024 | tf_op jit(solution)/shard_map/attention/pallas_call | solution.py:137
  100.2 8.2 %collective-permute-done.17.refs_6_ = bf16[512,384]{1,0:T(8,128)(2,1)S(1)} collective-permute-done((bf16[512,384]{1,0:T(8,128)(2,1)S(1)}, bf16[512,384]{1,0:T(8,128)(2,1)S(1)}, u32[]{:S(2)}, u32[]{:S(2)}) %collective-permute-start.17) | collective-permute-done | bytes 393248 | tf_op jit(solution)/shard_map/x_d/ppermute | solution.py:707
  109.7 4.0 %collective-permute-done.20.refs_10_ = bf16[1024,640]{1,0:T(8,128)(2,1)S(1)} collective-permute-done((bf16[1024,640]{1,0:T(8,128)(2,1)}, bf16[1024,640]{1,0:T(8,128)(2,1)S(1)}, u32[]{:S(2)}, u32[]{:S(2)}) %collective-permute-start.20) | collective-permute-done | bytes 1310752 | tf_op jit(solution)/shard_map/y_e/ppermute | solution.py:703
  115.3 7.6 %all-to-all-start.2 = ((bf16[16,128,256]{2,1,0:T(8,128)(2,1)}), bf16[16,128,256]{2,1,0:T(8,128)(2,1)}, u32[]{:S(2)}, u32[]{:S(2)}) async-start(bf16[16,128,256]{2,1,0:T(8,128)(2,1)} %bitcast.19), calls=%async_computation.2 | async-start | bytes 2097152 | tf_op jit(solution)/shard_map/all_to_all | solution.py:834
  123.7 2.2 %collective-permute-done.21.refs_11_ = bf16[1024,640]{1,0:T(8,128)(2,1)S(1)} collective-permute-done((bf16[1024,640]{1,0:T(8,128)(2,1)S(1)}, bf16[1024,640]{1,0:T(8,128)(2,1)S(1)}, u32[]{:S(2)}, u32[]{:S(2)}) %collective-permute-start.21) | collective-permute-done | bytes 1310752 | tf_op jit(solution)/shard_map/c_e/ppermute | solution.py:711
  127.0 19.4 %mlp_both_ways.1 = (f32[128,1024]{1,0:T(8,128)}, f32[128,1024]{1,0:T(8,128)}, bf16[20,16,512]{2,1,0:T(8,128)(2,1)}) custom-call(bf16[128,1024]{1,0:T(8,128)(2,1)} %get-tuple-element.90.refs_0_, bf16[128,1024]{1,0:T(8,128)(2,1)} %bitcast.16, bf16[16,16,1024]{2,1,0:T(8,128)(2,1)} %copy-done, f32[128,16]{1,0:T(8,128)} %reshape.355.refs_3_, f32[1,9216]{1,0:T(1,128)} %bitcast.23, ...), custom_call_target="tpu_custom_call" | custom-call | flops 115000000 | bytes 1024 | tf_op jit(solution)/shard_map/mlp_both_ways/pallas_call | solution.py:137
  146.4 4.5 %adapter_gradients.1 = (bf16[128,1024]{1,0:T(8,128)(2,1)}, bf16[128,3072]{1,0:T(8,128)(2,1)}, bf16[128,16]{1,0:T(8,128)(2,1)}, bf16[128,16]{1,0:T(8,128)(2,1)}, bf16[32,16,512]{2,1,0:T(8,128)(2,1)}) custom-call(bf16[16,128,256]{2,1,0:T(8,128)(2,1)} %all-to-all-done.2.refs_0_, f32[3,128,128]{2,1,0:T(8,128)} %pad_maximum_fusion.refs_5_.refs_1_, ...), custom_call_target="tpu_custom_call" | custom-call | flops 5750000128 | bytes 1024 | tf_op jit(solution)/shard_map/adapter_gradients/pallas_call | solution.py:137
  151.0 8.0 %collective-permute-done.22.refs_17_ = bf16[256,3072]{1,0:T(8,128)(2,1)S(1)} collective-permute-done((bf16[256,3072]{1,0:T(8,128)(2,1)}, bf16[256,3072]{1,0:T(8,128)(2,1)S(1)}, u32[]{:S(2)}, u32[]{:S(2)}) %collective-permute-start.22) | collective-permute-done | bytes 1572896 | tf_op jit(solution)/shard_map/y_w/ppermute | solution.py:703
  160.1 5.2 %all-to-all-start.3 = ((bf16[32,16,512]{2,1,0:T(8,128)(2,1)}), bf16[32,16,512]{2,1,0:T(8,128)(2,1)}, u32[]{:S(2)}, u32[]{:S(2)}) async-start(bf16[32,16,512]{2,1,0:T(8,128)(2,1)} %get-tuple-element.101), calls=%async_computation.3 | async-start | bytes 1048576 | tf_op jit(solution)/shard_map/all_to_all | solution.py:902
  166.4 8.3 %outputs.1 = (bf16[128,1024]{1,0:T(8,128)(2,1)}, f32[128,1024]{1,0:T(8,128)}) custom-call(bf16[128,1024]{1,0:T(8,128)(2,1)} %bitcast.21, bf16[128,1024]{1,0:T(8,128)(2,1)} %bitcast.18, f32[2,1024]{1,0:T(2,128)} %refs_2_.9, bf16[128,1024]{1,0:T(8,128)(2,1)} %get-tuple-element.93.refs_3_, bf16[128,3072]{1,0:T(8,128)(2,1)} %get-tuple-element.94.refs_4_, ...), custom_call_target="tpu_custom_call" | custom-call | flops 115000000 | bytes 1024 | tf_op jit(solution)/shard_map/outputs/pallas_call | solution.py:137
  174.8 6.4 %all-to-all-done.3.refs_4_ = bf16[32,16,512]{2,1,0:T(8,128)(2,1)} async-done(((bf16[32,16,512]{2,1,0:T(8,128)(2,1)}), bf16[32,16,512]{2,1,0:T(8,128)(2,1)}, u32[]{:S(2)}, u32[]{:S(2)}) %all-to-all-start.3) | async-done | bytes 524320 | tf_op jit(solution)/shard_map/all_to_all | solution.py:902
  181.1 2.8 %adamw.1 = (f32[8,16,512]{2,1,0:T(8,128)}, f32[8,16,512]{2,1,0:T(8,128)}, f32[8,16,512]{2,1,0:T(8,128)}, f32[8,16,512]{2,1,0:T(8,128)}, bf16[8,16,512]{2,1,0:T(8,128)(2,1)}) custom-call(s32[2,1,8]{2,1,0:T(1,128)} %broadcast_select_fusion.refs_0_, f32[8,16,512]{2,1,0:T(8,128)} %refs_1_.9, f32[8,16,512]{2,1,0:T(8,128)} %refs_2_.10, f32[8,16,512]{2,1,0:T(8,128)} %refs_3_.3, ...), custom_call_target="tpu_custom_call" | custom-call | flops 2300000000 | bytes 1024 | tf_op jit(solution)/shard_map/adamw/pallas_call | solution.py:137
  (109 shorter events, 32.3 us)
Async XLA Ops:
  2.3 6.9 %collective-permute-start.1 = (bf16[144,512]{1,0:T(8,128)(2,1)}, bf16[144,512]{1,0:T(8,128)(2,1)S(1)}, u32[]{:S(2)}, u32[]{:S(2)}) collective-permute-start(bf16[144,512]{1,0:T(8,128)(2,1)} %give_adapters.1), channel_id=1, source_target_pairs={{0,1},{1,0},{2,3},{3,2},{4,5},{5,4},{6,7},{7,6},{8,9},{9,8},{10,11... | collective-permute-start | bytes 442376 | tf_op jit(solution)/shard_map/y_adapters/ppermute | solution.py:703
  6.8 12.3 %collective-permute-start = (bf16[128,512]{1,0:T(8,128)(2,1)}, bf16[128,512]{1,0:T(8,128)(2,1)S(1)}, u32[]{:S(2)}, u32[]{:S(2)}) collective-permute-start(bf16[128,512]{1,0:T(8,128)(2,1)} %get-tuple-element.61), channel_id=1, source_target_pairs={{0,1},{1,0},{2,3},{3,2},{4,5},{5,4},{6,7},{7,6},{8,9},{9,8},{10,11... | collective-permute-start | bytes 393224 | tf_op jit(solution)/shard_map/y_h/ppermute | solution.py:703
  6.9 12.3 %collective-permute-start.2 = (bf16[128,1024]{1,0:T(8,128)(2,1)}, bf16[128,1024]{1,0:T(8,128)(2,1)S(1)}, u32[]{:S(2)}, u32[]{:S(2)}) collective-permute-start(bf16[128,1024]{1,0:T(8,128)(2,1)} %get-tuple-element.66), channel_id=1, source_target_pairs={{0,1},{1,0},{2,3},{3,2},{4,5},{5,4},{6,7},{7,6},{8,9},{9,8},{10,11... | collective-permute-start | bytes 786440 | tf_op jit(solution)/shard_map/y_o/ppermute | solution.py:703
  11.8 29.2 %all-to-all-start = ((bf16[16,16,1024]{2,1,0:T(8,128)(2,1)}), bf16[16,16,1024]{2,1,0:T(8,128)(2,1)S(1)}, u32[]{:S(2)}, u32[]{:S(2)}) async-start(bf16[16,16,1024]{2,1,0:T(8,128)(2,1)} %choose_adapters.1), calls=%async_computation | async-start | bytes 1048576 | tf_op jit(solution)/shard_map/all_to_all | solution.py:744
  19.2 7.9 %collective-permute-start.3 = (bf16[128,1024]{1,0:T(8,128)(2,1)S(1)}, bf16[128,1024]{1,0:T(8,128)(2,1)S(1)}, u32[]{:S(2)}, u32[]{:S(2)}) collective-permute-start(bf16[128,1024]{1,0:T(8,128)(2,1)S(1)} %copy-done.21), channel_id=1, source_target_pairs={{0,1},{1,0},{2,3},{3,2},{4,5},{5,4},{6,7},{7,6},{8,9},{9,8},{10,11... | collective-permute-start | bytes 786440 | tf_op jit(solution)/shard_map/y_t/ppermute | solution.py:703
  23.8 17.2 %collective-permute-start.4 = (bf16[128,2048]{1,0:T(8,128)(2,1)}, bf16[128,2048]{1,0:T(8,128)(2,1)S(1)}, u32[]{:S(2)}, u32[]{:S(2)}) collective-permute-start(bf16[128,2048]{1,0:T(8,128)(2,1)} %get-tuple-element.64), channel_id=1, source_target_pairs={{0,1},{1,0},{2,3},{3,2},{4,5},{5,4},{6,7},{7,6},{8,9},{9,8},{10,11... | collective-permute-start | bytes 1572872 | tf_op jit(solution)/shard_map/y_qk/ppermute | solution.py:703
  24.8 16.2 %collective-permute-start.6 = (bf16[128,1024]{1,0:T(8,128)(2,1)S(1)}, bf16[128,1024]{1,0:T(8,128)(2,1)S(1)}, u32[]{:S(2)}, u32[]{:S(2)}) collective-permute-start(bf16[128,1024]{1,0:T(8,128)(2,1)S(1)} %collective-permute-done.2.refs_9_.refs_11_), channel_id=1, source_target_pairs={{0,2},{2,0},{4,6},{6,4},{8,10},{10,8},{12,14},{14,12},{16,18},{18,... | collective-permute-start | bytes 786440 | tf_op jit(solution)/shard_map/c_oy/ppermute | solution.py:711
  25.4 10.2 %collective-permute-start.5 = (bf16[128,1024]{1,0:T(8,128)(2,1)S(1)}, bf16[128,1024]{1,0:T(8,128)(2,1)S(1)}, u32[]{:S(2)}, u32[]{:S(2)}) collective-permute-start(bf16[128,1024]{1,0:T(8,128)(2,1)S(1)} %collective-permute-done.2.refs_9_.refs_11_), channel_id=1, source_target_pairs={{0,4},{2,6},{4,0},{6,2},{8,12},{10,14},{12,8},{14,10},{16,20},{18,... | collective-permute-start | bytes 786440 | tf_op jit(solution)/shard_map/x_o/ppermute | solution.py:707
  29.9 18.0 %collective-permute-start.8 = (bf16[128,1024]{1,0:T(8,128)(2,1)}, bf16[128,1024]{1,0:T(8,128)(2,1)S(1)}, u32[]{:S(2)}, u32[]{:S(2)}) collective-permute-start(bf16[128,1024]{1,0:T(8,128)(2,1)} %get-tuple-element.69), channel_id=1, source_target_pairs={{0,1},{1,0},{2,3},{3,2},{4,5},{5,4},{6,7},{7,6},{8,9},{9,8},{10,11... | collective-permute-start | bytes 786440 | tf_op jit(solution)/shard_map/y_v/ppermute | solution.py:703
  51.0 29.0 %all-to-all-start.1 = ((bf16[16,2,128,128]{3,2,1,0:T(8,128)(2,1)}), bf16[16,2,128,128]{3,2,1,0:T(8,128)(2,1)S(1)}, u32[]{:S(2)}, u32[]{:S(2)}) async-start(bf16[16,2,128,128]{3,2,1,0:T(8,128)(2,1)} %values_grads.1), calls=%async_computation.1 | async-start | bytes 2097152 | tf_op jit(solution)/shard_map/all_to_all | solution.py:834
  56.9 19.0 %collective-permute-start.9 = (bf16[128,3072]{1,0:T(8,128)(2,1)S(1)}, bf16[128,3072]{1,0:T(8,128)(2,1)}, u32[]{:S(2)}, u32[]{:S(2)}) collective-permute-start(bf16[128,3072]{1,0:T(8,128)(2,1)S(1)} %copy-done.18), channel_id=1, source_target_pairs={{0,1},{1,0},{2,3},{3,2},{4,5},{5,4},{6,7},{7,6},{8,9},{9,8},{10,11... | collective-permute-start | bytes 2359304 | tf_op jit(solution)/shard_map/y_u/ppermute | solution.py:703
  57.6 15.8 %collective-permute-start.10 = (bf16[128,1024]{1,0:T(8,128)(2,1)S(1)}, bf16[128,1024]{1,0:T(8,128)(2,1)S(1)}, u32[]{:S(2)}, u32[]{:S(2)}) collective-permute-start(bf16[128,1024]{1,0:T(8,128)(2,1)S(1)} %collective-permute-done.3.refs_12_), channel_id=1, source_target_pairs={{0,4},{2,6},{4,0},{6,2},{8,12},{10,14},{12,8},{14,10},{16,20},{18,... | collective-permute-start | bytes 786440 | tf_op jit(solution)/shard_map/x_t/ppermute | solution.py:707
  59.0 19.7 %collective-permute-start.11 = (bf16[128,1024]{1,0:T(8,128)(2,1)S(1)}, bf16[128,1024]{1,0:T(8,128)(2,1)S(1)}, u32[]{:S(2)}, u32[]{:S(2)}) collective-permute-start(bf16[128,1024]{1,0:T(8,128)(2,1)S(1)} %collective-permute-done.3.refs_12_), channel_id=1, source_target_pairs={{0,2},{2,0},{4,6},{6,4},{8,10},{10,8},{12,14},{14,12},{16,18},{18,... | collective-permute-start | bytes 786440 | tf_op jit(solution)/shard_map/c_ty/ppermute | solution.py:711
  75.9 21.9 %collective-permute-start.16 = (bf16[512,384]{1,0:T(8,128)(2,1)}, bf16[512,384]{1,0:T(8,128)(2,1)S(1)}, u32[]{:S(2)}, u32[]{:S(2)}) collective-permute-start(bf16[512,384]{1,0:T(8,128)(2,1)} %get-tuple-element.82), channel_id=1, source_target_pairs={{0,1},{1,0},{2,3},{3,2},{4,5},{5,4},{6,7},{7,6},{8,9},{9,8},{10,11... | collective-permute-start | bytes 1179656 | tf_op jit(solution)/shard_map/y_d/ppermute | solution.py:703
  76.5 37.2 %collective-permute-start.20 = (bf16[1024,640]{1,0:T(8,128)(2,1)}, bf16[1024,640]{1,0:T(8,128)(2,1)S(1)}, u32[]{:S(2)}, u32[]{:S(2)}) collective-permute-start(bf16[1024,640]{1,0:T(8,128)(2,1)} %get-tuple-element.86), channel_id=1, source_target_pairs={{0,1},{1,0},{2,3},{3,2},{4,5},{5,4},{6,7},{7,6},{8,9},{9,8},{10,11... | collective-permute-start | bytes 3932168 | tf_op jit(solution)/shard_map/y_e/ppermute | solution.py:703
  77.4 22.3 %collective-permute-start.13 = (bf16[128,3072]{1,0:T(8,128)(2,1)}, bf16[128,3072]{1,0:T(8,128)(2,1)}, u32[]{:S(2)}, u32[]{:S(2)}) collective-permute-start(bf16[128,3072]{1,0:T(8,128)(2,1)} %collective-permute-done.9.refs_16_), channel_id=1, source_target_pairs={{0,4},{2,6},{4,0},{6,2},{8,12},{10,14},{12,8},{14,10},{16,20},{18,... | collective-permute-start | bytes 2359304 | tf_op jit(solution)/shard_map/x_u/ppermute | solution.py:707
  97.9 10.5 %collective-permute-start.17 = (bf16[512,384]{1,0:T(8,128)(2,1)S(1)}, bf16[512,384]{1,0:T(8,128)(2,1)S(1)}, u32[]{:S(2)}, u32[]{:S(2)}) collective-permute-start(bf16[512,384]{1,0:T(8,128)(2,1)S(1)} %collective-permute-done.16.refs_5_), channel_id=1, source_target_pairs={{0,4},{2,6},{4,0},{6,2},{8,12},{10,14},{12,8},{14,10},{16,20},{18,... | collective-permute-start | bytes 1179656 | tf_op jit(solution)/shard_map/x_d/ppermute | solution.py:707
  99.6 14.1 %collective-permute-start.14 = (bf16[128,3072]{1,0:T(8,128)(2,1)}, bf16[128,3072]{1,0:T(8,128)(2,1)}, u32[]{:S(2)}, u32[]{:S(2)}) collective-permute-start(bf16[128,3072]{1,0:T(8,128)(2,1)} %collective-permute-done.9.refs_16_), channel_id=1, source_target_pairs={{0,2},{2,0},{4,6},{6,4},{8,10},{10,8},{12,14},{14,12},{16,18},{18,... | collective-permute-start | bytes 2359304 | tf_op jit(solution)/shard_map/c_uy/ppermute | solution.py:711
  99.6 14.1 %collective-permute-start.15 = (bf16[128,3072]{1,0:T(8,128)(2,1)}, bf16[128,3072]{1,0:T(8,128)(2,1)}, u32[]{:S(2)}, u32[]{:S(2)}) collective-permute-start(bf16[128,3072]{1,0:T(8,128)(2,1)} %collective-permute-done.13.refs_17_), channel_id=1, source_target_pairs={{0,2},{2,0},{4,6},{6,4},{8,10},{10,8},{12,14},{14,12},{16,18},{18,... | collective-permute-start | bytes 2359304 | tf_op jit(solution)/shard_map/c_ux/ppermute | solution.py:711
  100.1 13.6 %collective-permute-start.18 = (bf16[512,384]{1,0:T(8,128)(2,1)S(1)}, bf16[512,384]{1,0:T(8,128)(2,1)S(1)}, u32[]{:S(2)}, u32[]{:S(2)}) collective-permute-start(bf16[512,384]{1,0:T(8,128)(2,1)S(1)} %collective-permute-done.16.refs_5_), channel_id=1, source_target_pairs={{0,2},{2,0},{4,6},{6,4},{8,10},{10,8},{12,14},{14,12},{16,18},{18,... | collective-permute-start | bytes 1179656 | tf_op jit(solution)/shard_map/c_dy/ppermute | solution.py:711
  115.3 31.1 %all-to-all-start.2 = ((bf16[16,128,256]{2,1,0:T(8,128)(2,1)}), bf16[16,128,256]{2,1,0:T(8,128)(2,1)}, u32[]{:S(2)}, u32[]{:S(2)}) async-start(bf16[16,128,256]{2,1,0:T(8,128)(2,1)} %bitcast.19), calls=%async_computation.2 | async-start | bytes 2097152 | tf_op jit(solution)/shard_map/all_to_all | solution.py:834
  123.1 35.9 %collective-permute-start.22 = (bf16[256,3072]{1,0:T(8,128)(2,1)}, bf16[256,3072]{1,0:T(8,128)(2,1)S(1)}, u32[]{:S(2)}, u32[]{:S(2)}) collective-permute-start(bf16[256,3072]{1,0:T(8,128)(2,1)} %get-tuple-element.100), channel_id=1, source_target_pairs={{0,1},{1,0},{2,3},{3,2},{4,5},{5,4},{6,7},{7,6},{8,9},{9,8},{10,11... | collective-permute-start | bytes 4718600 | tf_op jit(solution)/shard_map/y_w/ppermute | solution.py:703
  159.0 6.3 %collective-permute-start.23 = (bf16[256,3072]{1,0:T(8,128)(2,1)S(1)}, bf16[256,3072]{1,0:T(8,128)(2,1)S(1)}, u32[]{:S(2)}, u32[]{:S(2)}) collective-permute-start(bf16[256,3072]{1,0:T(8,128)(2,1)S(1)} %collective-permute-done.22.refs_17_), channel_id=1, source_target_pairs={{0,2},{2,0},{4,6},{6,4},{8,10},{10,8},{12,14},{14,12},{16,18},{18,... | collective-permute-start | bytes 4718600 | tf_op jit(solution)/shard_map/c_w/ppermute | solution.py:711
  160.1 21.0 %all-to-all-start.3 = ((bf16[32,16,512]{2,1,0:T(8,128)(2,1)}), bf16[32,16,512]{2,1,0:T(8,128)(2,1)}, u32[]{:S(2)}, u32[]{:S(2)}) async-start(bf16[32,16,512]{2,1,0:T(8,128)(2,1)} %get-tuple-element.101), calls=%async_computation.3 | async-start | bytes 1048576 | tf_op jit(solution)/shard_map/all_to_all | solution.py:902
  (29 other events, 219.7 us)

commit v2 on v1

--- a/solution.py
+++ b/solution.py
@@ -19,8 +19,8 @@
 CB = 512
 NB = COLS // CB
 WIDE = 512
-UP_CUT = 1024
-DOWN_CUT = 384
+W_CUT = 2560
+HALF = FF // 2 // CB
 TILE = 256
 
 A_QKV, A_OUT, A_UP, A_DOWN = 0, 1, 2, 3
@@ -145,7 +145,7 @@
         + [pltpu.SemaphoreType.DMA((len(loads) + len(scalars) + 1,))]
         + [pltpu.SemaphoreType.DMA((parts.get(n, 1),)) for n in results]
         + list(scratch),
-        compiler_params=pltpu.CompilerParams(vmem_limit_bytes=56 * 1024 * 1024),
+        compiler_params=pltpu.CompilerParams(vmem_limit_bytes=64 * 1024 * 1024),
         input_output_aliases={
             len(scalars) + len(loads) + raw_names.index(a): list(results).index(b) for a, b in alias.items()
         },
@@ -176,27 +176,58 @@
     stage.store(give)
 
 
-def layer_norms(stage, sems):
-    raw, out = stage.raw, stage.out
-    copies = [
-        pltpu.make_async_copy(raw.out.at[own_part(raw.out, 4), :], out.o, sems.at[0]),
-        pltpu.make_async_copy(raw.up.at[own_part(raw.up, 4), :UP_CUT], out.t, sems.at[1]),
-    ]
-    for copy in copies:
-        copy.start()
+def layer_norms(stage):
+    out = stage.out
     normed, _ = normalize(stage.tok[...].astype(f32))
     gain, shift = stage.gain, stage.shift
-    attn = stage.out.attn
-    attn[...] = (normed * gain[0:1, :] + shift[0:1, :]).astype(bf16)
     half = pl.multiple_of((1 - lax.axis_index("wsh")) * (D // 2), D // 2)
-    stage.out.give[...] = attn[:, pl.ds(half, D // 2)]
-    stage.store(stage.out.give)
-    stage.store(attn)
-    for copy, buffer in zip(copies, (out.o, out.t)):
-        copy.wait()
-        stage.store(buffer)
-    stage.out.mlp[...] = (normed * gain[1:2, :] + shift[1:2, :]).astype(bf16)
-    stage.store(stage.out.mlp)
+    for i, buffer in enumerate((out.attn, out.mlp)):
+        buffer[...] = (normed * gain[i : i + 1, :] + shift[i : i + 1, :]).astype(bf16)
+        out.give[:, cut(i, D // 2)] = buffer[:, pl.ds(half, D // 2)]
+    stage.store(out.give)
+    stage.store(out.attn)
+    stage.store(out.mlp)
+
+
+def tables(stage):
+    order, starts, out = stage.scalar.order, stage.scalar.starts, stage.out
+    rows, lanes = out.tab.shape[1:]
+    ndoc = starts.shape[1]
+    ctx = lax.axis_index("ctx")
+    half = rows // 2
+
+    def positions(dims, axis):
+        index = lax.broadcasted_iota(jnp.int32, dims, axis)
+        block = jnp.where(index < half, order[0, 2 * ctx], order[0, 2 * ctx + 1])
+        return block * half + index % half
+
+    pos = positions((rows, lanes), 0)
+    start = jnp.zeros((rows, lanes), jnp.int32)
+    for j in range(1, ndoc):
+        start = jnp.where(pos >= starts[0, j], starts[0, j], start)
+    lane = lax.broadcasted_iota(jnp.int32, (rows, lanes), 1) % HEAD_DIM
+    frequency = jnp.ones((rows, lanes), f32)
+    for i in range(1, ROT // 2):
+        frequency = jnp.where(lane % (ROT // 2) == i, rope_base ** (-2.0 * i / ROT), frequency)
+    angle = (pos - start).astype(f32) * frequency
+    sine = jnp.sin(angle)
+    out.tab[0] = jnp.where(lane < ROT, jnp.cos(angle), 1.0)
+    out.tab[1] = jnp.where(lane < ROT // 2, -sine, 0.0)
+    out.tab[2] = jnp.where((lane >= ROT // 2) & (lane < ROT), sine, 0.0)
+    stage.store(out.tab)
+
+    def used(dims, row_axis):
+        pos = positions(dims, row_axis)
+        doc = lax.broadcasted_iota(jnp.int32, dims, 1 - row_axis) // RANK
+        held = jnp.zeros(dims, jnp.int32)
+        for j in range(1, ndoc):
+            held = jnp.where(pos >= starts[0, j], j, held)
+        return (held == doc).astype(f32)
+
+    out.mask[...] = used(out.mask.shape, 0)
+    out.mask_t[...] = used(out.mask_t.shape, 1)
+    stage.store(out.mask)
+    stage.store(out.mask_t)
 
 
 def choose_adapters(stage):
@@ -235,26 +266,6 @@
     return rows_at(part_orders(share)[0] * rows, rows)
 
 
-def cut_parts(stage, sems):
-    raw, out = stage.raw, stage.out
-    plan = [
-        (out.u, raw.up, own_part(raw.up, 4), UP_CUT, FF, 0),
-        (out.d, raw.down, own_part(raw.down, 4), 0, DOWN_CUT, 0),
-        (out.e, raw.down, own_part(raw.down, 2), DOWN_CUT, D, 0),
-        (out.w, raw.qkv, own_part(raw.qkv, 2), 0, 3 * D, 0),
-    ]
-    copies = []
-    for i, (buffer, source, rows, first, last, at) in enumerate(plan):
-        copies.append(
-            pltpu.make_async_copy(source.at[rows, first:last], buffer.at[:, at : at + last - first], sems.at[i])
-        )
-        copies[-1].start()
-    for i, (buffer, *_) in enumerate(plan):
-        copies[i].wait()
-        if i + 1 == len(plan) or plan[i + 1][0] is not buffer:
-            stage.store(buffer)
-
-
 def place_weights(own, chunks, target, sems, first):
     half = own.shape[0]
     own_half = lax.axis_index("wsh")
@@ -287,9 +298,9 @@
     return one, two
 
 
-def both_streams(stage):
+def both_streams(stage, side=0):
     half = pl.multiple_of(lax.axis_index("wsh") * (D // 2), D // 2)
-    return jnp.concatenate([stage.h[:, pl.ds(half, D // 2)], stage.given[...]], axis=0)
+    return jnp.concatenate([stage.h[:, pl.ds(half, D // 2)], stage.given[:, cut(side, D // 2)]], axis=0)
 
 
 def weight_columns(source, first, weights, sems):
@@ -315,8 +326,10 @@
     stage.store(stage.out.kept)
 
 
-def partial_v(stage, weights, sems):
+def partial_vg(stage, weights, out_rows, sems):
     copies = weight_columns(stage.raw.qkv, 2 * D, weights, sems)
+    out_copy = pltpu.make_async_copy(stage.raw.out, out_rows, sems.at[len(copies)])
+    out_copy.start()
     both = both_streams(stage)
     rows = both.shape[0] // 2
     for n, copy in enumerate(copies):
@@ -324,12 +337,16 @@
         part = dot_nn(both, weights[n])
         stage.out.give[:, cut(n, WIDE)] = part[rows:].astype(bf16)
         stage.out.kept[n] = part[:rows]
+    grads = jnp.concatenate([stage.grad[...], stage.grad_given[...]], axis=0)
+    out_copy.wait()
+    part = dot_nt(grads, out_rows[...])
+    stage.out.give[:, D:] = part[rows:].astype(bf16)
     stage.store(stage.out.give)
+    stage.out.kept[D // WIDE] = part[:rows]
     stage.store(stage.out.kept)
 
 
-def queries_keys(stage, wo, sems):
-    copies = place_weights(stage.raw.out, [(0, 0, D, stage.raw.o)], wo, sems, 0)
+def queries_keys(stage):
     low, mask, bias, tab, kept, given = stage.low, stage.mask[...], stage.bias, stage.tab, stage.kept, stage.given
     inner = (dot_nt(stage.h[...], low[A_QKV]) * mask).astype(bf16)
     stage.out.inner[...] = inner
@@ -351,23 +368,21 @@
             for i, both in enumerate(swap_halves(query, key)):
                 stage.out.send[head + i] = both.astype(bf16)
     stage.store(stage.out.send, into=(slice(None), 0))
-    base, grad, kept = stage.out.base, stage.grad[...], stage.kept_v
+    base, kept, wsh = stage.out.base, stage.kept_vg, lax.axis_index("wsh")
     for n in range(steps):
         base[n] = kept[n] + bias[:, 2 * D + n * WIDE : 2 * D + (n + 1) * WIDE]
         base[n] += adapter_scale * dot_nn(inner, low[B_QKV + 2][:, cut(n, WIDE)])
-    for copy in copies:
-        copy.wait()
-    for n in range(steps):
-        base[steps + n] = dot_nt(grad, wo[cut(n, WIDE), :]) + dot_nn(grad_inner, low[A_OUT][:, cut(n, WIDE)])
+        base[steps + n] = jnp.where(wsh == n, kept[steps], 0.0) + dot_nn(grad_inner, low[A_OUT][:, cut(n, WIDE)])
     stage.store(base)
 
 
 def values_grads(stage):
     base, given = stage.base, stage.given
     steps = D // WIDE
+    wsh = lax.axis_index("wsh")
     for n in range(steps):
         value = base[n] + given[:, cut(n, WIDE)].astype(f32)
-        grad = base[steps + n]
+        grad = base[steps + n] + jnp.where(wsh == n, 0.0, given[:, D:].astype(f32))
         for pair in range(WIDE // 128):
             head = n * WIDE // HEAD_DIM + 2 * pair
             for i, both in enumerate(swap_halves(value[:, cut(pair, 128)], grad[:, cut(pair, 128)])):
@@ -501,50 +516,177 @@
     return jnp.concatenate([att_dq.reshape(rows, 2 * hd), sums.astype(bf16)], axis=1)
 
 
-def mlp_both_ways(stage, wu, wd, sems):
-    raw = stage.raw
-    copies = place_weights(raw.up, [(0, 0, UP_CUT, raw.t), (UP_CUT, 0, FF - UP_CUT, raw.u)], wu, sems, 0)
-    copies += place_weights(raw.down, [(0, 0, DOWN_CUT, raw.d), (DOWN_CUT, 0, D - DOWN_CUT, raw.e)], wd, sems, 9)
-    h, grad, low, mask, bias = stage.h[...], stage.grad[...], stage.low, stage.mask[...], stage.bias
-    rows, rank = mask.shape
-    out, back, grads = stage.out.out, stage.out.back, stage.out.grads
-    inner_up = (dot_nt(h, low[A_UP]) * mask).astype(bf16)
-    gi_down = (adapter_scale * dot_nt(grad, low[B_DOWN]) * mask).astype(bf16)
+def swapped(rows):
+    half = rows.shape[0] // 2
+    return jnp.concatenate([rows[half:], rows[:half]], axis=0)
+
+
+def hidden_block(j):
+    wsh = lax.axis_index("wsh")
+    return (wsh if j < HALF else 1 - wsh) * HALF + j % HALF
+
+
+def hidden_columns(j):
+    return pl.ds(pl.multiple_of(hidden_block(j // HALF * HALF) * CB, HALF * CB), HALF * CB)
+
+
+def up_blocks(source, weights, sems, order):
+    copies = {}
+    for j in order:
+        first = pl.multiple_of(hidden_block(j) * CB, CB)
+        copies[j] = pltpu.make_async_copy(source.at[:, pl.ds(first, CB)], weights.at[j], sems.at[j])
+        copies[j].start()
+    return copies
+
+
+def adapter_block(low, first, j):
+    return low[first + hidden_block(j) // 2, :, cut(j % 2, CB)]
+
+
+def mlp_up(stage, weights, sems):
+    out = stage.out
+    order = [*range(HALF, 2 * HALF), *range(HALF)]
+    copies = up_blocks(stage.raw.up, weights, sems, order)
+    both = both_streams(stage, 1)
+    for j in order:
+        copies[j].wait()
+        part = dot_nn(both, weights[j])
+        if j < HALF:
+            out.kept[j] = part
+        elif j == HALF:
+            out.early[...] = part.astype(bf16)
+            stage.store(out.early)
+        else:
+            out.late[:, cut(j - HALF - 1, CB)] = part.astype(bf16)
+            if j == 2 * HALF - 1:
+                stage.store(out.late, into=pl.ds(0, part.shape[0]))
+    stage.store(out.kept)
+
+
+def share_at(kind, j, rank, rows):
+    down, right = divmod(kind * HALF + j, HALF - 1)
+    return pl.ds(rows + down * rank, rank), cut(right, CB)
+
+
+def mlp_share(stage, sems):
+    out = stage.out
+    qkv, weight = stage.raw.qkv, stage.raw.out
+    mine = own_part(qkv, 4)
+    copies = [
+        pltpu.make_async_copy(weight.at[mine, :], out.first.at[:, :D], sems.at[0]),
+        pltpu.make_async_copy(qkv.at[mine, :W_CUT], out.first.at[:, D:], sems.at[1]),
+        pltpu.make_async_copy(qkv.at[own_part(qkv, 2), W_CUT:], out.second, sems.at[2]),
+        pltpu.make_async_copy(stage.raw.up.at[mine, hidden_columns(HALF)], out.up, sems.at[3]),
+    ]
+    for copy in copies:
+        copy.start()
+    share, low, mask = out.late, stage.low, stage.mask_t[...]
+    rank, rows = mask.shape
+    for j in range(HALF):
+        share[share_at(0, j, rank, 0)] = adapter_block(low, A_DOWN, HALF + j)
+        share[share_at(1, j, rank, 0)] = adapter_block(low, B_UP, HALF + j)
+    inner = (dot_nt(low[A_UP], stage.h[...]) * mask).astype(bf16)
+    back = (adapter_scale * dot_nt(low[B_DOWN], stage.grad[...]) * mask).astype(bf16)
+    zero = jnp.zeros((rank, CB - 2 * rows), bf16)
+    share[share_at(2, 0, rank, 0)] = jnp.concatenate([inner, back, zero], axis=1)
+    stage.store(share, into=pl.ds(2 * rows, 3 * rank))
+    out.products[...] = jnp.concatenate([inner, back], axis=1)
+    stage.store(out.products)
     for copy in copies:
         copy.wait()
-    inner_down = jnp.zeros((rows, rank), f32)
-    gi_up = jnp.zeros((rows, rank), f32)
-    out[...] = jnp.zeros_like(out)
-    back[...] = jnp.zeros_like(back)
-    for f in range(FF // CB):
-        big, small = divmod(f * CB, D)
-        a_down = low[A_DOWN + big][:, small : small + CB]
-        b_up = low[B_UP + big][:, small : small + CB]
-        up = dot_nn(h, wu[:, cut(f, CB)]) + bias[:, 4 * D + f * CB : 4 * D + (f + 1) * CB]
-        up = up + adapter_scale * dot_nn(inner_up, b_up)
+    for buffer in (out.up, out.first, out.second):
+        stage.store(buffer)
+
+
+def diagonal(one, two):
+    zero = jnp.zeros_like(one)
+    return jnp.concatenate([jnp.concatenate([one, zero], axis=1), jnp.concatenate([zero, two], axis=1)], axis=0)
+
+
+def mlp_middle(stage, weights, sems):
+    out, low = stage.out, stage.low
+    copies = []
+    for j in range(HALF):
+        copies.append(pltpu.make_async_copy(stage.raw.down.at[cut(j, CB), :], weights.at[j], sems.at[j]))
+        copies[-1].start()
+    grads = jnp.concatenate([stage.grad[...], stage.grad_given[...]], axis=0)
+    rows = grads.shape[0] // 2
+    products, late = stage.products[...], stage.late
+    rank = products.shape[0]
+    other = late[share_at(2, 0, rank, 2 * rows)]
+    inner, back = (diagonal(products[:, cut(i, rows)], other[:, cut(i, rows)]) for i in range(2))
+    sums = None
+    for j in range(HALF):
+        at = cut(j, CB)
+        a_both = jnp.concatenate([adapter_block(low, A_DOWN, j), late[share_at(0, j, rank, 2 * rows)]], axis=0)
+        b_both = jnp.concatenate([adapter_block(low, B_UP, j), late[share_at(1, j, rank, 2 * rows)]], axis=0)
+        part = stage.early[...] if j == 0 else late[: 2 * rows, cut(j - 1, CB)]
+        shift = pl.multiple_of(4 * D + hidden_block(j) * CB, CB)
+        up = stage.kept[j] + swapped(part.astype(f32)) + stage.bias[:, pl.ds(shift, CB)]
+        up = up + adapter_scale * dot_tn(inner, b_both)
         spread = 0.5 * (1.0 + lax.erf(up * (0.5**0.5)))
         hidden = (up * spread).astype(bf16)
         slope = spread + up * (jnp.exp(-0.5 * up * up) * (0.5 / jnp.pi) ** 0.5)
-        down_rows = wd[cut(f, CB), :]
-        out[...] += dot_nn(hidden, down_rows)
-        inner_down = inner_down + dot_nt(hidden, a_down)
-        grad_hidden = dot_nt(grad, down_rows) + dot_nn(gi_down, a_down)
+        copies[j].wait()
+        down = weights[j]
+        grad_hidden = dot_nt(grads, down) + dot_tn(back, a_both)
         grad_up = (grad_hidden * slope).astype(bf16)
-        back[...] += dot_nt(grad_up, wu[:, cut(f, CB)])
-        gi_up = gi_up + dot_nt(grad_up, b_up)
-        grads[2 + f] = dot_tn(gi_down, hidden).astype(bf16)
-        grads[10 + f] = (adapter_scale * dot_tn(inner_up, grad_up)).astype(bf16)
-    inner_down = (inner_down * mask).astype(bf16)
-    gi_up = (adapter_scale * gi_up * mask).astype(bf16)
+        out.grad_up[j] = grad_up
+        stage.store(out.grad_up, j)
+        parts = dot_nn(hidden, down), dot_nt(a_both, hidden), dot_nt(b_both, grad_up)
+        sums = parts if sums is None else tuple(one + two for one, two in zip(sums, parts))
+        a_grad = dot_nn(back, hidden).astype(bf16)
+        b_grad = (adapter_scale * dot_nn(inner, grad_up)).astype(bf16)
+        out.grads[j], out.grads[HALF + j] = a_grad[:rank], b_grad[:rank]
+        out.pack[0:rank, at], out.pack[rank : 2 * rank, at] = a_grad[rank:], b_grad[rank:]
+    down, inner_down, gi_up = sums
+    out.down[...] = down[:rows]
+    out.small[0], out.small[1] = inner_down[:rank, :rows], gi_up[:rank, :rows]
+    out.pack[2 * rank : 3 * rank, :] = jnp.zeros((rank, 2 * D), bf16)
+    out.pack[2 * rank : 3 * rank, 0:rows] = inner_down[rank:, rows:].astype(bf16)
+    out.pack[2 * rank : 3 * rank, rows : 2 * rows] = gi_up[rank:, rows:].astype(bf16)
+    out.rest[...] = down[rows:].astype(bf16)
+    for buffer in (out.pack, out.small, out.grads, out.rest, out.down):
+        stage.store(buffer)
+
+
+def mlp_back(stage, weights, sems):
+    copies = place_weights(stage.raw.up.at[:, hidden_columns(0)], [(0, 0, HALF * CB, stage.raw.u)], weights, sems, 0)
+    for copy in copies:
+        copy.wait()
+    total = None
+    for j in range(HALF):
+        part = dot_nt(stage.grad_up[j], weights[:, cut(j, CB)])
+        total = part if total is None else total + part
+    rows = total.shape[0] // 2
+    stage.out.give[...] = total[rows:].astype(bf16)
+    stage.store(stage.out.give)
+    stage.out.kept[...] = total[:rows]
+    stage.store(stage.out.kept)
+
+
+def mlp_finish(stage):
+    out, low, mask = stage.out, stage.low, stage.mask_t[...]
+    rank, rows = mask.shape
+    pack, small, wsh = stage.pack, stage.small, lax.axis_index("wsh")
+    extra = pack[2 * rank : 3 * rank, :].astype(f32)
+    inner_down = ((small[0] + extra[:, 0:rows]) * mask).astype(bf16)
+    gi_up = (adapter_scale * (small[1] + extra[:, rows : 2 * rows]) * mask).astype(bf16)
+    for j in range(HALF):
+        for kind in range(2):
+            out.grads[2 + kind * 2 * HALF + wsh * HALF + j] = stage.grads[kind * HALF + j]
+            other = pack[kind * rank : (kind + 1) * rank, cut(j, CB)]
+            out.grads[2 + kind * 2 * HALF + (1 - wsh) * HALF + j] = other
+    up_grad = dot_nn(gi_up, stage.h[...])
+    down_grad = adapter_scale * dot_nn(inner_down, stage.grad[...])
     for i in range(2):
-        at = cut(i, CB)
-        grads[i] = dot_tn(gi_up, h[:, at]).astype(bf16)
-        grads[18 + i] = (adapter_scale * dot_tn(inner_down, grad[:, at])).astype(bf16)
-    stage.store(grads)
-    out[...] += bias[:, 4 * D + FF : 5 * D + FF] + adapter_scale * dot_nn(inner_down, low[B_DOWN])
-    stage.store(out)
-    back[...] += dot_nn(gi_up, low[A_UP])
-    stage.store(back)
+        out.grads[i] = up_grad[:, cut(i, CB)].astype(bf16)
+        out.grads[18 + i] = down_grad[:, cut(i, CB)].astype(bf16)
+    stage.store(out.grads)
+    out.inner_down[...] = inner_down
+    stage.store(out.inner_down)
+    out.back[...] = stage.kept[...] + stage.given[...].astype(f32) + dot_tn(gi_up, low[A_UP])
+    stage.store(out.back)
 
 
 def adapter_gradients(stage):
@@ -586,18 +728,21 @@
 
 def outputs(stage, wq, wo, sems):
     raw = stage.raw
-    o_copies = place_weights(raw.out, [(0, 0, D, raw.o)], wo, sems, 0)
-    q_copies = place_weights(raw.qkv, [(0, 0, 3 * D, raw.w)], wq, sems, 5)
+    o_copies = place_weights(raw.out, [(0, 0, D, raw.v)], wo, sems, 0)
+    q_copies = place_weights(raw.qkv, [(0, D, W_CUT, raw.v), (W_CUT, 0, 3 * D - W_CUT, raw.w)], wq, sems, 5)
     tok, grad, low, gain, bias = stage.tok, stage.grad, stage.low, stage.gain, stage.bias
-    att, inner_out, mlp_out, back = stage.att[...], stage.inner_out[...], stage.mlp_out, stage.back
+    att, inner_out, inner_down, back = stage.att[...], stage.inner_out[...], stage.inner_down[...], stage.back
     block = stage.out.block
     for copy in o_copies:
         copy.wait()
     for n in range(D // WIDE):
         at = cut(n, WIDE)
-        part = dot_nn(att, wo[:, at]) + bias[:, 3 * D + n * WIDE : 3 * D + (n + 1) * WIDE]
+        shift = n * WIDE
+        part = dot_nn(att, wo[:, at]) + bias[:, 3 * D + shift : 3 * D + shift + WIDE]
         part = part + adapter_scale * dot_nn(inner_out, low[B_OUT][:, at])
-        block[:, at] = (part + tok[:, at].astype(f32) + mlp_out[:, at]).astype(bf16)
+        mlp = stage.down[:, at] + stage.rest[:, at].astype(f32) + bias[:, 4 * D + FF + shift : 4 * D + FF + shift + WIDE]
+        mlp = mlp + adapter_scale * dot_tn(inner_down, low[B_DOWN][:, at])
+        block[:, at] = (part + tok[:, at].astype(f32) + mlp).astype(bf16)
     stage.store(block)
     normed, scale = normalize(tok[...].astype(f32))
     for copy in q_copies:
@@ -611,6 +756,7 @@
 
 def adamw(stage):
     chosen, parts, out = stage.scalar.chosen, stage.parts, stage.out
+    given, wsh = stage.given, lax.axis_index("wsh")
     sums = []
     for stream in range(2):
         total = parts[stream].astype(f32)
@@ -622,8 +768,9 @@
         grad = None
         for stream in range(2):
             for j in range(ndoc):
-                pick = chosen[stream, j, a].astype(f32)
-                term = pick * sums[stream][cut(j, RANK), :]
+                own = chosen[0, j, a].astype(f32)
+                other = given[ADAPTERS * RANK + j : ADAPTERS * RANK + j + 1, a : a + 1].astype(f32)
+                term = jnp.where(wsh == stream, own, other) * sums[stream][cut(j, RANK), :]
                 grad = term if grad is None else grad + term
         new_first = beta_first * stage.first[a] + (1.0 - beta_first) * grad
         new_second = beta_second * stage.second[a] + (1.0 - beta_second) * grad * grad
@@ -651,17 +798,6 @@
     doc = jnp.sum(inside * jnp.arange(starts_row.shape[0], dtype=jnp.int32)[None, :], axis=1)
     place = pos - jnp.sum(inside * starts_row[None, :], axis=1)
     return pos, doc, place, inside
-
-
-def turn_tables(place):
-    frequency = rope_base ** (-jnp.arange(0, ROT, 2, dtype=f32) / ROT)
-    lane = jnp.arange(128, dtype=jnp.int32) % HEAD_DIM
-    angles = place.astype(f32)[:, None] * jnp.tile(frequency, 128 // (ROT // 2))[None, :]
-    cosine = jnp.where(lane < ROT, jnp.cos(angles), 1.0)
-    sine = jnp.sin(angles)
-    left = jnp.where(lane < ROT // 2, -sine, 0.0)
-    right = jnp.where((lane >= ROT // 2) & (lane < ROT), sine, 0.0)
-    return jnp.stack([cosine, left, right])
 
 
 def tie(first, *others):
@@ -720,19 +856,11 @@
     normed = staged(
         layer_norms,
         dict(tok=tie(tok, give), gain=norm_gains, shift=norm_biases),
-        dict(
-            attn=shape(tok.shape),
-            mlp=shape(tok.shape),
-            give=shape((tok_dev, D // 2)),
-            o=shape((D // 8, D)),
-            t=shape((D // 8, UP_CUT)),
-        ),
-        raws=dict(out=out_weight, up=up_weight),
-        scratch=[pltpu.SemaphoreType.DMA((2,))],
+        dict(attn=shape(tok.shape), mlp=shape(tok.shape), give=shape((tok_dev, D))),
     )
     h_attn, h_mlp = normed.attn, normed.mlp
-    o_y = to_y(normed.o, "o")
     given = to_y(normed.give, "h")
+    grad_given = to_y(tie(grad, normed.give), "grad")
     chosen_rows = staged(
         choose_adapters,
         dict(adapters=adapters, given=tie(adapters_given, h_attn)),
@@ -745,8 +873,6 @@
     if n_ctx != HEADS:
         low = low.reshape(COLS // D, n_ctx // HEADS, rank, 2 * columns).transpose(0, 2, 1, 3).reshape(COLS // D, rank, D)
 
-    t_y = to_y(tie(normed.t, o_y), "t")
-    o_x = to_x(o_y, "o")
     both = staged(
         partial_qk,
         dict(h=h_attn, given=tie(given, chosen_rows)),
@@ -758,45 +884,46 @@
     kept_qk, give_qk = both.kept, both.give
     given_qk = to_y(give_qk, "qk")
     both = staged(
-        partial_v,
-        dict(h=tie(h_attn, give_qk, t_y), given=given),
-        dict(give=shape((tok_dev, D)), kept=shape((D // WIDE, tok_dev, WIDE), f32)),
-        raws=dict(qkv=qkv_weight),
-        scratch=[pltpu.VMEM((D // WIDE, D // 2, WIDE), bf16), pltpu.SemaphoreType.DMA((D // WIDE,))],
+        partial_vg,
+        dict(h=tie(h_attn, give_qk), given=given, grad=grad, grad_given=grad_given),
+        dict(give=shape((tok_dev, 3 * D // 2)), kept=shape((D // WIDE + 1, tok_dev, WIDE), f32)),
+        raws=dict(qkv=qkv_weight, out=out_weight),
+        scratch=[
+            pltpu.VMEM((D // WIDE, D // 2, WIDE), bf16),
+            pltpu.VMEM((D // 2, D), bf16),
+            pltpu.SemaphoreType.DMA((D // WIDE + 1,)),
+        ],
         micros=3,
     )
-    given_v = to_y(both.give, "v")
-    my_rows = ctx * tok_dev + jnp.arange(tok_dev, dtype=jnp.int32)
-    _, _, place, inside = stream_layout(tie(block_order, both.give)[0], doc_starts[0], my_rows, total_rows, half_dev)
-    mask = jnp.repeat(inside.astype(f32), RANK, axis=1)
-    tab = turn_tables(place)
-    t_x = to_x(t_y, "t")
-
-    def quarters(y, x, name, *after):
-        return [y, x, to_core(tie(y, *after), name + "y"), to_core(tie(x, *after), name + "x")]
-
-    def halves(y, name, *after):
-        return [y, to_core(tie(y, *after), name)]
-
-    o_parts, t_parts = quarters(o_y, o_x, "o"), quarters(t_y, t_x, "t")
-    cuts = staged(
-        cut_parts,
+    given_vg = to_y(both.give, "vg")
+    table = staged(
+        tables,
         {},
+        dict(tab=shape((3, tok_dev, 128), f32), mask=shape((tok_dev, rank), f32), mask_t=shape((rank, tok_dev), f32)),
+        scalars=dict(order=tie(block_order, both.give), starts=doc_starts),
+        micros=0.1,
+    )
+    tab, mask, mask_t = table.tab, table.mask, table.mask_t
+    up = staged(
+        mlp_up,
+        dict(h=tie(h_mlp, both.give), given=given),
         dict(
-            u=shape((D // 8, FF - UP_CUT)),
-            d=shape((FF // 8, DOWN_CUT)),
-            e=shape((FF // 4, D - DOWN_CUT)),
-            w=shape((D // 4, 3 * D)),
+            early=shape((2 * tok_dev, CB)),
+            late=shape((2 * tok_dev + 3 * rank, (HALF - 1) * CB)),
+            kept=shape((HALF, 2 * tok_dev, CB), f32),
         ),
-        raws=dict(up=tie(up_weight, both.give), down=down_weight, qkv=qkv_weight),
-        scratch=[pltpu.SemaphoreType.DMA((4,))],
-    )
+        raws=dict(up=up_weight),
+        inside=dict(late=(2 * tok_dev, (HALF - 1) * CB)),
+        scratch=[pltpu.VMEM((2 * HALF, D // 2, CB), bf16), pltpu.SemaphoreType.DMA((2 * HALF,))],
+        micros=0.1,
+    )
+    early_given = to_y(up.early, "early")
     heads = shape((HEADS, 2, tok_dev, 2 * HEAD_DIM))
     one = (HEADS, tok_dev, 2 * HEAD_DIM)
     made = staged(
         queries_keys,
         dict(
-            h=tie(h_attn, cuts.u),
+            h=tie(h_attn, up.early),
             grad=grad,
             low=low,
             mask=mask,
@@ -804,7 +931,7 @@
             tab=tab,
             kept=kept_qk,
             given=given_qk,
-            kept_v=both.kept,
+            kept_vg=both.kept,
         ),
         dict(
             inner=shape((tok_dev, rank)),
@@ -812,15 +939,13 @@
             send=heads,
             base=shape((2 * D // WIDE, tok_dev, WIDE), f32),
         ),
-        raws=dict(out=out_weight, o=o_parts),
         inside=dict(send=one),
-        scratch=[pltpu.VMEM((D, D), bf16), pltpu.SemaphoreType.DMA((5,))],
-        micros=4,
+        micros=0.1,
     )
     inner_qkv, grad_inner_out = made.inner, made.grad_inner
     made = staged(
         values_grads,
-        dict(base=made.base, given=given_v),
+        dict(base=made.base, given=given_vg),
         dict(send=heads),
         raws=dict(send=made.send),
         inside=dict(send=one),
@@ -833,15 +958,54 @@
     def exchange(a):
         return lax.all_to_all(a, "ctx", 0, 0, tiled=True, axis_index_groups=near)
 
-    u_y = to_y(cuts.u, "u")
-    d_y = to_y(tie(cuts.d, u_y), "d")
-    e_y = to_y(tie(cuts.e, u_y), "e")
+    shared = staged(
+        mlp_share,
+        dict(h=h_mlp, grad=grad, low=low, mask_t=mask_t),
+        dict(
+            late=shape(up.late.shape),
+            products=shape((rank, 2 * tok_dev)),
+            first=shape((D // 8, D + W_CUT)),
+            second=shape((D // 4, 3 * D - W_CUT)),
+            up=shape((D // 8, HALF * CB)),
+        ),
+        raws=dict(late=up.late, qkv=qkv_weight, out=out_weight, up=up_weight),
+        inside=dict(late=(3 * rank, (HALF - 1) * CB)),
+        alias=dict(late="late"),
+        scratch=[pltpu.SemaphoreType.DMA((4,))],
+    )
+    late_given = to_y(shared.late, "late")
+    middle = staged(
+        mlp_middle,
+        dict(
+            kept=up.kept,
+            early=early_given,
+            late=late_given,
+            grad=grad,
+            grad_given=grad_given,
+            low=low,
+            bias=bias,
+            products=shared.products,
+        ),
+        dict(
+            grad_up=shape((HALF, 2 * tok_dev, CB)),
+            down=shape((tok_dev, D), f32),
+            small=shape((2, rank, tok_dev), f32),
+            grads=shape((2 * HALF, rank, CB)),
+            pack=shape((3 * rank, 2 * D)),
+            rest=shape((tok_dev, D)),
+        ),
+        raws=dict(down=down_weight),
+        scratch=[pltpu.VMEM((HALF, CB, D), bf16), pltpu.SemaphoreType.DMA((HALF,))],
+        parts=dict(grad_up=HALF),
+        micros=0.1,
+    )
+    def quarters(y, x, name, *after):
+        return [y, x, to_core(tie(y, *after), name + "y"), to_core(tie(x, *after), name + "x")]
+
+    u_y = to_y(tie(shared.up, late_given), "u")
     u_x = to_x(u_y, "u")
-
-    other = adapters_given[ADAPTERS * RANK : ADAPTERS * RANK + ndoc, :ADAPTERS].astype(jnp.int32)[None]
-    chosen = jnp.where(wsh == 0, jnp.concatenate([doc_adapter, other]), jnp.concatenate([other, doc_adapter]))
-
-    arrived = tie(exchange(made.send), u_y, *t_parts, chosen)
+    v_y = to_y(tie(shared.first, middle.pack), "v")
+    arrived = tie(exchange(tie(made.send, early_given, shared.products)), middle.pack, u_y)
     if parts == 1 and ndoc == 1:
         done = attention_one_document(block_order, arrived)
     else:
@@ -850,28 +1014,34 @@
         )
         far = None if parts == 1 else [[g * HEADS + i for g in range(parts)] for i in range(HEADS)]
         done = attention_documents(arrived, all_pos, all_doc, far, ctx // HEADS * HEADS * tok_dev)
-    d_x = to_x(tie(d_y, done), "d")
-    u_parts, d_parts = quarters(u_y, u_x, "u", done), quarters(d_y, d_x, "d", done)
-    back = exchange(tie(done.reshape(HEADS, tok_dev, 4 * HEAD_DIM), *u_parts, *d_parts, e_y))
-
-    w_y = to_y(tie(cuts.w, done), "w")
+    back = exchange(tie(done.reshape(HEADS, tok_dev, 4 * HEAD_DIM), v_y, u_x))
+    v_x = to_x(tie(v_y, done), "v")
+    pack_given = to_y(tie(middle.pack, done), "pack")
+    last = staged(
+        mlp_back,
+        dict(grad_up=tie(middle.grad_up, pack_given)),
+        dict(give=shape((tok_dev, D)), kept=shape((tok_dev, D), f32)),
+        raws=dict(up=up_weight, u=quarters(u_y, u_x, "u", done)),
+        scratch=[pltpu.VMEM((D, HALF * CB), bf16), pltpu.SemaphoreType.DMA((5,))],
+        micros=0.1,
+    )
+    back_given = to_y(last.give, "back")
+    w_y = to_y(tie(shared.second, last.give), "w")
+    rest_given = to_y(tie(middle.rest, last.give), "rest")
     mlp = staged(
-        mlp_both_ways,
-        dict(h=h_mlp, grad=grad, low=low, mask=mask, bias=bias),
-        dict(out=shape((tok_dev, D), f32), back=shape((tok_dev, D), f32), grads=shape((20, rank, CB))),
-        raws=dict(
-            up=up_weight,
-            down=down_weight,
-            t=t_parts,
-            u=u_parts,
-            d=d_parts,
-            e=halves(e_y, "e", done),
+        mlp_finish,
+        dict(
+            small=middle.small,
+            grads=middle.grads,
+            pack=pack_given,
+            kept=last.kept,
+            given=back_given,
+            h=h_mlp,
+            grad=grad,
+            low=low,
+            mask_t=mask_t,
         ),
-        scratch=[
-            pltpu.VMEM((D, FF), bf16),
-            pltpu.VMEM((FF, D), bf16),
-            pltpu.SemaphoreType.DMA((18,)),
-        ],
+        dict(inner_down=shape((rank, tok_dev)), back=shape((tok_dev, D), f32), grads=shape((20, rank, CB))),
         micros=0.1,
     )
     tail = staged(
@@ -894,12 +1064,12 @@
             gi=shape((tok_dev, rank)),
             flat=shape((NB, rank, CB)),
         ),
-        micros=5,
+        micros=0.1,
     )
     flat = tail.flat
     if columns != CB:
         flat = flat.reshape(NB, rank, CB // columns, columns).transpose(0, 2, 1, 3).reshape(n_dev, rank, columns)
-    shares = lax.all_to_all(flat, ("ctx", "wsh"), 0, 0, tiled=True)
+    shares = lax.all_to_all(tie(flat, w_y, rest_given), ("ctx", "wsh"), 0, 0, tiled=True)
     ends = staged(
         outputs,
         dict(
@@ -912,20 +1082,27 @@
             gi=tail.gi,
             low=low,
             bias=bias,
-            mlp_out=mlp.out,
+            down=middle.down,
+            rest=rest_given,
+            inner_down=mlp.inner_down,
             back=mlp.back,
         ),
         dict(block=shape((tok_dev, D)), tokens=shape((tok_dev, D), f32)),
-        raws=dict(qkv=qkv_weight, out=out_weight, o=o_parts, w=halves(w_y, "w", tail.flat)),
-        scratch=[pltpu.VMEM((D, 3 * D), bf16), pltpu.VMEM((D, D), bf16), pltpu.SemaphoreType.DMA((10,))],
+        raws=dict(
+            qkv=qkv_weight,
+            out=out_weight,
+            v=quarters(v_y, v_x, "v", done),
+            w=[w_y, to_core(w_y, "w")],
+        ),
+        scratch=[pltpu.VMEM((D, 3 * D), bf16), pltpu.VMEM((D, D), bf16), pltpu.SemaphoreType.DMA((14,))],
         micros=0.1,
     )
     full = shape(adapters.shape, f32)
     new = staged(
         adamw,
-        dict(adapters=adapters, first=first_moment, second=second_moment, parts=tie(shares, ends.block)),
+        dict(adapters=adapters, first=first_moment, second=second_moment, parts=tie(shares, ends.block), given=adapters_given),
         dict(grad=full, new=full, first=full, second=full, low=shape(adapters.shape)),
-        scalars=dict(chosen=chosen),
+        scalars=dict(chosen=doc_adapter),
         parts=dict(grad=ADAPTERS, new=ADAPTERS, first=ADAPTERS, second=ADAPTERS, low=ADAPTERS),
     )
     return (ends.block[None], ends.tokens[None], new.grad, new.new, new.first, new.second, new.low)

time: 185 us -> 177 us (0.957)
  local copies, waits for them, and re-layouts: 7.36 us -> 0 us
  Pallas kernels: 76.3 us -> 81.5 us
  other arithmetic: 2.46 us -> 0 us
  waiting for transfers between devices: 49.2 us -> 46.8 us
    ppermute x10 -> x13, waiting for transfers between devices: 12.6 us -> 40.6 us  [to_y(): return lax.ppermute(a, 'wsh', [(0, 1), (1, 0)])]
    ppermute x4 -> x2, waiting for transfers between devices: 26.7 us -> 0.01 us  [to_x(): return lax.ppermute(a, 'ctx', [(i, i ^ 2) for i in range(n_ctx)])]
    unnamed x50 -> x0, local copies, waits for them, and re-layouts: 6.35 us -> none
    ppermute x10 -> x13, starting transfers between devices: 8.76 us -> 14.3 us  [to_y(): return lax.ppermute(a, 'wsh', [(0, 1), (1, 0)])]
    pallas_call x13 -> x17, Pallas kernels: 76.3 us -> 81.5 us  [staged(): pl.pallas_call(kernel, out_shape=tuple(results.values()), in_specs=[HBM]...]
    ppermute x10 -> x5, starting transfers between devices: 6.1 us -> 1.55 us  [to_core(): return lax.ppermute(a, 'ctx', [(i, i ^ 1) for i in range(n_ctx)])]
    all_to_all x1, waiting for transfers between devices: 6.37 us -> 2.22 us  [on_device(): lax.all_to_all(tie(flat, w_y, rest_given), ('ctx', 'wsh'), 0, 0, tiled=True)]
    ppermute x4 -> x2, starting transfers between devices: 6.09 us -> 2.71 us  [to_x(): return lax.ppermute(a, 'ctx', [(i, i ^ 2) for i in range(n_ctx)])]
  transfers between devices with their start and end apart: 28 -> 24, of which waited for: 10 -> 12; matrix products, arithmetic and copies ran while one was open for 2% -> 0% of each run, Pallas kernels for 38% -> 44%
where the time goes in v2:
time: 177 us; the launch traced here: 176 us
  Pallas kernels  81.5 us (46%)
  waiting for transfers between devices  46.8 us (26%)
  starting transfers between devices  46.4 us (26%)
    pallas_call x17, Pallas kernels, staged(): pl.pallas_call(kernel, out_shape=tuple(results.values()), in_specs=[HBM]...  81.5 us
    ppermute x13, waiting for transfers between devices, to_y(): return lax.ppermute(a, 'wsh', [(0, 1), (1, 0)])  40.6 us
    ppermute x13, starting transfers between devices, to_y(): return lax.ppermute(a, 'wsh', [(0, 1), (1, 0)])  14.3 us
    all_to_all x2, starting transfers between devices, exchange(): return lax.all_to_all(a, 'ctx', 0, 0, tiled=True, axis_index_groups=near)  14 us
    all_to_all x1, starting transfers between devices, on_device(): low = lax.all_to_all(chosen_rows, 'ctx', 0, 0, tiled=True)  7.28 us
    all_to_all x1, starting transfers between devices, on_device(): lax.all_to_all(tie(flat, w_y, rest_given), ('ctx', 'wsh'), 0, 0, tiled=True)  6.56 us
    ppermute x5, waiting for transfers between devices, to_core(): return lax.ppermute(a, 'ctx', [(i, i ^ 1) for i in range(n_ctx)])  3.66 us
  transfers between devices with their start and end apart: 24, of which 12 were waited for; matrix products, arithmetic and copies ran while one was open for 0% of the time, Pallas kernels for 44%

profile of v2, /device:TPU:1, one launch (start us, length us, event | category | flops | bytes accessed | tf_op | source)
XLA Modules:
  0.0 176.4 jit_solution(2624753435543419746)
XLA Ops:
  4.4 2.3 %layer_norms.1 = (bf16[128,1024]{1,0:T(8,128)(2,1)}, bf16[128,1024]{1,0:T(8,128)(2,1)}, bf16[128,1024]{1,0:T(8,128)(2,1)}) custom-call(bf16[128,1024]{1,0:T(8,128)(2,1)} %bitcast.18, f32[2,1024]{1,0:T(2,128)} %refs_2_.8, f32[2,1024]{1,0:T(2,128)} %refs_2_.5), custom_call_target="tpu_custom_call" | custom-call | flops 2300000000 | bytes 1024 | tf_op jit(solution)/shard_map/layer_norms/pallas_call | solution.py:137
  10.3 7.3 %all-to-all-start = ((bf16[16,16,1024]{2,1,0:T(8,128)(2,1)}), bf16[16,16,1024]{2,1,0:T(8,128)(2,1)}, u32[]{:S(2)}, u32[]{:S(2)}) async-start(bf16[16,16,1024]{2,1,0:T(8,128)(2,1)} %choose_adapters.1), calls=%async_computation | async-start | bytes 1048576 | tf_op jit(solution)/shard_map/all_to_all | solution.py:872
  17.6 4.0 %partial_qk.1 = (bf16[128,2048]{1,0:T(8,128)(2,1)}, f32[4,128,512]{2,1,0:T(8,128)}) custom-call(bf16[128,1024]{1,0:T(8,128)(2,1)} %get-tuple-element.87.refs_0_.refs_4_, bf16[128,1024]{1,0:T(8,128)(2,1)} %collective-permute-done.refs_1_, bf16[512,3072]{1,0:T(8,128)(2,1)} %refs_14_.1), custom_call_target="tpu_custom_call" | custom-call | flops 3449999872 | bytes 1024 | tf_op jit(solution)/shard_map/partial_qk/pallas_call | solution.py:137
  23.4 3.4 %partial_vg.1 = (bf16[128,1536]{1,0:T(8,128)(2,1)}, f32[3,128,512]{2,1,0:T(8,128)}) custom-call(bf16[128,1024]{1,0:T(8,128)(2,1)} %get-tuple-element.87.refs_0_.refs_4_, bf16[128,1024]{1,0:T(8,128)(2,1)} %collective-permute-done.refs_1_, bf16[128,1024]{1,0:T(8,128)(2,1)} %bitcast.7, bf16[128,1024]{1,0:T(8,128)(2,1)} %collective-permute-done.2.refs_3_.refs_4_, ...), custom_call_target="tpu_custom_call" | custom-call | flops 3449999872 | bytes 1024 | tf_op jit(solution)/shard_map/partial_vg/pallas_call | solution.py:137
  27.6 6.1 %mlp_up.1 = (bf16[256,512]{1,0:T(8,128)(2,1)}, bf16[304,1536]{1,0:T(8,128)(2,1)}, f32[4,256,512]{2,1,0:T(8,128)}) custom-call(bf16[128,1024]{1,0:T(8,128)(2,1)} %get-tuple-element.85.refs_0_.refs_5_, bf16[128,1024]{1,0:T(8,128)(2,1)} %collective-permute-done.refs_1_, bf16[512,4096]{1,0:T(8,128)(2,1)} %refs_5_.5), custom_call_target="tpu_custom_call" | custom-call | flops 115000000 | bytes 1024 | tf_op jit(solution)/shard_map/mlp_up/pallas_call | solution.py:137
  36.9 4.6 %queries_keys.1 = (bf16[128,16]{1,0:T(8,128)(2,1)}, bf16[128,16]{1,0:T(8,128)(2,1)}, bf16[16,2,128,128]{3,2,1,0:T(8,128)(2,1)}, f32[4,128,512]{2,1,0:T(8,128)}) custom-call(bf16[128,1024]{1,0:T(8,128)(2,1)} %get-tuple-element.87.refs_0_.refs_4_, bf16[128,1024]{1,0:T(8,128)(2,1)} %bitcast.8, bf16[16,16,1024]{2,1,0:T(8,128)(2,1)} %all-to-all-done.refs_2_.refs_5_.refs_7_, ...), custom_call_target="tpu_custom_call" | custom-call | flops 115000000 | bytes 1024 | tf_op jit(solution)/shard_map/queries_keys/pallas_call | solution.py:137
  41.5 2.8 %collective-permute-done.4.refs_1_ = bf16[128,1536]{1,0:T(8,128)(2,1)} collective-permute-done((bf16[128,1536]{1,0:T(8,128)(2,1)}, bf16[128,1536]{1,0:T(8,128)(2,1)}, u32[]{:S(2)}, u32[]{:S(2)}) %collective-permute-start.4) | collective-permute-done | bytes 393248 | tf_op jit(solution)/shard_map/y_vg/ppermute | solution.py:839
  44.3 2.4 %values_grads.1 = bf16[16,2,128,128]{3,2,1,0:T(8,128)(2,1)} custom-call(f32[4,128,512]{2,1,0:T(8,128)} %get-tuple-element.93.refs_0_, bf16[128,1536]{1,0:T(8,128)(2,1)} %collective-permute-done.4.refs_1_, bf16[16,2,128,128]{3,2,1,0:T(8,128)(2,1)} %get-tuple-element.94.refs_2_), custom_call_target="tpu_custom_call", output_to_operand_aliasing={{}: (2, {})} | custom-call | flops 3449999872 | bytes 1024 | tf_op jit(solution)/shard_map/values_grads/pallas_call | solution.py:137
  46.7 3.2 %mlp_share.1 = (bf16[304,1536]{1,0:T(8,128)(2,1)}, bf16[16,256]{1,0:T(8,128)(2,1)}, bf16[128,3584]{1,0:T(8,128)(2,1)}, bf16[256,512]{1,0:T(8,128)(2,1)}, bf16[128,2048]{1,0:T(8,128)(2,1)}) custom-call(bf16[128,1024]{1,0:T(8,128)(2,1)} %get-tuple-element.85.refs_0_.refs_5_, bf16[128,1024]{1,0:T(8,128)(2,1)} %bitcast.9, ...), custom_call_target="tpu_custom_call", output_to_operand_aliasing={{0}: (4, {})} | custom-call | flops 2300000000 | bytes 1024 | tf_op jit(solution)/shard_map/mlp_share/pallas_call | solution.py:137
  50.0 6.9 %all-to-all-start.1 = ((bf16[16,2,128,128]{3,2,1,0:T(8,128)(2,1)}), bf16[16,2,128,128]{3,2,1,0:T(8,128)(2,1)}, u32[]{:S(2)}, u32[]{:S(2)}) async-start(bf16[16,2,128,128]{3,2,1,0:T(8,128)(2,1)} %values_grads.1), calls=%async_computation.1 | async-start | bytes 2097152 | tf_op jit(solution)/shard_map/all_to_all | solution.py:959
  58.8 21.1 %collective-permute-done.6.refs_2_ = bf16[304,1536]{1,0:T(8,128)(2,1)} collective-permute-done((bf16[304,1536]{1,0:T(8,128)(2,1)}, bf16[304,1536]{1,0:T(8,128)(2,1)}, u32[]{:S(2)}, u32[]{:S(2)}) %collective-permute-start.6) | collective-permute-done | bytes 933920 | tf_op jit(solution)/shard_map/y_late/ppermute | solution.py:839
  81.0 9.1 %mlp_middle.1 = (bf16[4,256,512]{2,1,0:T(8,128)(2,1)}, f32[128,1024]{1,0:T(8,128)}, f32[2,16,128]{2,1,0:T(8,128)}, bf16[8,16,512]{2,1,0:T(8,128)(2,1)}, bf16[48,...) custom-call(f32[4,256,512]{2,1,0:T(8,128)} %get-tuple-element.99.refs_0_, bf16[256,512]{1,0:T(8,128)(2,1)} %collective-permute-done.5.refs_1_, ...), custom_call_target="tpu_custom_call" | custom-call | flops 115000000 | bytes 1024 | tf_op jit(solution)/shard_map/mlp_middle/pallas_call | solution.py:137
  90.5 2.3 %collective-permute-done.7.refs_1_ = bf16[128,2048]{1,0:T(8,128)(2,1)} collective-permute-done((bf16[128,2048]{1,0:T(8,128)(2,1)}, bf16[128,2048]{1,0:T(8,128)(2,1)}, u32[]{:S(2)}, u32[]{:S(2)}) %collective-permute-start.7) | collective-permute-done | bytes 524320 | tf_op jit(solution)/shard_map/y_u/ppermute | solution.py:839
  94.1 16.8 %attention.1 = bf16[2048,256]{1,0:T(8,128)(2,1)} custom-call(s32[1,32]{1,0:T(1,128)} %refs_0_.7, bf16[16,2,128,128]{3,2,1,0:T(8,128)(2,1)} %all-to-all-done.1.refs_1_), custom_call_target="tpu_custom_call" | custom-call | flops 19549999104 | bytes 1024 | tf_op jit(solution)/shard_map/attention/pallas_call | solution.py:137
  112.8 7.1 %all-to-all-start.2 = ((bf16[16,128,256]{2,1,0:T(8,128)(2,1)}), bf16[16,128,256]{2,1,0:T(8,128)(2,1)}, u32[]{:S(2)}, u32[]{:S(2)}) async-start(bf16[16,128,256]{2,1,0:T(8,128)(2,1)} %bitcast.14), calls=%async_computation.2 | async-start | bytes 2097152 | tf_op jit(solution)/shard_map/all_to_all | solution.py:959
  123.0 5.1 %collective-permute-done.10.refs_2_ = bf16[48,2048]{1,0:T(8,128)(2,1)} collective-permute-done((bf16[48,2048]{1,0:T(8,128)(2,1)}, bf16[48,2048]{1,0:T(8,128)(2,1)}, u32[]{:S(2)}, u32[]{:S(2)}) %collective-permute-start.10) | collective-permute-done | bytes 196640 | tf_op jit(solution)/shard_map/y_pack/ppermute | solution.py:839
  128.1 4.7 %mlp_back.1 = (bf16[128,1024]{1,0:T(8,128)(2,1)}, f32[128,1024]{1,0:T(8,128)}) custom-call(bf16[4,256,512]{2,1,0:T(8,128)(2,1)} %get-tuple-element.114.refs_0_, bf16[128,2048]{1,0:T(8,128)(2,1)} %collective-permute-done.7.refs_1_, bf16[128,2048]{1,0:T(8,128)(2,1)} %collective-permute-done.9.refs_2_, bf16[128,2048]{1,0:T(8,128)(2,1)} %collective-permute-done.11.refs_3_, ...), custom_call_target="tpu_custom_call" | custom-call | flops 115000000 | bytes 1024 | tf_op jit(solution)/shard_map/mlp_back/pallas_call | solution.py:137
  135.5 4.2 %collective-permute-done.13.refs_4_ = bf16[128,1024]{1,0:T(8,128)(2,1)} collective-permute-done((bf16[128,1024]{1,0:T(8,128)(2,1)}, bf16[128,1024]{1,0:T(8,128)(2,1)}, u32[]{:S(2)}, u32[]{:S(2)}) %collective-permute-start.13) | collective-permute-done | bytes 262176 | tf_op jit(solution)/shard_map/y_back/ppermute | solution.py:839
  139.6 3.1 %mlp_finish.1 = (bf16[16,128]{1,0:T(8,128)(2,1)}, f32[128,1024]{1,0:T(8,128)}, bf16[20,16,512]{2,1,0:T(8,128)(2,1)}) custom-call(f32[2,16,128]{2,1,0:T(8,128)} %get-tuple-element.110.refs_0_, bf16[8,16,512]{2,1,0:T(8,128)(2,1)} %get-tuple-element.111.refs_1_, bf16[48,2048]{1,0:T(8,128)(2,1)} %collective-permute-done.10.refs_2_, ...), custom_call_target="tpu_custom_call" | custom-call | flops 115000000 | bytes 1024 | tf_op jit(solution)/shard_map/mlp_finish/pallas_call | solution.py:137
  143.1 4.5 %adapter_gradients.1 = (bf16[128,1024]{1,0:T(8,128)(2,1)}, bf16[128,3072]{1,0:T(8,128)(2,1)}, bf16[128,16]{1,0:T(8,128)(2,1)}, bf16[128,16]{1,0:T(8,128)(2,1)}, bf16[32,16,512]{2,1,0:T(8,128)(2,1)}) custom-call(bf16[16,128,256]{2,1,0:T(8,128)(2,1)} %all-to-all-done.2.refs_0_, f32[3,128,128]{2,1,0:T(8,128)} %get-tuple-element.90.refs_5_.refs_1_, ...), custom_call_target="tpu_custom_call" | custom-call | flops 115000000 | bytes 1024 | tf_op jit(solution)/shard_map/adapter_gradients/pallas_call | solution.py:137
  147.6 3.2 %collective-permute-done.18.refs_19_ = bf16[256,512]{1,0:T(8,128)(2,1)} collective-permute-done((bf16[256,512]{1,0:T(8,128)(2,1)}, bf16[256,512]{1,0:T(8,128)(2,1)}, u32[]{:S(2)}, u32[]{:S(2)}) %collective-permute-start.18) | collective-permute-done | bytes 262176 | tf_op jit(solution)/shard_map/y_w/ppermute | solution.py:839
  150.9 6.6 %all-to-all-start.3 = ((bf16[32,16,512]{2,1,0:T(8,128)(2,1)}), bf16[32,16,512]{2,1,0:T(8,128)(2,1)}, u32[]{:S(2)}, u32[]{:S(2)}) async-start(bf16[32,16,512]{2,1,0:T(8,128)(2,1)} %get-tuple-element.136), calls=%async_computation.3 | async-start | bytes 1048576 | tf_op jit(solution)/shard_map/all_to_all | solution.py:1072
  162.0 9.1 %outputs.1 = (bf16[128,1024]{1,0:T(8,128)(2,1)}, f32[128,1024]{1,0:T(8,128)}) custom-call(bf16[128,1024]{1,0:T(8,128)(2,1)} %bitcast.19, bf16[128,1024]{1,0:T(8,128)(2,1)} %bitcast.13, f32[2,1024]{1,0:T(2,128)} %refs_2_.8, bf16[128,1024]{1,0:T(8,128)(2,1)} %get-tuple-element.120.refs_3_, bf16[128,3072]{1,0:T(8,128)(2,1)} %get-tuple-element.121.refs_4_, ...), custom_call_target="tpu_custom_call" | custom-call | flops 115000000 | bytes 1024 | tf_op jit(solution)/shard_map/outputs/pallas_call | solution.py:137
  173.3 2.9 %adamw.1 = (f32[8,16,512]{2,1,0:T(8,128)}, f32[8,16,512]{2,1,0:T(8,128)}, f32[8,16,512]{2,1,0:T(8,128)}, f32[8,16,512]{2,1,0:T(8,128)}, bf16[8,16,512]{2,1,0:T(8,128)(2,1)}) custom-call(s32[1,1,8]{2,1,0:T(1,128)} %refs_0_.8, f32[8,16,512]{2,1,0:T(8,128)} %refs_1_.8, f32[8,16,512]{2,1,0:T(8,128)} %refs_2_.9, f32[8,16,512]{2,1,0:T(8,128)} %refs_3_.1, ...), custom_call_target="tpu_custom_call" | custom-call | flops 2300000000 | bytes 1024 | tf_op jit(solution)/shard_map/adamw/pallas_call | solution.py:137
  (41 shorter events, 32.0 us)
Async XLA Ops:
  2.3 6.0 %collective-permute-start.1 = (bf16[144,512]{1,0:T(8,128)(2,1)}, bf16[144,512]{1,0:T(8,128)(2,1)}, u32[]{:S(2)}, u32[]{:S(2)}) collective-permute-start(bf16[144,512]{1,0:T(8,128)(2,1)} %give_adapters.1), channel_id=1, source_target_pairs={{0,1},{1,0},{2,3},{3,2},{4,5},{5,4},{6,7},{7,6},{8,9},{9,8},{10,11... | collective-permute-start | bytes 442376 | tf_op jit(solution)/shard_map/y_adapters/ppermute | solution.py:839
  6.7 10.9 %collective-permute-start = (bf16[128,1024]{1,0:T(8,128)(2,1)}, bf16[128,1024]{1,0:T(8,128)(2,1)}, u32[]{:S(2)}, u32[]{:S(2)}) collective-permute-start(bf16[128,1024]{1,0:T(8,128)(2,1)} %get-tuple-element.78), channel_id=1, source_target_pairs={{0,1},{1,0},{2,3},{3,2},{4,5},{5,4},{6,7},{7,6},{8,9},{9,8},{10,11... | collective-permute-start | bytes 786440 | tf_op jit(solution)/shard_map/y_h/ppermute | solution.py:839
  6.8 16.6 %collective-permute-start.2 = (bf16[128,1024]{1,0:T(8,128)(2,1)}, bf16[128,1024]{1,0:T(8,128)(2,1)}, u32[]{:S(2)}, u32[]{:S(2)}) collective-permute-start(bf16[128,1024]{1,0:T(8,128)(2,1)} %bitcast.6), channel_id=1, source_target_pairs={{0,1},{1,0},{2,3},{3,2},{4,5},{5,4},{6,7},{7,6},{8,9},{9,8},{10,11... | collective-permute-start | bytes 786440 | tf_op jit(solution)/shard_map/y_grad/ppermute | solution.py:839
  10.3 26.6 %all-to-all-start = ((bf16[16,16,1024]{2,1,0:T(8,128)(2,1)}), bf16[16,16,1024]{2,1,0:T(8,128)(2,1)}, u32[]{:S(2)}, u32[]{:S(2)}) async-start(bf16[16,16,1024]{2,1,0:T(8,128)(2,1)} %choose_adapters.1), calls=%async_computation | async-start | bytes 1048576 | tf_op jit(solution)/shard_map/all_to_all | solution.py:872
  21.6 15.3 %collective-permute-start.3 = (bf16[128,2048]{1,0:T(8,128)(2,1)}, bf16[128,2048]{1,0:T(8,128)(2,1)}, u32[]{:S(2)}, u32[]{:S(2)}) collective-permute-start(bf16[128,2048]{1,0:T(8,128)(2,1)} %get-tuple-element.81), channel_id=1, source_target_pairs={{0,1},{1,0},{2,3},{3,2},{4,5},{5,4},{6,7},{7,6},{8,9},{9,8},{10,11... | collective-permute-start | bytes 1572872 | tf_op jit(solution)/shard_map/y_qk/ppermute | solution.py:839
  26.8 17.5 %collective-permute-start.4 = (bf16[128,1536]{1,0:T(8,128)(2,1)}, bf16[128,1536]{1,0:T(8,128)(2,1)}, u32[]{:S(2)}, u32[]{:S(2)}) collective-permute-start(bf16[128,1536]{1,0:T(8,128)(2,1)} %get-tuple-element.84), channel_id=1, source_target_pairs={{0,1},{1,0},{2,3},{3,2},{4,5},{5,4},{6,7},{7,6},{8,9},{9,8},{10,11... | collective-permute-start | bytes 1179656 | tf_op jit(solution)/shard_map/y_vg/ppermute | solution.py:839
  33.7 16.3 %collective-permute-start.5 = (bf16[256,512]{1,0:T(8,128)(2,1)}, bf16[256,512]{1,0:T(8,128)(2,1)}, u32[]{:S(2)}, u32[]{:S(2)}) collective-permute-start(bf16[256,512]{1,0:T(8,128)(2,1)} %get-tuple-element.86), channel_id=1, source_target_pairs={{0,1},{1,0},{2,3},{3,2},{4,5},{5,4},{6,7},{7,6},{8,9},{9,8},{10,11... | collective-permute-start | bytes 786440 | tf_op jit(solution)/shard_map/y_early/ppermute | solution.py:839
  50.0 44.1 %all-to-all-start.1 = ((bf16[16,2,128,128]{3,2,1,0:T(8,128)(2,1)}), bf16[16,2,128,128]{3,2,1,0:T(8,128)(2,1)}, u32[]{:S(2)}, u32[]{:S(2)}) async-start(bf16[16,2,128,128]{3,2,1,0:T(8,128)(2,1)} %values_grads.1), calls=%async_computation.1 | async-start | bytes 2097152 | tf_op jit(solution)/shard_map/all_to_all | solution.py:959
  56.9 23.0 %collective-permute-start.6 = (bf16[304,1536]{1,0:T(8,128)(2,1)}, bf16[304,1536]{1,0:T(8,128)(2,1)}, u32[]{:S(2)}, u32[]{:S(2)}) collective-permute-start(bf16[304,1536]{1,0:T(8,128)(2,1)} %get-tuple-element.100), channel_id=1, source_target_pairs={{0,1},{1,0},{2,3},{3,2},{4,5},{5,4},{6,7},{7,6},{8,9},{9,8},{10,11... | collective-permute-start | bytes 2801672 | tf_op jit(solution)/shard_map/y_late/ppermute | solution.py:839
  79.9 12.9 %collective-permute-start.7 = (bf16[128,2048]{1,0:T(8,128)(2,1)}, bf16[128,2048]{1,0:T(8,128)(2,1)}, u32[]{:S(2)}, u32[]{:S(2)}) collective-permute-start(bf16[128,2048]{1,0:T(8,128)(2,1)} %get-tuple-element.103), channel_id=1, source_target_pairs={{0,1},{1,0},{2,3},{3,2},{4,5},{5,4},{6,7},{7,6},{8,9},{9,8},{10,11... | collective-permute-start | bytes 1572872 | tf_op jit(solution)/shard_map/y_u/ppermute | solution.py:839
  90.1 22.7 %collective-permute-start.8 = (bf16[128,3584]{1,0:T(8,128)(2,1)}, bf16[128,3584]{1,0:T(8,128)(2,1)}, u32[]{:S(2)}, u32[]{:S(2)}) collective-permute-start(bf16[128,3584]{1,0:T(8,128)(2,1)} %get-tuple-element.106), channel_id=1, source_target_pairs={{0,1},{1,0},{2,3},{3,2},{4,5},{5,4},{6,7},{7,6},{8,9},{9,8},{10,11... | collective-permute-start | bytes 2752520 | tf_op jit(solution)/shard_map/y_v/ppermute | solution.py:839
  92.8 20.0 %collective-permute-start.9 = (bf16[128,2048]{1,0:T(8,128)(2,1)}, bf16[128,2048]{1,0:T(8,128)(2,1)}, u32[]{:S(2)}, u32[]{:S(2)}) collective-permute-start(bf16[128,2048]{1,0:T(8,128)(2,1)} %collective-permute-done.7.refs_1_), channel_id=1, source_target_pairs={{0,4},{2,6},{4,0},{6,2},{8,12},{10,14},{12,8},{14,10},{16,20},{18,... | collective-permute-start | bytes 1572872 | tf_op jit(solution)/shard_map/x_u/ppermute | solution.py:843
  112.8 30.3 %all-to-all-start.2 = ((bf16[16,128,256]{2,1,0:T(8,128)(2,1)}), bf16[16,128,256]{2,1,0:T(8,128)(2,1)}, u32[]{:S(2)}, u32[]{:S(2)}) async-start(bf16[16,128,256]{2,1,0:T(8,128)(2,1)} %bitcast.14), calls=%async_computation.2 | async-start | bytes 2097152 | tf_op jit(solution)/shard_map/all_to_all | solution.py:959
  119.8 38.0 %collective-permute-start.15 = (bf16[128,3584]{1,0:T(8,128)(2,1)}, bf16[128,3584]{1,0:T(8,128)(2,1)}, u32[]{:S(2)}, u32[]{:S(2)}) collective-permute-start(bf16[128,3584]{1,0:T(8,128)(2,1)} %collective-permute-done.8.refs_15_), channel_id=1, source_target_pairs={{0,4},{2,6},{4,0},{6,2},{8,12},{10,14},{12,8},{14,10},{16,20},{18,... | collective-permute-start | bytes 2752520 | tf_op jit(solution)/shard_map/x_v/ppermute | solution.py:843
  121.2 6.9 %collective-permute-start.11 = (bf16[128,2048]{1,0:T(8,128)(2,1)}, bf16[128,2048]{1,0:T(8,128)(2,1)}, u32[]{:S(2)}, u32[]{:S(2)}) collective-permute-start(bf16[128,2048]{1,0:T(8,128)(2,1)} %collective-permute-done.7.refs_1_), channel_id=1, source_target_pairs={{0,2},{2,0},{4,6},{6,4},{8,10},{10,8},{12,14},{14,12},{16,18},{18,... | collective-permute-start | bytes 1572872 | tf_op jit(solution)/shard_map/c_uy/ppermute | solution.py:847
  121.9 6.3 %collective-permute-start.12 = (bf16[128,2048]{1,0:T(8,128)(2,1)}, bf16[128,2048]{1,0:T(8,128)(2,1)}, u32[]{:S(2)}, u32[]{:S(2)}) collective-permute-start(bf16[128,2048]{1,0:T(8,128)(2,1)} %collective-permute-done.9.refs_2_), channel_id=1, source_target_pairs={{0,2},{2,0},{4,6},{6,4},{8,10},{10,8},{12,14},{14,12},{16,18},{18,... | collective-permute-start | bytes 1572872 | tf_op jit(solution)/shard_map/c_ux/ppermute | solution.py:847
  121.9 6.3 %collective-permute-start.10 = (bf16[48,2048]{1,0:T(8,128)(2,1)}, bf16[48,2048]{1,0:T(8,128)(2,1)}, u32[]{:S(2)}, u32[]{:S(2)}) collective-permute-start(bf16[48,2048]{1,0:T(8,128)(2,1)} %get-tuple-element.112), channel_id=1, source_target_pairs={{0,1},{1,0},{2,3},{3,2},{4,5},{5,4},{6,7},{7,6},{8,9},{9,8},{10,11... | collective-permute-start | bytes 589832 | tf_op jit(solution)/shard_map/y_pack/ppermute | solution.py:839
  132.8 6.8 %collective-permute-start.13 = (bf16[128,1024]{1,0:T(8,128)(2,1)}, bf16[128,1024]{1,0:T(8,128)(2,1)}, u32[]{:S(2)}, u32[]{:S(2)}) collective-permute-start(bf16[128,1024]{1,0:T(8,128)(2,1)} %get-tuple-element.118), channel_id=1, source_target_pairs={{0,1},{1,0},{2,3},{3,2},{4,5},{5,4},{6,7},{7,6},{8,9},{9,8},{10,11... | collective-permute-start | bytes 786440 | tf_op jit(solution)/shard_map/y_back/ppermute | solution.py:839
  134.0 13.6 %collective-permute-start.14 = (bf16[128,1024]{1,0:T(8,128)(2,1)}, bf16[128,1024]{1,0:T(8,128)(2,1)}, u32[]{:S(2)}, u32[]{:S(2)}) collective-permute-start(bf16[128,1024]{1,0:T(8,128)(2,1)} %get-tuple-element.126), channel_id=1, source_target_pairs={{0,1},{1,0},{2,3},{3,2},{4,5},{5,4},{6,7},{7,6},{8,9},{9,8},{10,11... | collective-permute-start | bytes 786440 | tf_op jit(solution)/shard_map/y_rest/ppermute | solution.py:839
  134.3 16.5 %collective-permute-start.18 = (bf16[256,512]{1,0:T(8,128)(2,1)}, bf16[256,512]{1,0:T(8,128)(2,1)}, u32[]{:S(2)}, u32[]{:S(2)}) collective-permute-start(bf16[256,512]{1,0:T(8,128)(2,1)} %get-tuple-element.132), channel_id=1, source_target_pairs={{0,1},{1,0},{2,3},{3,2},{4,5},{5,4},{6,7},{7,6},{8,9},{9,8},{10,11... | collective-permute-start | bytes 786440 | tf_op jit(solution)/shard_map/y_w/ppermute | solution.py:839
  150.9 22.4 %all-to-all-start.3 = ((bf16[32,16,512]{2,1,0:T(8,128)(2,1)}), bf16[32,16,512]{2,1,0:T(8,128)(2,1)}, u32[]{:S(2)}, u32[]{:S(2)}) async-start(bf16[32,16,512]{2,1,0:T(8,128)(2,1)} %get-tuple-element.136), calls=%async_computation.3 | async-start | bytes 1048576 | tf_op jit(solution)/shard_map/all_to_all | solution.py:1072
  157.4 2.9 %collective-permute-start.16 = (bf16[128,3584]{1,0:T(8,128)(2,1)}, bf16[128,3584]{1,0:T(8,128)(2,1)}, u32[]{:S(2)}, u32[]{:S(2)}) collective-permute-start(bf16[128,3584]{1,0:T(8,128)(2,1)} %collective-permute-done.8.refs_15_), channel_id=1, source_target_pairs={{0,2},{2,0},{4,6},{6,4},{8,10},{10,8},{12,14},{14,12},{16,18},{18,... | collective-permute-start | bytes 2752520 | tf_op jit(solution)/shard_map/c_vy/ppermute | solution.py:847
  157.8 4.2 %collective-permute-start.17 = (bf16[128,3584]{1,0:T(8,128)(2,1)}, bf16[128,3584]{1,0:T(8,128)(2,1)}, u32[]{:S(2)}, u32[]{:S(2)}) collective-permute-start(bf16[128,3584]{1,0:T(8,128)(2,1)} %collective-permute-done.15.refs_16_), channel_id=1, source_target_pairs={{0,2},{2,0},{4,6},{6,4},{8,10},{10,8},{12,14},{14,12},{16,18},{18,... | collective-permute-start | bytes 2752520 | tf_op jit(solution)/shard_map/c_vx/ppermute | solution.py:847
  158.0 4.0 %collective-permute-start.19 = (bf16[256,512]{1,0:T(8,128)(2,1)}, bf16[256,512]{1,0:T(8,128)(2,1)}, u32[]{:S(2)}, u32[]{:S(2)}) collective-permute-start(bf16[256,512]{1,0:T(8,128)(2,1)} %collective-permute-done.18.refs_19_), channel_id=1, source_target_pairs={{0,2},{2,0},{4,6},{6,4},{8,10},{10,8},{12,14},{14,12},{16,18},{18,... | collective-permute-start | bytes 786440 | tf_op jit(solution)/shard_map/c_w/ppermute | solution.py:847

commit v3 on v2

--- a/solution.py
+++ b/solution.py
@@ -19,7 +19,7 @@
 CB = 512
 NB = COLS // CB
 WIDE = 512
-W_CUT = 2560
+W_CUT = 1536
 HALF = FF // 2 // CB
 TILE = 256
 
@@ -84,14 +84,12 @@
         copy.start()
         self.pending.append(copy)
 
-    def store(self, buffer, at=None, into=None):
+    def store(self, buffer, at=None, into=None, sem=0):
         target, sems = self.targets[id(buffer)]
-        if into is not None:
-            self.start(buffer, target.at[into], sems.at[0])
-        elif at is None:
-            self.start(buffer, target, sems.at[0])
-        else:
-            self.start(buffer.at[at], target.at[at], sems.at[at])
+        if at is not None and into is None:
+            into, sem = at, at
+        source = buffer if at is None else buffer.at[at]
+        self.start(source, target if into is None else target.at[into], sems.at[sem])
 
 
 def staged(body, loads, results, raws=None, scalars=None, scratch=(), parts=None, micros=2, inside=None, alias=None):
@@ -189,8 +187,11 @@
     stage.store(out.mlp)
 
 
-def tables(stage):
+def tables(stage, sem):
     order, starts, out = stage.scalar.order, stage.scalar.starts, stage.out
+    source = stage.raw.up
+    copy = pltpu.make_async_copy(source.at[own_part(source, 4), hidden_columns(HALF)], out.up, sem)
+    copy.start()
     rows, lanes = out.tab.shape[1:]
     ndoc = starts.shape[1]
     ctx = lax.axis_index("ctx")
@@ -228,6 +229,8 @@
     out.mask_t[...] = used(out.mask_t.shape, 1)
     stage.store(out.mask)
     stage.store(out.mask_t)
+    copy.wait()
+    stage.store(out.up)
 
 
 def choose_adapters(stage):
@@ -266,7 +269,7 @@
     return rows_at(part_orders(share)[0] * rows, rows)
 
 
-def place_weights(own, chunks, target, sems, first):
+def place_weights(own, chunks, target, sems, first=0):
     half = own.shape[0]
     own_half = lax.axis_index("wsh")
     copies = [pltpu.make_async_copy(own, target.at[rows_at(own_half * half, half), :], sems.at[first])]
@@ -575,8 +578,7 @@
     copies = [
         pltpu.make_async_copy(weight.at[mine, :], out.first.at[:, :D], sems.at[0]),
         pltpu.make_async_copy(qkv.at[mine, :W_CUT], out.first.at[:, D:], sems.at[1]),
-        pltpu.make_async_copy(qkv.at[own_part(qkv, 2), W_CUT:], out.second, sems.at[2]),
-        pltpu.make_async_copy(stage.raw.up.at[mine, hidden_columns(HALF)], out.up, sems.at[3]),
+        pltpu.make_async_copy(qkv.at[mine, W_CUT:], out.second, sems.at[2]),
     ]
     for copy in copies:
         copy.start()
@@ -594,7 +596,7 @@
     stage.store(out.products)
     for copy in copies:
         copy.wait()
-    for buffer in (out.up, out.first, out.second):
+    for buffer in (out.first, out.second):
         stage.store(buffer)
 
 
@@ -603,12 +605,15 @@
     return jnp.concatenate([jnp.concatenate([one, zero], axis=1), jnp.concatenate([zero, two], axis=1)], axis=0)
 
 
-def mlp_middle(stage, weights, sems):
+def mlp_middle(stage, down_rows, up_rows, down_sems, up_sems):
     out, low = stage.out, stage.low
     copies = []
     for j in range(HALF):
-        copies.append(pltpu.make_async_copy(stage.raw.down.at[cut(j, CB), :], weights.at[j], sems.at[j]))
+        copies.append(pltpu.make_async_copy(stage.raw.down.at[cut(j, CB), :], down_rows.at[j], down_sems.at[j]))
         copies[-1].start()
+    up_copies = place_weights(
+        stage.raw.up.at[:, hidden_columns(0)], [(0, 0, HALF * CB, stage.raw.u)], up_rows, up_sems, 0
+    )
     grads = jnp.concatenate([stage.grad[...], stage.grad_given[...]], axis=0)
     rows = grads.shape[0] // 2
     products, late = stage.products[...], stage.late
@@ -616,6 +621,7 @@
     other = late[share_at(2, 0, rank, 2 * rows)]
     inner, back = (diagonal(products[:, cut(i, rows)], other[:, cut(i, rows)]) for i in range(2))
     sums = None
+    grad_ups = []
     for j in range(HALF):
         at = cut(j, CB)
         a_both = jnp.concatenate([adapter_block(low, A_DOWN, j), late[share_at(0, j, rank, 2 * rows)]], axis=0)
@@ -628,64 +634,62 @@
         hidden = (up * spread).astype(bf16)
         slope = spread + up * (jnp.exp(-0.5 * up * up) * (0.5 / jnp.pi) ** 0.5)
         copies[j].wait()
-        down = weights[j]
+        down = down_rows[j]
         grad_hidden = dot_nt(grads, down) + dot_tn(back, a_both)
         grad_up = (grad_hidden * slope).astype(bf16)
-        out.grad_up[j] = grad_up
-        stage.store(out.grad_up, j)
+        grad_ups.append(grad_up)
         parts = dot_nn(hidden, down), dot_nt(a_both, hidden), dot_nt(b_both, grad_up)
         sums = parts if sums is None else tuple(one + two for one, two in zip(sums, parts))
         a_grad = dot_nn(back, hidden).astype(bf16)
         b_grad = (adapter_scale * dot_nn(inner, grad_up)).astype(bf16)
         out.grads[j], out.grads[HALF + j] = a_grad[:rank], b_grad[:rank]
-        out.pack[0:rank, at], out.pack[rank : 2 * rank, at] = a_grad[rank:], b_grad[rank:]
+        out.pack[pack_at(0, j, rank)], out.pack[pack_at(1, j, rank)] = a_grad[rank:], b_grad[rank:]
     down, inner_down, gi_up = sums
-    out.down[...] = down[:rows]
     out.small[0], out.small[1] = inner_down[:rank, :rows], gi_up[:rank, :rows]
-    out.pack[2 * rank : 3 * rank, :] = jnp.zeros((rank, 2 * D), bf16)
-    out.pack[2 * rank : 3 * rank, 0:rows] = inner_down[rank:, rows:].astype(bf16)
-    out.pack[2 * rank : 3 * rank, rows : 2 * rows] = gi_up[rank:, rows:].astype(bf16)
-    out.rest[...] = down[rows:].astype(bf16)
-    for buffer in (out.pack, out.small, out.grads, out.rest, out.down):
-        stage.store(buffer)
-
-
-def mlp_back(stage, weights, sems):
-    copies = place_weights(stage.raw.up.at[:, hidden_columns(0)], [(0, 0, HALF * CB, stage.raw.u)], weights, sems, 0)
-    for copy in copies:
+    out.pack[4 * rank : 5 * rank, :] = jnp.zeros((rank, D), bf16)
+    out.pack[4 * rank : 5 * rank, 0:rows] = inner_down[rank:, rows:].astype(bf16)
+    out.pack[4 * rank : 5 * rank, rows : 2 * rows] = gi_up[rank:, rows:].astype(bf16)
+    for copy in up_copies:
         copy.wait()
     total = None
     for j in range(HALF):
-        part = dot_nt(stage.grad_up[j], weights[:, cut(j, CB)])
+        part = dot_nt(grad_ups[j], up_rows[:, cut(j, CB)])
         total = part if total is None else total + part
-    rows = total.shape[0] // 2
-    stage.out.give[...] = total[rows:].astype(bf16)
-    stage.store(stage.out.give)
-    stage.out.kept[...] = total[:rows]
-    stage.store(stage.out.kept)
+    out.pack[5 * rank :, :] = total[rows:].astype(bf16)
+    stage.store(out.pack)
+    out.kept[...] = total[:rows]
+    out.rest[...] = down[rows:].astype(bf16)
+    out.down[...] = down[:rows]
+    for buffer in (out.small, out.grads, out.kept, out.rest, out.down):
+        stage.store(buffer)
+
+
+def pack_at(kind, j, rank):
+    return pl.ds((2 * kind + j // 2) * rank, rank), cut(j % 2, CB)
 
 
 def mlp_finish(stage):
     out, low, mask = stage.out, stage.low, stage.mask_t[...]
     rank, rows = mask.shape
     pack, small, wsh = stage.pack, stage.small, lax.axis_index("wsh")
-    extra = pack[2 * rank : 3 * rank, :].astype(f32)
+    extra = pack[4 * rank : 5 * rank, :].astype(f32)
     inner_down = ((small[0] + extra[:, 0:rows]) * mask).astype(bf16)
     gi_up = (adapter_scale * (small[1] + extra[:, rows : 2 * rows]) * mask).astype(bf16)
     for j in range(HALF):
         for kind in range(2):
-            out.grads[2 + kind * 2 * HALF + wsh * HALF + j] = stage.grads[kind * HALF + j]
-            other = pack[kind * rank : (kind + 1) * rank, cut(j, CB)]
-            out.grads[2 + kind * 2 * HALF + (1 - wsh) * HALF + j] = other
+            out.flat[2 + kind * 2 * HALF + wsh * HALF + j] = stage.grads[kind * HALF + j]
+            out.flat[2 + kind * 2 * HALF + (1 - wsh) * HALF + j] = pack[pack_at(kind, j, rank)]
     up_grad = dot_nn(gi_up, stage.h[...])
     down_grad = adapter_scale * dot_nn(inner_down, stage.grad[...])
     for i in range(2):
-        out.grads[i] = up_grad[:, cut(i, CB)].astype(bf16)
-        out.grads[18 + i] = down_grad[:, cut(i, CB)].astype(bf16)
-    stage.store(out.grads)
+        out.flat[i] = up_grad[:, cut(i, CB)].astype(bf16)
+        out.flat[18 + i] = down_grad[:, cut(i, CB)].astype(bf16)
+    per = D // CB
+    stage.store(out.flat, at=pl.ds(0, 10), into=pl.ds(A_UP * per, 10), sem=0)
+    stage.store(out.flat, at=pl.ds(10, 10), into=pl.ds(B_UP * per, 10), sem=1)
     out.inner_down[...] = inner_down
     stage.store(out.inner_down)
-    out.back[...] = stage.kept[...] + stage.given[...].astype(f32) + dot_tn(gi_up, low[A_UP])
+    out.back[...] = stage.kept[...] + pack[5 * rank :, :].astype(f32) + dot_tn(gi_up, low[A_UP])
     stage.store(out.back)
 
 
@@ -713,26 +717,25 @@
     per = D // CB
 
     def put(block, value):
+        place = block if block < A_UP else block - B_QKV + A_UP
         for i in range(per):
-            flat[block * per + i] = value[:, cut(i, CB)].astype(bf16)
+            flat[place * per + i] = value[:, cut(i, CB)].astype(bf16)
 
     put(A_QKV, dot_tn(gi, h[...]))
     put(A_OUT, dot_tn(stage.grad_inner[...], att[...]))
     put(B_OUT, adapter_scale * dot_tn(inner_out, grad[...]))
     for i in range(3):
         put(B_QKV + i, adapter_scale * dot_tn(stage.inner[...], gq[:, cut(i)]))
-    flat[A_UP * per : A_UP * per + 10] = stage.mlp[0:10]
-    flat[B_UP * per : B_UP * per + 10] = stage.mlp[10:20]
-    stage.store(flat)
-
-
-def outputs(stage, wq, wo, sems):
-    raw = stage.raw
-    o_copies = place_weights(raw.out, [(0, 0, D, raw.v)], wo, sems, 0)
-    q_copies = place_weights(raw.qkv, [(0, D, W_CUT, raw.v), (W_CUT, 0, 3 * D - W_CUT, raw.w)], wq, sems, 5)
-    tok, grad, low, gain, bias = stage.tok, stage.grad, stage.low, stage.gain, stage.bias
-    att, inner_out, inner_down, back = stage.att[...], stage.inner_out[...], stage.inner_down[...], stage.back
-    block = stage.out.block
+    first, rest = A_UP * per, (B_UP - B_QKV) * per
+    stage.store(flat, at=pl.ds(0, first), into=pl.ds(0, first), sem=0)
+    stage.store(flat, at=pl.ds(first, rest), into=pl.ds(B_QKV * per, rest), sem=1)
+
+
+def first_outputs(stage, wq, wo, sems):
+    raw, low, bias = stage.raw, stage.low, stage.bias
+    o_copies = place_weights(raw.out, [(0, 0, D, raw.v)], wo, sems)
+    q_copies = place_weights(raw.qkv.at[:, :W_CUT], [(0, D, W_CUT, raw.v)], wq, sems, 5)
+    att, inner_out, inner_down = stage.att[...], stage.inner_out[...], stage.inner_down[...]
     for copy in o_copies:
         copy.wait()
     for n in range(D // WIDE):
@@ -740,18 +743,29 @@
         shift = n * WIDE
         part = dot_nn(att, wo[:, at]) + bias[:, 3 * D + shift : 3 * D + shift + WIDE]
         part = part + adapter_scale * dot_nn(inner_out, low[B_OUT][:, at])
-        mlp = stage.down[:, at] + stage.rest[:, at].astype(f32) + bias[:, 4 * D + FF + shift : 4 * D + FF + shift + WIDE]
+        mlp = stage.down[:, at] + bias[:, 4 * D + FF + shift : 4 * D + FF + shift + WIDE]
         mlp = mlp + adapter_scale * dot_tn(inner_down, low[B_DOWN][:, at])
-        block[:, at] = (part + tok[:, at].astype(f32) + mlp).astype(bf16)
-    stage.store(block)
-    normed, scale = normalize(tok[...].astype(f32))
+        stage.out.block[:, at] = part + stage.tok[:, at].astype(f32) + mlp
+    stage.store(stage.out.block)
     for copy in q_copies:
         copy.wait()
-    grad_h = dot_nt(stage.gq[...], wq[...]) + dot_nn(stage.gi[...], low[A_QKV])
-    grad_n = grad_h * gain[0:1, :] + back[...] * gain[1:2, :]
+    stage.out.grad_h[...] = dot_nt(stage.gq[:, :W_CUT], wq[...]) + dot_nn(stage.gi[...], low[A_QKV])
+    stage.store(stage.out.grad_h)
+
+
+def last_outputs(stage, wq, sems):
+    raw, gain, out = stage.raw, stage.gain, stage.out
+    copies = place_weights(raw.qkv.at[:, W_CUT:], [(0, 0, 3 * D - W_CUT, raw.w)], wq, sems)
+    normed, scale = normalize(stage.tok[...].astype(f32))
+    out.block[...] = (stage.block[...] + stage.rest[...].astype(f32)).astype(bf16)
+    stage.store(out.block)
+    for copy in copies:
+        copy.wait()
+    grad_h = stage.grad_h[...] + dot_nt(stage.gq[:, W_CUT:], wq[...])
+    grad_n = grad_h * gain[0:1, :] + stage.back[...] * gain[1:2, :]
     grad_v = grad_n - jnp.mean(grad_n, axis=-1, keepdims=True) - normed * jnp.mean(grad_n * normed, axis=-1, keepdims=True)
-    stage.out.tokens[...] = grad[...].astype(f32) + scale * grad_v
-    stage.store(stage.out.tokens)
+    out.tokens[...] = stage.grad[...].astype(f32) + scale * grad_v
+    stage.store(out.tokens)
 
 
 def adamw(stage):
@@ -899,8 +913,10 @@
     table = staged(
         tables,
         {},
-        dict(tab=shape((3, tok_dev, 128), f32), mask=shape((tok_dev, rank), f32), mask_t=shape((rank, tok_dev), f32)),
+        dict(tab=shape((3, tok_dev, 128), f32), mask=shape((tok_dev, rank), f32), mask_t=shape((rank, tok_dev), f32), up=shape((D // 8, HALF * CB))),
+        raws=dict(up=up_weight),
         scalars=dict(order=tie(block_order, both.give), starts=doc_starts),
+        scratch=[pltpu.SemaphoreType.DMA],
         micros=0.1,
     )
     tab, mask, mask_t = table.tab, table.mask, table.mask_t
@@ -917,13 +933,12 @@
         scratch=[pltpu.VMEM((2 * HALF, D // 2, CB), bf16), pltpu.SemaphoreType.DMA((2 * HALF,))],
         micros=0.1,
     )
-    early_given = to_y(up.early, "early")
     heads = shape((HEADS, 2, tok_dev, 2 * HEAD_DIM))
     one = (HEADS, tok_dev, 2 * HEAD_DIM)
     made = staged(
         queries_keys,
         dict(
-            h=tie(h_attn, up.early),
+            h=tie(h_attn, up.kept),
             grad=grad,
             low=low,
             mask=mask,
@@ -965,20 +980,37 @@
             late=shape(up.late.shape),
             products=shape((rank, 2 * tok_dev)),
             first=shape((D // 8, D + W_CUT)),
-            second=shape((D // 4, 3 * D - W_CUT)),
-            up=shape((D // 8, HALF * CB)),
+            second=shape((D // 8, 3 * D - W_CUT)),
         ),
-        raws=dict(late=up.late, qkv=qkv_weight, out=out_weight, up=up_weight),
+        raws=dict(late=up.late, qkv=qkv_weight, out=out_weight),
         inside=dict(late=(3 * rank, (HALF - 1) * CB)),
         alias=dict(late="late"),
-        scratch=[pltpu.SemaphoreType.DMA((4,))],
-    )
+        scratch=[pltpu.SemaphoreType.DMA((3,))],
+    )
+
+    def quarters(y, x, name, *after):
+        return [y, x, to_core(tie(y, *after), name + "y"), to_core(tie(x, *after), name + "x")]
+
+    u_y = to_y(table.up, "u")
+    early_given = to_y(up.early, "early")
+    u_x = to_x(tie(u_y, early_given, shared.products), "u")
     late_given = to_y(shared.late, "late")
+    arrived = tie(exchange(made.send), u_y)
+    if parts == 1 and ndoc == 1:
+        done = attention_one_document(block_order, arrived)
+    else:
+        all_pos, all_doc, _, _ = stream_layout(
+            block_order[0], doc_starts[0], jnp.arange(total_rows, dtype=jnp.int32), total_rows, half_dev
+        )
+        far = None if parts == 1 else [[g * HEADS + i for g in range(parts)] for i in range(HEADS)]
+        done = attention_documents(arrived, all_pos, all_doc, far, ctx // HEADS * HEADS * tok_dev)
+    back = exchange(tie(done.reshape(HEADS, tok_dev, 4 * HEAD_DIM), u_x, late_given))
+    v_y = to_y(tie(shared.first, done), "v")
     middle = staged(
         mlp_middle,
         dict(
             kept=up.kept,
-            early=early_given,
+            early=tie(early_given, done),
             late=late_given,
             grad=grad,
             grad_given=grad_given,
@@ -987,63 +1019,26 @@
             products=shared.products,
         ),
         dict(
-            grad_up=shape((HALF, 2 * tok_dev, CB)),
-            down=shape((tok_dev, D), f32),
+            pack=shape((5 * rank + tok_dev, D)),
             small=shape((2, rank, tok_dev), f32),
             grads=shape((2 * HALF, rank, CB)),
-            pack=shape((3 * rank, 2 * D)),
+            kept=shape((tok_dev, D), f32),
             rest=shape((tok_dev, D)),
+            down=shape((tok_dev, D), f32),
         ),
-        raws=dict(down=down_weight),
-        scratch=[pltpu.VMEM((HALF, CB, D), bf16), pltpu.SemaphoreType.DMA((HALF,))],
-        parts=dict(grad_up=HALF),
+        raws=dict(down=down_weight, up=up_weight, u=quarters(u_y, u_x, "u", done)),
+        scratch=[
+            pltpu.VMEM((HALF, CB, D), bf16),
+            pltpu.VMEM((D, HALF * CB), bf16),
+            pltpu.SemaphoreType.DMA((HALF,)),
+            pltpu.SemaphoreType.DMA((5,)),
+        ],
         micros=0.1,
     )
-    def quarters(y, x, name, *after):
-        return [y, x, to_core(tie(y, *after), name + "y"), to_core(tie(x, *after), name + "x")]
-
-    u_y = to_y(tie(shared.up, late_given), "u")
-    u_x = to_x(u_y, "u")
-    v_y = to_y(tie(shared.first, middle.pack), "v")
-    arrived = tie(exchange(tie(made.send, early_given, shared.products)), middle.pack, u_y)
-    if parts == 1 and ndoc == 1:
-        done = attention_one_document(block_order, arrived)
-    else:
-        all_pos, all_doc, _, _ = stream_layout(
-            block_order[0], doc_starts[0], jnp.arange(total_rows, dtype=jnp.int32), total_rows, half_dev
-        )
-        far = None if parts == 1 else [[g * HEADS + i for g in range(parts)] for i in range(HEADS)]
-        done = attention_documents(arrived, all_pos, all_doc, far, ctx // HEADS * HEADS * tok_dev)
-    back = exchange(tie(done.reshape(HEADS, tok_dev, 4 * HEAD_DIM), v_y, u_x))
-    v_x = to_x(tie(v_y, done), "v")
-    pack_given = to_y(tie(middle.pack, done), "pack")
-    last = staged(
-        mlp_back,
-        dict(grad_up=tie(middle.grad_up, pack_given)),
-        dict(give=shape((tok_dev, D)), kept=shape((tok_dev, D), f32)),
-        raws=dict(up=up_weight, u=quarters(u_y, u_x, "u", done)),
-        scratch=[pltpu.VMEM((D, HALF * CB), bf16), pltpu.SemaphoreType.DMA((5,))],
-        micros=0.1,
-    )
-    back_given = to_y(last.give, "back")
-    w_y = to_y(tie(shared.second, last.give), "w")
-    rest_given = to_y(tie(middle.rest, last.give), "rest")
-    mlp = staged(
-        mlp_finish,
-        dict(
-            small=middle.small,
-            grads=middle.grads,
-            pack=pack_given,
-            kept=last.kept,
-            given=back_given,
-            h=h_mlp,
-            grad=grad,
-            low=low,
-            mask_t=mask_t,
-        ),
-        dict(inner_down=shape((rank, tok_dev)), back=shape((tok_dev, D), f32), grads=shape((20, rank, CB))),
-        micros=0.1,
-    )
+    pack_given = to_y(middle.pack, "pack")
+    v_x = to_x(tie(v_y, middle.pack), "v")
+    w_y = to_y(tie(shared.second, pack_given), "w")
+    rest_given = to_y(tie(middle.rest, pack_given), "rest")
     tail = staged(
         adapter_gradients,
         dict(
@@ -1055,7 +1050,6 @@
             grad=grad,
             inner=inner_qkv,
             grad_inner=grad_inner_out,
-            mlp=mlp.grads,
         ),
         dict(
             att=shape((tok_dev, D)),
@@ -1064,18 +1058,39 @@
             gi=shape((tok_dev, rank)),
             flat=shape((NB, rank, CB)),
         ),
+        inside=dict(flat=(12, rank, CB)),
+        parts=dict(flat=2),
         micros=0.1,
     )
-    flat = tail.flat
+    mlp = staged(
+        mlp_finish,
+        dict(
+            small=middle.small,
+            grads=middle.grads,
+            pack=pack_given,
+            kept=middle.kept,
+            h=h_mlp,
+            grad=grad,
+            low=low,
+            mask_t=mask_t,
+        ),
+        dict(inner_down=shape((rank, tok_dev)), back=shape((tok_dev, D), f32), flat=shape((NB, rank, CB))),
+        raws=dict(flat=tail.flat),
+        inside=dict(flat=(20, rank, CB)),
+        alias=dict(flat="flat"),
+        parts=dict(flat=2),
+        micros=0.1,
+    )
+    flat = mlp.flat
     if columns != CB:
         flat = flat.reshape(NB, rank, CB // columns, columns).transpose(0, 2, 1, 3).reshape(n_dev, rank, columns)
-    shares = lax.all_to_all(tie(flat, w_y, rest_given), ("ctx", "wsh"), 0, 0, tiled=True)
-    ends = staged(
-        outputs,
+    shares = lax.all_to_all(tie(flat, w_y), ("ctx", "wsh"), 0, 0, tiled=True)
+    v_parts = quarters(v_y, v_x, "v", tail.att)
+    w_x = to_x(tie(w_y, flat), "w")
+    firsts = staged(
+        first_outputs,
         dict(
             tok=tok,
-            grad=grad,
-            gain=norm_gains,
             att=tail.att,
             gq=tail.gq,
             inner_out=tail.inner_out,
@@ -1083,24 +1098,34 @@
             low=low,
             bias=bias,
             down=middle.down,
+            inner_down=mlp.inner_down,
+        ),
+        dict(block=shape((tok_dev, D), f32), grad_h=shape((tok_dev, D), f32)),
+        raws=dict(qkv=qkv_weight, out=out_weight, v=v_parts),
+        scratch=[pltpu.VMEM((D, W_CUT), bf16), pltpu.VMEM((D, D), bf16), pltpu.SemaphoreType.DMA((10,))],
+        micros=0.1,
+    )
+    ends = staged(
+        last_outputs,
+        dict(
+            tok=tok,
+            grad=grad,
+            gain=norm_gains,
+            gq=tail.gq,
+            back=mlp.back,
             rest=rest_given,
-            inner_down=mlp.inner_down,
-            back=mlp.back,
+            block=firsts.block,
+            grad_h=firsts.grad_h,
         ),
         dict(block=shape((tok_dev, D)), tokens=shape((tok_dev, D), f32)),
-        raws=dict(
-            qkv=qkv_weight,
-            out=out_weight,
-            v=quarters(v_y, v_x, "v", done),
-            w=[w_y, to_core(w_y, "w")],
-        ),
-        scratch=[pltpu.VMEM((D, 3 * D), bf16), pltpu.VMEM((D, D), bf16), pltpu.SemaphoreType.DMA((14,))],
+        raws=dict(qkv=qkv_weight, w=quarters(w_y, w_x, "w", firsts.block, rest_given)),
+        scratch=[pltpu.VMEM((D, 3 * D - W_CUT), bf16), pltpu.SemaphoreType.DMA((5,))],
         micros=0.1,
     )
     full = shape(adapters.shape, f32)
     new = staged(
         adamw,
-        dict(adapters=adapters, first=first_moment, second=second_moment, parts=tie(shares, ends.block), given=adapters_given),
+        dict(adapters=adapters, first=first_moment, second=second_moment, parts=shares, given=adapters_given),
         dict(grad=full, new=full, first=full, second=full, low=shape(adapters.shape)),
         scalars=dict(chosen=doc_adapter),
         parts=dict(grad=ADAPTERS, new=ADAPTERS, first=ADAPTERS, second=ADAPTERS, low=ADAPTERS),

time: 177 us -> 172 us (0.972)
  waiting for transfers between devices: 46.8 us -> 39.4 us
  starting transfers between devices: 46.4 us -> 48.3 us
    ppermute x13 -> x12, waiting for transfers between devices: 40.6 us -> 34 us  [to_y(): return lax.ppermute(a, 'wsh', [(0, 1), (1, 0)])]
    ppermute x2 -> x3, waiting for transfers between devices: 0.01 us -> 2.81 us  [to_x(): return lax.ppermute(a, 'ctx', [(i, i ^ 2) for i in range(n_ctx)])]
    ppermute x5 -> x6, waiting for transfers between devices: 3.66 us -> 1.33 us  [to_core(): return lax.ppermute(a, 'ctx', [(i, i ^ 1) for i in range(n_ctx)])]
    all_to_all x1, waiting for transfers between devices: 2.22 us -> 0.01 us  [on_device(): shares = lax.all_to_all(tie(flat, w_y), ('ctx', 'wsh'), 0, 0, tiled=True)]
    ppermute x2 -> x3, starting transfers between devices: 2.71 us -> 3.96 us  [to_x(): return lax.ppermute(a, 'ctx', [(i, i ^ 2) for i in range(n_ctx)])]
    ppermute x13 -> x12, starting transfers between devices: 14.3 us -> 14.3 us  [to_y(): return lax.ppermute(a, 'wsh', [(0, 1), (1, 0)])]
  transfers between devices with their start and end apart: 24 -> 25, of which waited for: 12 -> 13; matrix products, arithmetic and copies ran while one was open for 0% -> 0% of each run, Pallas kernels for 44% -> 42%
where the time goes in v3:
time: 172 us; the launch traced here: 171 us
  Pallas kernels  81.5 us (47%)
  starting transfers between devices  48.3 us (28%)
  waiting for transfers between devices  39.4 us (23%)
    pallas_call x17, Pallas kernels, staged(): pl.pallas_call(kernel, out_shape=tuple(results.values()), in_specs=[HBM]...  81.5 us
    ppermute x12, waiting for transfers between devices, to_y(): return lax.ppermute(a, 'wsh', [(0, 1), (1, 0)])  34 us
    ppermute x12, starting transfers between devices, to_y(): return lax.ppermute(a, 'wsh', [(0, 1), (1, 0)])  14.3 us
    all_to_all x2, starting transfers between devices, exchange(): return lax.all_to_all(a, 'ctx', 0, 0, tiled=True, axis_index_groups=near)  13.4 us
    all_to_all x1, starting transfers between devices, on_device(): shares = lax.all_to_all(tie(flat, w_y), ('ctx', 'wsh'), 0, 0, tiled=True)  7.49 us
    all_to_all x1, starting transfers between devices, on_device(): low = lax.all_to_all(chosen_rows, 'ctx', 0, 0, tiled=True)  7.28 us
    ppermute x3, starting transfers between devices, to_x(): return lax.ppermute(a, 'ctx', [(i, i ^ 2) for i in range(n_ctx)])  3.96 us
  transfers between devices with their start and end apart: 25, of which 13 were waited for; matrix products, arithmetic and copies ran while one was open for 0% of the time, Pallas kernels for 42%

profile of v3, /device:TPU:1, one launch (start us, length us, event | category | flops | bytes accessed | tf_op | source)
XLA Modules:
  0.0 170.9 jit_solution(17164895727215474617)
XLA Ops:
  4.4 2.3 %layer_norms.1 = (bf16[128,1024]{1,0:T(8,128)(2,1)}, bf16[128,1024]{1,0:T(8,128)(2,1)}, bf16[128,1024]{1,0:T(8,128)(2,1)}) custom-call(bf16[128,1024]{1,0:T(8,128)(2,1)} %bitcast.15, f32[2,1024]{1,0:T(2,128)} %refs_2_.10, f32[2,1024]{1,0:T(2,128)} %refs_2_.6), custom_call_target="tpu_custom_call" | custom-call | flops 2300000000 | bytes 1024 | tf_op jit(solution)/shard_map/layer_norms/pallas_call | solution.py:135
  10.3 7.3 %all-to-all-start = ((bf16[16,16,1024]{2,1,0:T(8,128)(2,1)}), bf16[16,16,1024]{2,1,0:T(8,128)(2,1)}, u32[]{:S(2)}, u32[]{:S(2)}) async-start(bf16[16,16,1024]{2,1,0:T(8,128)(2,1)} %choose_adapters.1), calls=%async_computation | async-start | bytes 1048576 | tf_op jit(solution)/shard_map/all_to_all | solution.py:886
  17.6 4.0 %partial_qk.1 = (bf16[128,2048]{1,0:T(8,128)(2,1)}, f32[4,128,512]{2,1,0:T(8,128)}) custom-call(bf16[128,1024]{1,0:T(8,128)(2,1)} %get-tuple-element.88.refs_0_.refs_4_, bf16[128,1024]{1,0:T(8,128)(2,1)} %collective-permute-done.refs_1_, bf16[512,3072]{1,0:T(8,128)(2,1)} %refs_8_.3), custom_call_target="tpu_custom_call" | custom-call | flops 3449999872 | bytes 1024 | tf_op jit(solution)/shard_map/partial_qk/pallas_call | solution.py:135
  23.4 3.4 %partial_vg.1 = (bf16[128,1536]{1,0:T(8,128)(2,1)}, f32[3,128,512]{2,1,0:T(8,128)}) custom-call(bf16[128,1024]{1,0:T(8,128)(2,1)} %get-tuple-element.88.refs_0_.refs_4_, bf16[128,1024]{1,0:T(8,128)(2,1)} %collective-permute-done.refs_1_, bf16[128,1024]{1,0:T(8,128)(2,1)} %bitcast.7, bf16[128,1024]{1,0:T(8,128)(2,1)} %collective-permute-done.2.refs_3_.refs_4_, ...), custom_call_target="tpu_custom_call" | custom-call | flops 3449999872 | bytes 1024 | tf_op jit(solution)/shard_map/partial_vg/pallas_call | solution.py:135
  27.6 6.0 %mlp_up.1 = (bf16[256,512]{1,0:T(8,128)(2,1)}, bf16[304,1536]{1,0:T(8,128)(2,1)}, f32[4,256,512]{2,1,0:T(8,128)}) custom-call(bf16[128,1024]{1,0:T(8,128)(2,1)} %get-tuple-element.86.refs_0_.refs_4_, bf16[128,1024]{1,0:T(8,128)(2,1)} %collective-permute-done.refs_1_, bf16[512,4096]{1,0:T(8,128)(2,1)} %refs_13_.1), custom_call_target="tpu_custom_call" | custom-call | flops 115000000 | bytes 1024 | tf_op jit(solution)/shard_map/mlp_up/pallas_call | solution.py:135
  33.6 2.7 %tables.1 = (f32[3,128,128]{2,1,0:T(8,128)}, f32[128,16]{1,0:T(8,128)}, f32[16,128]{1,0:T(8,128)}, bf16[128,2048]{1,0:T(8,128)(2,1)}) custom-call(s32[1,32]{1,0:T(1,128)} %refs_0_.7, s32[1,1]{1,0:T(1,128)S(6)} %copy.28.refs_1_, bf16[512,4096]{1,0:T(8,128)(2,1)} %refs_13_.1), custom_call_target="tpu_custom_call" | custom-call | flops 115000000 | bytes 1024 | tf_op jit(solution)/shard_map/tables/pallas_call | solution.py:135
  36.4 4.6 %queries_keys.1 = (bf16[128,16]{1,0:T(8,128)(2,1)}, bf16[128,16]{1,0:T(8,128)(2,1)}, bf16[16,2,128,128]{3,2,1,0:T(8,128)(2,1)}, f32[4,128,512]{2,1,0:T(8,128)}) custom-call(bf16[128,1024]{1,0:T(8,128)(2,1)} %get-tuple-element.88.refs_0_.refs_4_, bf16[128,1024]{1,0:T(8,128)(2,1)} %bitcast.8, bf16[16,16,1024]{2,1,0:T(8,128)(2,1)} %all-to-all-done.refs_2_.refs_5_.refs_6_, ...), custom_call_target="tpu_custom_call" | custom-call | flops 115000000 | bytes 1024 | tf_op jit(solution)/shard_map/queries_keys/pallas_call | solution.py:135
  41.0 3.3 %collective-permute-done.4.refs_1_ = bf16[128,1536]{1,0:T(8,128)(2,1)} collective-permute-done((bf16[128,1536]{1,0:T(8,128)(2,1)}, bf16[128,1536]{1,0:T(8,128)(2,1)}, u32[]{:S(2)}, u32[]{:S(2)}) %collective-permute-start.4) | collective-permute-done | bytes 393248 | tf_op jit(solution)/shard_map/y_vg/ppermute | solution.py:853
  44.3 2.4 %values_grads.1 = bf16[16,2,128,128]{3,2,1,0:T(8,128)(2,1)} custom-call(f32[4,128,512]{2,1,0:T(8,128)} %get-tuple-element.94.refs_0_, bf16[128,1536]{1,0:T(8,128)(2,1)} %collective-permute-done.4.refs_1_, bf16[16,2,128,128]{3,2,1,0:T(8,128)(2,1)} %get-tuple-element.95.refs_2_), custom_call_target="tpu_custom_call", output_to_operand_aliasing={{}: (2, {})} | custom-call | flops 3449999872 | bytes 1024 | tf_op jit(solution)/shard_map/values_grads/pallas_call | solution.py:135
  46.7 6.4 %all-to-all-start.1 = ((bf16[16,2,128,128]{3,2,1,0:T(8,128)(2,1)}), bf16[16,2,128,128]{3,2,1,0:T(8,128)(2,1)}, u32[]{:S(2)}, u32[]{:S(2)}) async-start(bf16[16,2,128,128]{3,2,1,0:T(8,128)(2,1)} %values_grads.1), calls=%async_computation.1 | async-start | bytes 2097152 | tf_op jit(solution)/shard_map/all_to_all | solution.py:974
  54.7 2.9 %mlp_share.1 = (bf16[304,1536]{1,0:T(8,128)(2,1)}, bf16[16,256]{1,0:T(8,128)(2,1)}, bf16[128,2560]{1,0:T(8,128)(2,1)}, bf16[128,1536]{1,0:T(8,128)(2,1)}) custom-call(bf16[128,1024]{1,0:T(8,128)(2,1)} %get-tuple-element.86.refs_0_.refs_4_, bf16[128,1024]{1,0:T(8,128)(2,1)} %bitcast.9, ...), custom_call_target="tpu_custom_call", output_to_operand_aliasing={{0}: (4, {})} | custom-call | flops 2300000000 | bytes 1024 | tf_op jit(solution)/shard_map/mlp_share/pallas_call | solution.py:135
  57.6 14.7 %collective-permute-done.6.refs_1_ = bf16[256,512]{1,0:T(8,128)(2,1)} collective-permute-done((bf16[256,512]{1,0:T(8,128)(2,1)}, bf16[256,512]{1,0:T(8,128)(2,1)}, u32[]{:S(2)}, u32[]{:S(2)}) %collective-permute-start.6) | collective-permute-done | bytes 262176 | tf_op jit(solution)/shard_map/y_early/ppermute | solution.py:853
  76.4 16.8 %attention.1 = bf16[2048,256]{1,0:T(8,128)(2,1)} custom-call(s32[1,32]{1,0:T(1,128)} %refs_0_.7, bf16[16,2,128,128]{3,2,1,0:T(8,128)(2,1)} %all-to-all-done.1.refs_1_), custom_call_target="tpu_custom_call" | custom-call | flops 19549999104 | bytes 1024 | tf_op jit(solution)/shard_map/attention/pallas_call | solution.py:135
  94.7 6.9 %all-to-all-start.2 = ((bf16[16,128,256]{2,1,0:T(8,128)(2,1)}), bf16[16,128,256]{2,1,0:T(8,128)(2,1)}, u32[]{:S(2)}, u32[]{:S(2)}) async-start(bf16[16,128,256]{2,1,0:T(8,128)(2,1)} %bitcast.14), calls=%async_computation.2 | async-start | bytes 2097152 | tf_op jit(solution)/shard_map/all_to_all | solution.py:974
  104.6 10.6 %mlp_middle.1 = (bf16[208,1024]{1,0:T(8,128)(2,1)}, f32[2,16,128]{2,1,0:T(8,128)}, bf16[8,16,512]{2,1,0:T(8,128)(2,1)}, f32[128,1024]{1,0:T(8,128)}, bf16[128,1024]{1,0:T(8,128)(2,1)}, /*index=5*/f32[128,1024]{1,0:T(8,128)}) custom-call(f32[4,256,512]{2,1,0:T(8,128)} %get-tuple-element.87.refs_0_, bf16[256,512]{1,0:T(8,128)(2,1)} %collective-permute-done.6.refs_1_, ...), custom_call_target="tpu_custom_call" | custom-call | flops 115000000 | bytes 1024 | tf_op jit(solution)/shard_map/mlp_middle/pallas_call | solution.py:135
  119.8 7.9 %collective-permute-done.11.refs_2_ = bf16[208,1024]{1,0:T(8,128)(2,1)} collective-permute-done((bf16[208,1024]{1,0:T(8,128)(2,1)}, bf16[208,1024]{1,0:T(8,128)(2,1)}, u32[]{:S(2)}, u32[]{:S(2)}) %collective-permute-start.11) | collective-permute-done | bytes 426016 | tf_op jit(solution)/shard_map/y_pack/ppermute | solution.py:853
  129.2 4.4 %adapter_gradients.1 = (bf16[128,1024]{1,0:T(8,128)(2,1)}, bf16[128,3072]{1,0:T(8,128)(2,1)}, bf16[128,16]{1,0:T(8,128)(2,1)}, bf16[128,16]{1,0:T(8,128)(2,1)}, bf16[32,16,512]{2,1,0:T(8,128)(2,1)}) custom-call(bf16[16,128,256]{2,1,0:T(8,128)(2,1)} %all-to-all-done.2.refs_0_, f32[3,128,128]{2,1,0:T(8,128)} %get-tuple-element.91.refs_5_.refs_1_, ...), custom_call_target="tpu_custom_call" | custom-call | flops 115000000 | bytes 1024 | tf_op jit(solution)/shard_map/adapter_gradients/pallas_call | solution.py:135
  133.6 3.1 %mlp_finish.1 = (bf16[16,128]{1,0:T(8,128)(2,1)}, f32[128,1024]{1,0:T(8,128)}, bf16[32,16,512]{2,1,0:T(8,128)(2,1)}) custom-call(f32[2,16,128]{2,1,0:T(8,128)} %get-tuple-element.111.refs_0_, bf16[8,16,512]{2,1,0:T(8,128)(2,1)} %get-tuple-element.112.refs_1_, bf16[208,1024]{1,0:T(8,128)(2,1)} %collective-permute-done.11.refs_2_, ...), custom_call_target="tpu_custom_call", output_to_operand_aliasing={{2}: (8, {})} | custom-call | flops 115000000 | bytes 1024 | tf_op jit(solution)/shard_map/mlp_finish/pallas_call | solution.py:135
  137.6 7.5 %all-to-all-start.3 = ((bf16[32,16,512]{2,1,0:T(8,128)(2,1)}), bf16[32,16,512]{2,1,0:T(8,128)(2,1)}, u32[]{:S(2)}, u32[]{:S(2)}) async-start(bf16[32,16,512]{2,1,0:T(8,128)(2,1)} %get-tuple-element.139), calls=%async_computation.3 | async-start | bytes 1048576 | tf_op jit(solution)/shard_map/all_to_all | solution.py:1087
  148.6 6.4 %first_outputs.1 = (f32[128,1024]{1,0:T(8,128)}, f32[128,1024]{1,0:T(8,128)}) custom-call(bf16[128,1024]{1,0:T(8,128)(2,1)} %bitcast.16, bf16[128,1024]{1,0:T(8,128)(2,1)} %get-tuple-element.119.refs_1_, bf16[128,3072]{1,0:T(8,128)(2,1)} %get-tuple-element.107.refs_2_.refs_3_, bf16[128,16]{1,0:T(8,128)(2,1)} %get-tuple-element.120.refs_3_, ...), custom_call_target="tpu_custom_call" | custom-call | flops 115000000 | bytes 1024 | tf_op jit(solution)/shard_map/first_outputs/pallas_call | solution.py:135
  155.0 3.7 %collective-permute-done.12.refs_5_ = bf16[128,1024]{1,0:T(8,128)(2,1)} collective-permute-done((bf16[128,1024]{1,0:T(8,128)(2,1)}, bf16[128,1024]{1,0:T(8,128)(2,1)}, u32[]{:S(2)}, u32[]{:S(2)}) %collective-permute-start.12) | collective-permute-done | bytes 262176 | tf_op jit(solution)/shard_map/y_rest/ppermute | solution.py:853
  158.7 2.8 %collective-permute-done.18.refs_10_ = bf16[128,1536]{1,0:T(8,128)(2,1)} collective-permute-done((bf16[128,1536]{1,0:T(8,128)(2,1)}, bf16[128,1536]{1,0:T(8,128)(2,1)}, u32[]{:S(2)}, u32[]{:S(2)}) %collective-permute-start.18) | collective-permute-done | bytes 393248 | tf_op jit(solution)/shard_map/x_w/ppermute | solution.py:857
  162.3 2.9 %adamw.1 = (f32[8,16,512]{2,1,0:T(8,128)}, f32[8,16,512]{2,1,0:T(8,128)}, f32[8,16,512]{2,1,0:T(8,128)}, f32[8,16,512]{2,1,0:T(8,128)}, bf16[8,16,512]{2,1,0:T(8,128)(2,1)}) custom-call(s32[1,1,8]{2,1,0:T(1,128)} %refs_0_.8, f32[8,16,512]{2,1,0:T(8,128)} %refs_1_.8, f32[8,16,512]{2,1,0:T(8,128)} %refs_2_.11, f32[8,16,512]{2,1,0:T(8,128)} %refs_3_.1, ...), custom_call_target="tpu_custom_call" | custom-call | flops 2300000000 | bytes 1024 | tf_op jit(solution)/shard_map/adamw/pallas_call | solution.py:135
  165.3 5.5 %last_outputs.1 = (bf16[128,1024]{1,0:T(8,128)(2,1)}, f32[128,1024]{1,0:T(8,128)}) custom-call(bf16[128,1024]{1,0:T(8,128)(2,1)} %bitcast.17, bf16[128,1024]{1,0:T(8,128)(2,1)} %bitcast.13, f32[2,1024]{1,0:T(2,128)} %refs_2_.10, bf16[128,3072]{1,0:T(8,128)(2,1)} %get-tuple-element.107.refs_2_.refs_3_, f32[128,1024]{1,0:T(8,128)} %get-tuple-element.116.refs_4_, ...), custom_call_target="tpu_custom_call" | custom-call | flops 115000000 | bytes 1024 | tf_op jit(solution)/shard_map/last_outputs/pallas_call | solution.py:135
  (43 shorter events, 30.8 us)
Async XLA Ops:
  2.3 6.0 %collective-permute-start.1 = (bf16[144,512]{1,0:T(8,128)(2,1)}, bf16[144,512]{1,0:T(8,128)(2,1)}, u32[]{:S(2)}, u32[]{:S(2)}) collective-permute-start(bf16[144,512]{1,0:T(8,128)(2,1)} %give_adapters.1), channel_id=1, source_target_pairs={{0,1},{1,0},{2,3},{3,2},{4,5},{5,4},{6,7},{7,6},{8,9},{9,8},{10,11... | collective-permute-start | bytes 442376 | tf_op jit(solution)/shard_map/y_adapters/ppermute | solution.py:853
  6.7 10.9 %collective-permute-start = (bf16[128,1024]{1,0:T(8,128)(2,1)}, bf16[128,1024]{1,0:T(8,128)(2,1)}, u32[]{:S(2)}, u32[]{:S(2)}) collective-permute-start(bf16[128,1024]{1,0:T(8,128)(2,1)} %get-tuple-element.79), channel_id=1, source_target_pairs={{0,1},{1,0},{2,3},{3,2},{4,5},{5,4},{6,7},{7,6},{8,9},{9,8},{10,11... | collective-permute-start | bytes 786440 | tf_op jit(solution)/shard_map/y_h/ppermute | solution.py:853
  6.8 16.6 %collective-permute-start.2 = (bf16[128,1024]{1,0:T(8,128)(2,1)}, bf16[128,1024]{1,0:T(8,128)(2,1)}, u32[]{:S(2)}, u32[]{:S(2)}) collective-permute-start(bf16[128,1024]{1,0:T(8,128)(2,1)} %bitcast.6), channel_id=1, source_target_pairs={{0,1},{1,0},{2,3},{3,2},{4,5},{5,4},{6,7},{7,6},{8,9},{9,8},{10,11... | collective-permute-start | bytes 786440 | tf_op jit(solution)/shard_map/y_grad/ppermute | solution.py:853
  10.3 26.1 %all-to-all-start = ((bf16[16,16,1024]{2,1,0:T(8,128)(2,1)}), bf16[16,16,1024]{2,1,0:T(8,128)(2,1)}, u32[]{:S(2)}, u32[]{:S(2)}) async-start(bf16[16,16,1024]{2,1,0:T(8,128)(2,1)} %choose_adapters.1), calls=%async_computation | async-start | bytes 1048576 | tf_op jit(solution)/shard_map/all_to_all | solution.py:886
  21.5 14.8 %collective-permute-start.3 = (bf16[128,2048]{1,0:T(8,128)(2,1)}, bf16[128,2048]{1,0:T(8,128)(2,1)}, u32[]{:S(2)}, u32[]{:S(2)}) collective-permute-start(bf16[128,2048]{1,0:T(8,128)(2,1)} %get-tuple-element.82), channel_id=1, source_target_pairs={{0,1},{1,0},{2,3},{3,2},{4,5},{5,4},{6,7},{7,6},{8,9},{9,8},{10,11... | collective-permute-start | bytes 1572872 | tf_op jit(solution)/shard_map/y_qk/ppermute | solution.py:853
  26.9 17.4 %collective-permute-start.4 = (bf16[128,1536]{1,0:T(8,128)(2,1)}, bf16[128,1536]{1,0:T(8,128)(2,1)}, u32[]{:S(2)}, u32[]{:S(2)}) collective-permute-start(bf16[128,1536]{1,0:T(8,128)(2,1)} %get-tuple-element.85), channel_id=1, source_target_pairs={{0,1},{1,0},{2,3},{3,2},{4,5},{5,4},{6,7},{7,6},{8,9},{9,8},{10,11... | collective-permute-start | bytes 1179656 | tf_op jit(solution)/shard_map/y_vg/ppermute | solution.py:853
  46.7 29.6 %all-to-all-start.1 = ((bf16[16,2,128,128]{3,2,1,0:T(8,128)(2,1)}), bf16[16,2,128,128]{3,2,1,0:T(8,128)(2,1)}, u32[]{:S(2)}, u32[]{:S(2)}) async-start(bf16[16,2,128,128]{3,2,1,0:T(8,128)(2,1)} %values_grads.1), calls=%async_computation.1 | async-start | bytes 2097152 | tf_op jit(solution)/shard_map/all_to_all | solution.py:974
  53.1 19.2 %collective-permute-start.5 = (bf16[128,2048]{1,0:T(8,128)(2,1)}, bf16[128,2048]{1,0:T(8,128)(2,1)}, u32[]{:S(2)}, u32[]{:S(2)}) collective-permute-start(bf16[128,2048]{1,0:T(8,128)(2,1)} %get-tuple-element.96), channel_id=1, source_target_pairs={{0,1},{1,0},{2,3},{3,2},{4,5},{5,4},{6,7},{7,6},{8,9},{9,8},{10,11... | collective-permute-start | bytes 1572872 | tf_op jit(solution)/shard_map/y_u/ppermute | solution.py:853
  54.6 17.6 %collective-permute-start.6 = (bf16[256,512]{1,0:T(8,128)(2,1)}, bf16[256,512]{1,0:T(8,128)(2,1)}, u32[]{:S(2)}, u32[]{:S(2)}) collective-permute-start(bf16[256,512]{1,0:T(8,128)(2,1)} %get-tuple-element.98), channel_id=1, source_target_pairs={{0,1},{1,0},{2,3},{3,2},{4,5},{5,4},{6,7},{7,6},{8,9},{9,8},{10,11... | collective-permute-start | bytes 786440 | tf_op jit(solution)/shard_map/y_early/ppermute | solution.py:853
  72.3 20.9 %collective-permute-start.7 = (bf16[128,2048]{1,0:T(8,128)(2,1)}, bf16[128,2048]{1,0:T(8,128)(2,1)}, u32[]{:S(2)}, u32[]{:S(2)}) collective-permute-start(bf16[128,2048]{1,0:T(8,128)(2,1)} %collective-permute-done.5.refs_9_), channel_id=1, source_target_pairs={{0,4},{2,6},{4,0},{6,2},{8,12},{10,14},{12,8},{14,10},{16,20},{18,... | collective-permute-start | bytes 1572872 | tf_op jit(solution)/shard_map/x_u/ppermute | solution.py:857
  73.7 21.0 %collective-permute-start.8 = (bf16[304,1536]{1,0:T(8,128)(2,1)}, bf16[304,1536]{1,0:T(8,128)(2,1)}, u32[]{:S(2)}, u32[]{:S(2)}) collective-permute-start(bf16[304,1536]{1,0:T(8,128)(2,1)} %get-tuple-element.103), channel_id=1, source_target_pairs={{0,1},{1,0},{2,3},{3,2},{4,5},{5,4},{6,7},{7,6},{8,9},{9,8},{10,11... | collective-permute-start | bytes 2801672 | tf_op jit(solution)/shard_map/y_late/ppermute | solution.py:853
  94.7 34.5 %all-to-all-start.2 = ((bf16[16,128,256]{2,1,0:T(8,128)(2,1)}), bf16[16,128,256]{2,1,0:T(8,128)(2,1)}, u32[]{:S(2)}, u32[]{:S(2)}) async-start(bf16[16,128,256]{2,1,0:T(8,128)(2,1)} %bitcast.14), calls=%async_computation.2 | async-start | bytes 2097152 | tf_op jit(solution)/shard_map/all_to_all | solution.py:974
  101.9 2.8 %collective-permute-start.10 = (bf16[128,2048]{1,0:T(8,128)(2,1)}, bf16[128,2048]{1,0:T(8,128)(2,1)}, u32[]{:S(2)}, u32[]{:S(2)}) collective-permute-start(bf16[128,2048]{1,0:T(8,128)(2,1)} %collective-permute-done.7.refs_10_), channel_id=1, source_target_pairs={{0,2},{2,0},{4,6},{6,4},{8,10},{10,8},{12,14},{14,12},{16,18},{18,... | collective-permute-start | bytes 1572872 | tf_op jit(solution)/shard_map/c_ux/ppermute | solution.py:861
  102.2 16.4 %collective-permute-start.13 = (bf16[128,2560]{1,0:T(8,128)(2,1)}, bf16[128,2560]{1,0:T(8,128)(2,1)}, u32[]{:S(2)}, u32[]{:S(2)}) collective-permute-start(bf16[128,2560]{1,0:T(8,128)(2,1)} %get-tuple-element.125), channel_id=1, source_target_pairs={{0,1},{1,0},{2,3},{3,2},{4,5},{5,4},{6,7},{7,6},{8,9},{9,8},{10,11... | collective-permute-start | bytes 1966088 | tf_op jit(solution)/shard_map/y_v/ppermute | solution.py:853
  115.3 12.4 %collective-permute-start.11 = (bf16[208,1024]{1,0:T(8,128)(2,1)}, bf16[208,1024]{1,0:T(8,128)(2,1)}, u32[]{:S(2)}, u32[]{:S(2)}) collective-permute-start(bf16[208,1024]{1,0:T(8,128)(2,1)} %get-tuple-element.113), channel_id=1, source_target_pairs={{0,1},{1,0},{2,3},{3,2},{4,5},{5,4},{6,7},{7,6},{8,9},{9,8},{10,11... | collective-permute-start | bytes 1277960 | tf_op jit(solution)/shard_map/y_pack/ppermute | solution.py:853
  118.6 26.9 %collective-permute-start.14 = (bf16[128,2560]{1,0:T(8,128)(2,1)}, bf16[128,2560]{1,0:T(8,128)(2,1)}, u32[]{:S(2)}, u32[]{:S(2)}) collective-permute-start(bf16[128,2560]{1,0:T(8,128)(2,1)} %collective-permute-done.13.refs_11_), channel_id=1, source_target_pairs={{0,4},{2,6},{4,0},{6,2},{8,12},{10,14},{12,8},{14,10},{16,20},{18,... | collective-permute-start | bytes 1966088 | tf_op jit(solution)/shard_map/x_v/ppermute | solution.py:857
  127.7 9.9 %collective-permute-start.17 = (bf16[128,1536]{1,0:T(8,128)(2,1)}, bf16[128,1536]{1,0:T(8,128)(2,1)}, u32[]{:S(2)}, u32[]{:S(2)}) collective-permute-start(bf16[128,1536]{1,0:T(8,128)(2,1)} %get-tuple-element.132), channel_id=1, source_target_pairs={{0,1},{1,0},{2,3},{3,2},{4,5},{5,4},{6,7},{7,6},{8,9},{9,8},{10,11... | collective-permute-start | bytes 1179656 | tf_op jit(solution)/shard_map/y_w/ppermute | solution.py:853
  137.6 24.7 %all-to-all-start.3 = ((bf16[32,16,512]{2,1,0:T(8,128)(2,1)}), bf16[32,16,512]{2,1,0:T(8,128)(2,1)}, u32[]{:S(2)}, u32[]{:S(2)}) async-start(bf16[32,16,512]{2,1,0:T(8,128)(2,1)} %get-tuple-element.139), calls=%async_computation.3 | async-start | bytes 1048576 | tf_op jit(solution)/shard_map/all_to_all | solution.py:1087
  145.1 3.2 %collective-permute-start.15 = (bf16[128,2560]{1,0:T(8,128)(2,1)}, bf16[128,2560]{1,0:T(8,128)(2,1)}, u32[]{:S(2)}, u32[]{:S(2)}) collective-permute-start(bf16[128,2560]{1,0:T(8,128)(2,1)} %collective-permute-done.13.refs_11_), channel_id=1, source_target_pairs={{0,2},{2,0},{4,6},{6,4},{8,10},{10,8},{12,14},{14,12},{16,18},{18,... | collective-permute-start | bytes 1966088 | tf_op jit(solution)/shard_map/c_vy/ppermute | solution.py:861
  145.5 3.0 %collective-permute-start.16 = (bf16[128,2560]{1,0:T(8,128)(2,1)}, bf16[128,2560]{1,0:T(8,128)(2,1)}, u32[]{:S(2)}, u32[]{:S(2)}) collective-permute-start(bf16[128,2560]{1,0:T(8,128)(2,1)} %collective-permute-done.14.refs_12_), channel_id=1, source_target_pairs={{0,2},{2,0},{4,6},{6,4},{8,10},{10,8},{12,14},{14,12},{16,18},{18,... | collective-permute-start | bytes 1966088 | tf_op jit(solution)/shard_map/c_vx/ppermute | solution.py:861
  145.7 15.8 %collective-permute-start.18 = (bf16[128,1536]{1,0:T(8,128)(2,1)}, bf16[128,1536]{1,0:T(8,128)(2,1)}, u32[]{:S(2)}, u32[]{:S(2)}) collective-permute-start(bf16[128,1536]{1,0:T(8,128)(2,1)} %collective-permute-done.17.refs_9_), channel_id=1, source_target_pairs={{0,4},{2,6},{4,0},{6,2},{8,12},{10,14},{12,8},{14,10},{16,20},{18,... | collective-permute-start | bytes 1179656 | tf_op jit(solution)/shard_map/x_w/ppermute | solution.py:857
  147.1 11.6 %collective-permute-start.12 = (bf16[128,1024]{1,0:T(8,128)(2,1)}, bf16[128,1024]{1,0:T(8,128)(2,1)}, u32[]{:S(2)}, u32[]{:S(2)}) collective-permute-start(bf16[128,1024]{1,0:T(8,128)(2,1)} %get-tuple-element.118), channel_id=1, source_target_pairs={{0,1},{1,0},{2,3},{3,2},{4,5},{5,4},{6,7},{7,6},{8,9},{9,8},{10,11... | collective-permute-start | bytes 786440 | tf_op jit(solution)/shard_map/y_rest/ppermute | solution.py:853
  161.5 3.8 %collective-permute-start.19 = (bf16[128,1536]{1,0:T(8,128)(2,1)}, bf16[128,1536]{1,0:T(8,128)(2,1)}, u32[]{:S(2)}, u32[]{:S(2)}) collective-permute-start(bf16[128,1536]{1,0:T(8,128)(2,1)} %collective-permute-done.17.refs_9_), channel_id=1, source_target_pairs={{0,2},{2,0},{4,6},{6,4},{8,10},{10,8},{12,14},{14,12},{16,18},{18,... | collective-permute-start | bytes 1179656 | tf_op jit(solution)/shard_map/c_wy/ppermute | solution.py:861
  162.3 2.9 %collective-permute-start.20 = (bf16[128,1536]{1,0:T(8,128)(2,1)}, bf16[128,1536]{1,0:T(8,128)(2,1)}, u32[]{:S(2)}, u32[]{:S(2)}) collective-permute-start(bf16[128,1536]{1,0:T(8,128)(2,1)} %collective-permute-done.18.refs_10_), channel_id=1, source_target_pairs={{0,2},{2,0},{4,6},{6,4},{8,10},{10,8},{12,14},{14,12},{16,18},{18,... | collective-permute-start | bytes 1179656 | tf_op jit(solution)/shard_map/c_wx/ppermute | solution.py:861
  (1 other events, 2.3 us)

commit v4 on v3

--- a/solution.py
+++ b/solution.py
@@ -19,9 +19,9 @@
 CB = 512
 NB = COLS // CB
 WIDE = 512
-W_CUT = 1536
+W_CUT = 2048
 HALF = FF // 2 // CB
-TILE = 256
+QUERIES, KEYS = 512, 512
 
 A_QKV, A_OUT, A_UP, A_DOWN = 0, 1, 2, 3
 B_QKV, B_OUT, B_UP, B_DOWN = 7, 10, 11, 15
@@ -396,7 +396,6 @@
 def attention(stage, xt, dks, dvs, ks, vs, aq, s_scr, e_scr):
     order = stage.scalar.order
     rows = aq.shape[0]
-    count = rows // TILE
     blocks = order.shape[1]
     half = rows // blocks
     hd = HEAD_DIM
@@ -406,54 +405,53 @@
         start = pl.multiple_of(order[0, i] * half, half)
         for side in range(2):
             aq[pl.ds(start, half), cut(side, 2 * hd)] = x[i // per, side, cut(i % per, half), :]
-    for t in range(count):
-        part = aq[cut(t, TILE), :]
-        ks[cut(t, TILE), :] = part[:, hd : 2 * hd]
-        vs[cut(t, TILE), :] = part[:, 2 * hd : 3 * hd]
-        xt[:, cut(t, TILE)] = part.T
+    for t in range(rows // KEYS):
+        part = aq[cut(t, KEYS), :]
+        ks[cut(t, KEYS), :] = part[:, hd : 2 * hd]
+        vs[cut(t, KEYS), :] = part[:, 2 * hd : 3 * hd]
+        xt[:, cut(t, KEYS)] = part.T
     dks[...] = jnp.zeros_like(dks)
     dvs[...] = jnp.zeros_like(dvs)
-    key_row = lax.broadcasted_iota(jnp.int32, (TILE, TILE), 0)
-    query_col = lax.broadcasted_iota(jnp.int32, (TILE, TILE), 1)
-    seen = key_row <= query_col
-    for b in range(count):
-        at = cut(b, TILE)
+    later = lax.broadcasted_iota(jnp.int32, (KEYS, QUERIES), 0) - lax.broadcasted_iota(jnp.int32, (KEYS, QUERIES), 1)
+    for b in range(rows // QUERIES):
+        at = cut(b, QUERIES)
         q_t = xt[0:hd, at]
         g_t = xt[3 * hd : 4 * hd, at]
-        top = jnp.full((8, TILE), masked_value, f32)
-        for t in range(b + 1):
-            s = dot_nn(ks[cut(t, TILE), :], q_t)
-            if t == b:
-                s = jnp.where(seen, s, masked_value)
-            s_scr[cut(t, TILE), :] = s
-            top = jnp.maximum(top, jnp.max(s.reshape(TILE // 8, 8, TILE), axis=0))
+        tiles = [(cut(t, KEYS), b * QUERIES - t * KEYS) for t in range(-(-(b + 1) * QUERIES // KEYS))]
+        top = jnp.full((8, QUERIES), masked_value, f32)
+        for part, ahead in tiles:
+            s = dot_nn(ks[part, :], q_t)
+            if ahead < KEYS - 1:
+                s = jnp.where(later <= ahead, s, masked_value)
+            s_scr[part, :] = s
+            top = jnp.maximum(top, jnp.max(s.reshape(KEYS // 8, 8, QUERIES), axis=0))
         top = jnp.max(top, axis=0, keepdims=True)
-        total = jnp.zeros((8, TILE), f32)
-        att = jnp.zeros((hd, TILE), f32)
-        for t in range(b + 1):
-            e = jnp.exp(s_scr[cut(t, TILE), :] - top)
-            total = total + jnp.sum(e.reshape(TILE // 8, 8, TILE), axis=0)
+        total = jnp.zeros((8, QUERIES), f32)
+        att = jnp.zeros((hd, QUERIES), f32)
+        for part, _ in tiles:
+            e = jnp.exp(s_scr[part, :] - top)
+            total = total + jnp.sum(e.reshape(KEYS // 8, 8, QUERIES), axis=0)
             e = e.astype(bf16)
-            e_scr[cut(t, TILE), :] = e
-            att = att + dot_nn(xt[2 * hd : 3 * hd, cut(t, TILE)], e)
+            e_scr[part, :] = e
+            att = att + dot_nn(xt[2 * hd : 3 * hd, part], e)
         inverse = 1.0 / jnp.sum(total, axis=0, keepdims=True)
         att = att * inverse
         g_f = g_t.astype(f32)
         delta = jnp.sum(g_f * att, axis=0, keepdims=True) * inverse
         g_n = (g_f * inverse).astype(bf16)
-        dq = jnp.zeros((hd, TILE), f32)
-        for t in range(b + 1):
-            e = e_scr[cut(t, TILE), :]
-            dp = dot_nn(vs[cut(t, TILE), :], g_n)
+        dq = jnp.zeros((hd, QUERIES), f32)
+        for part, _ in tiles:
+            e = e_scr[part, :]
+            dp = dot_nn(vs[part, :], g_n)
             ds = (e.astype(f32) * (dp - delta)).astype(bf16)
-            dq = dq + dot_nn(xt[hd : 2 * hd, cut(t, TILE)], ds)
-            dks[cut(t, TILE), :] += dot_nt(ds, q_t)
-            dvs[cut(t, TILE), :] += dot_nt(e, g_n)
+            dq = dq + dot_nn(xt[hd : 2 * hd, part], ds)
+            dks[part, :] += dot_nt(ds, q_t)
+            dvs[part, :] += dot_nt(e, g_n)
         both = jnp.concatenate([att, dq * hd**-0.5], axis=0)
         aq[at, 0 : 2 * hd] = both.T.astype(bf16)
-    for t in range(count):
-        aq[cut(t, TILE), 2 * hd : 3 * hd] = dks[cut(t, TILE), :].astype(bf16)
-        aq[cut(t, TILE), 3 * hd :] = dvs[cut(t, TILE), :].astype(bf16)
+    for t in range(rows // KEYS):
+        aq[cut(t, KEYS), 2 * hd : 3 * hd] = dks[cut(t, KEYS), :].astype(bf16)
+        aq[cut(t, KEYS), 3 * hd :] = dvs[cut(t, KEYS), :].astype(bf16)
     for i in range(blocks):
         start = pl.multiple_of(order[0, i] * half, half)
         stage.out.back[cut(i, half), :] = aq[pl.ds(start, half), :]
@@ -475,8 +473,8 @@
             pltpu.VMEM((rows, hd), bf16),
             pltpu.VMEM((rows, hd), bf16),
             pltpu.VMEM((rows, 4 * hd), bf16),
-            pltpu.VMEM((rows, TILE), f32),
-            pltpu.VMEM((rows, TILE), bf16),
+            pltpu.VMEM((rows, QUERIES), f32),
+            pltpu.VMEM((rows, QUERIES), bf16),
         ],
         micros=17,
     ).back
@@ -993,9 +991,9 @@
 
     u_y = to_y(table.up, "u")
     early_given = to_y(up.early, "early")
-    u_x = to_x(tie(u_y, early_given, shared.products), "u")
+    u_x = to_x(tie(u_y, shared.products), "u")
     late_given = to_y(shared.late, "late")
-    arrived = tie(exchange(made.send), u_y)
+    arrived = tie(exchange(made.send), u_y, early_given)
     if parts == 1 and ndoc == 1:
         done = attention_one_document(block_order, arrived)
     else:
@@ -1037,7 +1035,7 @@
     )
     pack_given = to_y(middle.pack, "pack")
     v_x = to_x(tie(v_y, middle.pack), "v")
-    w_y = to_y(tie(shared.second, pack_given), "w")
+    w_y = to_y(tie(shared.second, v_y, middle.pack), "w")
     rest_given = to_y(tie(middle.rest, pack_given), "rest")
     tail = staged(
         adapter_gradients,

time: 172 us -> 167 us (0.971)
  Pallas kernels: 81.5 us -> 77.1 us
  starting transfers between devices: 48.3 us -> 46.4 us
    pallas_call x17, Pallas kernels: 81.5 us -> 77.1 us  [staged(): pl.pallas_call(kernel, out_shape=tuple(results.values()), in_specs=[HBM]...]
    all_to_all x2, waiting for transfers between devices: 1.25 us -> 5.11 us  [exchange(): return lax.all_to_all(a, 'ctx', 0, 0, tiled=True, axis_index_groups=near)]
    ppermute x12, waiting for transfers between devices: 34 us -> 31 us  [to_y(): return lax.ppermute(a, 'wsh', [(0, 1), (1, 0)])]
    ppermute x3, waiting for transfers between devices: 2.81 us -> 0.01 us  [to_x(): return lax.ppermute(a, 'ctx', [(i, i ^ 2) for i in range(n_ctx)])]
    ppermute x6, waiting for transfers between devices: 1.33 us -> 3.24 us  [to_core(): return lax.ppermute(a, 'ctx', [(i, i ^ 1) for i in range(n_ctx)])]
  transfers between devices with their start and end apart: 25 -> 25, of which waited for: 13 -> 15; matrix products, arithmetic and copies ran while one was open for 0% -> 0% of each run, Pallas kernels for 42% -> 41%
where the time goes in v4:
time: 167 us; the launch traced here: 166 us
  Pallas kernels  77.1 us (46%)
  starting transfers between devices  46.4 us (28%)
  waiting for transfers between devices  41 us (25%)
    pallas_call x17, Pallas kernels, staged(): pl.pallas_call(kernel, out_shape=tuple(results.values()), in_specs=[HBM]...  77.1 us
    ppermute x12, waiting for transfers between devices, to_y(): return lax.ppermute(a, 'wsh', [(0, 1), (1, 0)])  31 us
    all_to_all x2, starting transfers between devices, exchange(): return lax.all_to_all(a, 'ctx', 0, 0, tiled=True, axis_index_groups=near)  13.2 us
    ppermute x12, starting transfers between devices, to_y(): return lax.ppermute(a, 'wsh', [(0, 1), (1, 0)])  13.1 us
    all_to_all x1, starting transfers between devices, on_device(): low = lax.all_to_all(chosen_rows, 'ctx', 0, 0, tiled=True)  7.28 us
    all_to_all x1, starting transfers between devices, on_device(): shares = lax.all_to_all(tie(flat, w_y), ('ctx', 'wsh'), 0, 0, tiled=True)  6.99 us
    all_to_all x2, waiting for transfers between devices, exchange(): return lax.all_to_all(a, 'ctx', 0, 0, tiled=True, axis_index_groups=near)  5.11 us
    ppermute x3, starting transfers between devices, to_x(): return lax.ppermute(a, 'ctx', [(i, i ^ 2) for i in range(n_ctx)])  3.52 us
  transfers between devices with their start and end apart: 25, of which 15 were waited for; matrix products, arithmetic and copies ran while one was open for 0% of the time, Pallas kernels for 41%

profile of v4, /device:TPU:1, one launch (start us, length us, event | category | flops | bytes accessed | tf_op | source)
XLA Modules:
  0.0 166.1 jit_solution(15642334860259006556)
XLA Ops:
  10.3 7.3 %all-to-all-start = ((bf16[16,16,1024]{2,1,0:T(8,128)(2,1)}), bf16[16,16,1024]{2,1,0:T(8,128)(2,1)}, u32[]{:S(2)}, u32[]{:S(2)}) async-start(bf16[16,16,1024]{2,1,0:T(8,128)(2,1)} %choose_adapters.1), calls=%async_computation | async-start | bytes 1048576 | tf_op jit(solution)/shard_map/all_to_all | solution.py:884
  17.6 4.0 %partial_qk.1 = (bf16[128,2048]{1,0:T(8,128)(2,1)}, f32[4,128,512]{2,1,0:T(8,128)}) custom-call(bf16[128,1024]{1,0:T(8,128)(2,1)} %get-tuple-element.88.refs_0_.refs_4_, bf16[128,1024]{1,0:T(8,128)(2,1)} %collective-permute-done.refs_1_, bf16[512,3072]{1,0:T(8,128)(2,1)} %refs_8_.3), custom_call_target="tpu_custom_call" | custom-call | flops 3449999872 | bytes 1024 | tf_op jit(solution)/shard_map/partial_qk/pallas_call | solution.py:135
  23.4 3.5 %partial_vg.1 = (bf16[128,1536]{1,0:T(8,128)(2,1)}, f32[3,128,512]{2,1,0:T(8,128)}) custom-call(bf16[128,1024]{1,0:T(8,128)(2,1)} %get-tuple-element.88.refs_0_.refs_4_, bf16[128,1024]{1,0:T(8,128)(2,1)} %collective-permute-done.refs_1_, bf16[128,1024]{1,0:T(8,128)(2,1)} %bitcast.7, bf16[128,1024]{1,0:T(8,128)(2,1)} %collective-permute-done.2.refs_3_.refs_4_, ...), custom_call_target="tpu_custom_call" | custom-call | flops 3449999872 | bytes 1024 | tf_op jit(solution)/shard_map/partial_vg/pallas_call | solution.py:135
  27.6 6.1 %mlp_up.1 = (bf16[256,512]{1,0:T(8,128)(2,1)}, bf16[304,1536]{1,0:T(8,128)(2,1)}, f32[4,256,512]{2,1,0:T(8,128)}) custom-call(bf16[128,1024]{1,0:T(8,128)(2,1)} %get-tuple-element.86.refs_0_.refs_4_, bf16[128,1024]{1,0:T(8,128)(2,1)} %collective-permute-done.refs_1_, bf16[512,4096]{1,0:T(8,128)(2,1)} %refs_13_.1), custom_call_target="tpu_custom_call" | custom-call | flops 115000000 | bytes 1024 | tf_op jit(solution)/shard_map/mlp_up/pallas_call | solution.py:135
  33.7 2.7 %tables.1 = (f32[3,128,128]{2,1,0:T(8,128)}, f32[128,16]{1,0:T(8,128)}, f32[16,128]{1,0:T(8,128)}, bf16[128,2048]{1,0:T(8,128)(2,1)}) custom-call(s32[1,32]{1,0:T(1,128)} %refs_0_.7, s32[1,1]{1,0:T(1,128)S(6)} %copy.28.refs_1_, bf16[512,4096]{1,0:T(8,128)(2,1)} %refs_13_.1), custom_call_target="tpu_custom_call" | custom-call | flops 115000000 | bytes 1024 | tf_op jit(solution)/shard_map/tables/pallas_call | solution.py:135
  36.4 4.6 %queries_keys.1 = (bf16[128,16]{1,0:T(8,128)(2,1)}, bf16[128,16]{1,0:T(8,128)(2,1)}, bf16[16,2,128,128]{3,2,1,0:T(8,128)(2,1)}, f32[4,128,512]{2,1,0:T(8,128)}) custom-call(bf16[128,1024]{1,0:T(8,128)(2,1)} %get-tuple-element.88.refs_0_.refs_4_, bf16[128,1024]{1,0:T(8,128)(2,1)} %bitcast.8, bf16[16,16,1024]{2,1,0:T(8,128)(2,1)} %all-to-all-done.refs_2_.refs_5_.refs_6_, ...), custom_call_target="tpu_custom_call" | custom-call | flops 115000000 | bytes 1024 | tf_op jit(solution)/shard_map/queries_keys/pallas_call | solution.py:135
  41.0 3.2 %collective-permute-done.4.refs_1_ = bf16[128,1536]{1,0:T(8,128)(2,1)} collective-permute-done((bf16[128,1536]{1,0:T(8,128)(2,1)}, bf16[128,1536]{1,0:T(8,128)(2,1)}, u32[]{:S(2)}, u32[]{:S(2)}) %collective-permute-start.4) | collective-permute-done | bytes 393248 | tf_op jit(solution)/shard_map/y_vg/ppermute | solution.py:851
  46.7 6.4 %all-to-all-start.1 = ((bf16[16,2,128,128]{3,2,1,0:T(8,128)(2,1)}), bf16[16,2,128,128]{3,2,1,0:T(8,128)(2,1)}, u32[]{:S(2)}, u32[]{:S(2)}) async-start(bf16[16,2,128,128]{3,2,1,0:T(8,128)(2,1)} %values_grads.1), calls=%async_computation.1 | async-start | bytes 2097152 | tf_op jit(solution)/shard_map/all_to_all | solution.py:972
  54.7 2.8 %mlp_share.1 = (bf16[304,1536]{1,0:T(8,128)(2,1)}, bf16[16,256]{1,0:T(8,128)(2,1)}, bf16[128,3072]{1,0:T(8,128)(2,1)}, bf16[128,1024]{1,0:T(8,128)(2,1)}) custom-call(bf16[128,1024]{1,0:T(8,128)(2,1)} %get-tuple-element.86.refs_0_.refs_4_, bf16[128,1024]{1,0:T(8,128)(2,1)} %bitcast.9, ...), custom_call_target="tpu_custom_call", output_to_operand_aliasing={{0}: (4, {})} | custom-call | flops 2300000000 | bytes 1024 | tf_op jit(solution)/shard_map/mlp_share/pallas_call | solution.py:135
  57.6 9.3 %collective-permute-done.5.refs_9_ = bf16[128,2048]{1,0:T(8,128)(2,1)} collective-permute-done((bf16[128,2048]{1,0:T(8,128)(2,1)}, bf16[128,2048]{1,0:T(8,128)(2,1)}, u32[]{:S(2)}, u32[]{:S(2)}) %collective-permute-start.5) | collective-permute-done | bytes 524320 | tf_op jit(solution)/shard_map/y_u/ppermute | solution.py:851
  69.5 3.0 %collective-permute-done.6.refs_1_ = bf16[256,512]{1,0:T(8,128)(2,1)} collective-permute-done((bf16[256,512]{1,0:T(8,128)(2,1)}, bf16[256,512]{1,0:T(8,128)(2,1)}, u32[]{:S(2)}, u32[]{:S(2)}) %collective-permute-start.6) | collective-permute-done | bytes 262176 | tf_op jit(solution)/shard_map/y_early/ppermute | solution.py:851
  72.5 3.9 %all-to-all-done.1.refs_1_ = bf16[16,2,128,128]{3,2,1,0:T(8,128)(2,1)} async-done(((bf16[16,2,128,128]{3,2,1,0:T(8,128)(2,1)}), bf16[16,2,128,128]{3,2,1,0:T(8,128)(2,1)}, u32[]{:S(2)}, u32[]{:S(2)}) %all-to-all-start.1) | async-done | bytes 1048608 | tf_op jit(solution)/shard_map/all_to_all | solution.py:972
  76.4 12.4 %attention.1 = bf16[2048,256]{1,0:T(8,128)(2,1)} custom-call(s32[1,32]{1,0:T(1,128)} %refs_0_.7, bf16[16,2,128,128]{3,2,1,0:T(8,128)(2,1)} %all-to-all-done.1.refs_1_), custom_call_target="tpu_custom_call" | custom-call | flops 19549999104 | bytes 1024 | tf_op jit(solution)/shard_map/attention/pallas_call | solution.py:135
  88.8 3.5 %collective-permute-done.8.refs_2_ = bf16[304,1536]{1,0:T(8,128)(2,1)} collective-permute-done((bf16[304,1536]{1,0:T(8,128)(2,1)}, bf16[304,1536]{1,0:T(8,128)(2,1)}, u32[]{:S(2)}, u32[]{:S(2)}) %collective-permute-start.8) | collective-permute-done | bytes 933920 | tf_op jit(solution)/shard_map/y_late/ppermute | solution.py:851
  92.3 6.8 %all-to-all-start.2 = ((bf16[16,128,256]{2,1,0:T(8,128)(2,1)}), bf16[16,128,256]{2,1,0:T(8,128)(2,1)}, u32[]{:S(2)}, u32[]{:S(2)}) async-start(bf16[16,128,256]{2,1,0:T(8,128)(2,1)} %bitcast.17), calls=%async_computation.2 | async-start | bytes 2097152 | tf_op jit(solution)/shard_map/all_to_all | solution.py:972
  103.7 10.6 %mlp_middle.1 = (bf16[208,1024]{1,0:T(8,128)(2,1)}, f32[2,16,128]{2,1,0:T(8,128)}, bf16[8,16,512]{2,1,0:T(8,128)(2,1)}, f32[128,1024]{1,0:T(8,128)}, bf16[128,1024]{1,0:T(8,128)(2,1)}, /*index=5*/f32[128,1024]{1,0:T(8,128)}) custom-call(f32[4,256,512]{2,1,0:T(8,128)} %get-tuple-element.87.refs_0_, bf16[256,512]{1,0:T(8,128)(2,1)} %collective-permute-done.6.refs_1_, ...), custom_call_target="tpu_custom_call" | custom-call | flops 115000000 | bytes 1024 | tf_op jit(solution)/shard_map/mlp_middle/pallas_call | solution.py:135
  114.4 4.1 %collective-permute-done.13.refs_11_ = bf16[128,3072]{1,0:T(8,128)(2,1)} collective-permute-done((bf16[128,3072]{1,0:T(8,128)(2,1)}, bf16[128,3072]{1,0:T(8,128)(2,1)}, u32[]{:S(2)}, u32[]{:S(2)}) %collective-permute-start.13) | collective-permute-done | bytes 786464 | tf_op jit(solution)/shard_map/y_v/ppermute | solution.py:851
  122.4 4.4 %adapter_gradients.1 = (bf16[128,1024]{1,0:T(8,128)(2,1)}, bf16[128,3072]{1,0:T(8,128)(2,1)}, bf16[128,16]{1,0:T(8,128)(2,1)}, bf16[128,16]{1,0:T(8,128)(2,1)}, bf16[32,16,512]{2,1,0:T(8,128)(2,1)}) custom-call(bf16[16,128,256]{2,1,0:T(8,128)(2,1)} %all-to-all-done.2.refs_0_, f32[3,128,128]{2,1,0:T(8,128)} %get-tuple-element.91.refs_5_.refs_1_, ...), custom_call_target="tpu_custom_call" | custom-call | flops 115000000 | bytes 1024 | tf_op jit(solution)/shard_map/adapter_gradients/pallas_call | solution.py:135
  126.8 3.0 %collective-permute-done.11.refs_2_ = bf16[208,1024]{1,0:T(8,128)(2,1)} collective-permute-done((bf16[208,1024]{1,0:T(8,128)(2,1)}, bf16[208,1024]{1,0:T(8,128)(2,1)}, u32[]{:S(2)}, u32[]{:S(2)}) %collective-permute-start.11) | collective-permute-done | bytes 426016 | tf_op jit(solution)/shard_map/y_pack/ppermute | solution.py:851
  129.8 3.0 %mlp_finish.1 = (bf16[16,128]{1,0:T(8,128)(2,1)}, f32[128,1024]{1,0:T(8,128)}, bf16[32,16,512]{2,1,0:T(8,128)(2,1)}) custom-call(f32[2,16,128]{2,1,0:T(8,128)} %get-tuple-element.111.refs_0_, bf16[8,16,512]{2,1,0:T(8,128)(2,1)} %get-tuple-element.112.refs_1_, bf16[208,1024]{1,0:T(8,128)(2,1)} %collective-permute-done.11.refs_2_, ...), custom_call_target="tpu_custom_call", output_to_operand_aliasing={{2}: (8, {})} | custom-call | flops 115000000 | bytes 1024 | tf_op jit(solution)/shard_map/mlp_finish/pallas_call | solution.py:135
  135.4 7.0 %all-to-all-start.3 = ((bf16[32,16,512]{2,1,0:T(8,128)(2,1)}), bf16[32,16,512]{2,1,0:T(8,128)(2,1)}, u32[]{:S(2)}, u32[]{:S(2)}) async-start(bf16[32,16,512]{2,1,0:T(8,128)(2,1)} %get-tuple-element.139), calls=%async_computation.3 | async-start | bytes 1048576 | tf_op jit(solution)/shard_map/all_to_all | solution.py:1085
  146.2 7.1 %first_outputs.1 = (f32[128,1024]{1,0:T(8,128)}, f32[128,1024]{1,0:T(8,128)}) custom-call(bf16[128,1024]{1,0:T(8,128)(2,1)} %bitcast.15, bf16[128,1024]{1,0:T(8,128)(2,1)} %get-tuple-element.119.refs_1_, bf16[128,3072]{1,0:T(8,128)(2,1)} %get-tuple-element.107.refs_2_.refs_3_, bf16[128,16]{1,0:T(8,128)(2,1)} %get-tuple-element.120.refs_3_, ...), custom_call_target="tpu_custom_call" | custom-call | flops 115000000 | bytes 1024 | tf_op jit(solution)/shard_map/first_outputs/pallas_call | solution.py:135
  158.3 2.9 %adamw.1 = (f32[8,16,512]{2,1,0:T(8,128)}, f32[8,16,512]{2,1,0:T(8,128)}, f32[8,16,512]{2,1,0:T(8,128)}, f32[8,16,512]{2,1,0:T(8,128)}, bf16[8,16,512]{2,1,0:T(8,128)(2,1)}) custom-call(s32[1,1,8]{2,1,0:T(1,128)} %refs_0_.8, f32[8,16,512]{2,1,0:T(8,128)} %refs_1_.8, f32[8,16,512]{2,1,0:T(8,128)} %refs_2_.11, f32[8,16,512]{2,1,0:T(8,128)} %refs_3_.1, ...), custom_call_target="tpu_custom_call" | custom-call | flops 2300000000 | bytes 1024 | tf_op jit(solution)/shard_map/adamw/pallas_call | solution.py:135
  161.2 4.7 %last_outputs.1 = (bf16[128,1024]{1,0:T(8,128)(2,1)}, f32[128,1024]{1,0:T(8,128)}) custom-call(bf16[128,1024]{1,0:T(8,128)(2,1)} %bitcast.16, bf16[128,1024]{1,0:T(8,128)(2,1)} %bitcast.13, f32[2,1024]{1,0:T(2,128)} %refs_2_.10, bf16[128,3072]{1,0:T(8,128)(2,1)} %get-tuple-element.107.refs_2_.refs_3_, f32[128,1024]{1,0:T(8,128)} %get-tuple-element.116.refs_4_, ...), custom_call_target="tpu_custom_call" | custom-call | flops 115000000 | bytes 1024 | tf_op jit(solution)/shard_map/last_outputs/pallas_call | solution.py:135
  (43 shorter events, 38.1 us)
Async XLA Ops:
  2.3 6.0 %collective-permute-start.1 = (bf16[144,512]{1,0:T(8,128)(2,1)}, bf16[144,512]{1,0:T(8,128)(2,1)}, u32[]{:S(2)}, u32[]{:S(2)}) collective-permute-start(bf16[144,512]{1,0:T(8,128)(2,1)} %give_adapters.1), channel_id=1, source_target_pairs={{0,1},{1,0},{2,3},{3,2},{4,5},{5,4},{6,7},{7,6},{8,9},{9,8},{10,11... | collective-permute-start | bytes 442376 | tf_op jit(solution)/shard_map/y_adapters/ppermute | solution.py:851
  6.7 10.9 %collective-permute-start = (bf16[128,1024]{1,0:T(8,128)(2,1)}, bf16[128,1024]{1,0:T(8,128)(2,1)}, u32[]{:S(2)}, u32[]{:S(2)}) collective-permute-start(bf16[128,1024]{1,0:T(8,128)(2,1)} %get-tuple-element.79), channel_id=1, source_target_pairs={{0,1},{1,0},{2,3},{3,2},{4,5},{5,4},{6,7},{7,6},{8,9},{9,8},{10,11... | collective-permute-start | bytes 786440 | tf_op jit(solution)/shard_map/y_h/ppermute | solution.py:851
  6.8 16.6 %collective-permute-start.2 = (bf16[128,1024]{1,0:T(8,128)(2,1)}, bf16[128,1024]{1,0:T(8,128)(2,1)}, u32[]{:S(2)}, u32[]{:S(2)}) collective-permute-start(bf16[128,1024]{1,0:T(8,128)(2,1)} %bitcast.6), channel_id=1, source_target_pairs={{0,1},{1,0},{2,3},{3,2},{4,5},{5,4},{6,7},{7,6},{8,9},{9,8},{10,11... | collective-permute-start | bytes 786440 | tf_op jit(solution)/shard_map/y_grad/ppermute | solution.py:851
  10.3 26.1 %all-to-all-start = ((bf16[16,16,1024]{2,1,0:T(8,128)(2,1)}), bf16[16,16,1024]{2,1,0:T(8,128)(2,1)}, u32[]{:S(2)}, u32[]{:S(2)}) async-start(bf16[16,16,1024]{2,1,0:T(8,128)(2,1)} %choose_adapters.1), calls=%async_computation | async-start | bytes 1048576 | tf_op jit(solution)/shard_map/all_to_all | solution.py:884
  21.5 14.8 %collective-permute-start.3 = (bf16[128,2048]{1,0:T(8,128)(2,1)}, bf16[128,2048]{1,0:T(8,128)(2,1)}, u32[]{:S(2)}, u32[]{:S(2)}) collective-permute-start(bf16[128,2048]{1,0:T(8,128)(2,1)} %get-tuple-element.82), channel_id=1, source_target_pairs={{0,1},{1,0},{2,3},{3,2},{4,5},{5,4},{6,7},{7,6},{8,9},{9,8},{10,11... | collective-permute-start | bytes 1572872 | tf_op jit(solution)/shard_map/y_qk/ppermute | solution.py:851
  26.9 17.4 %collective-permute-start.4 = (bf16[128,1536]{1,0:T(8,128)(2,1)}, bf16[128,1536]{1,0:T(8,128)(2,1)}, u32[]{:S(2)}, u32[]{:S(2)}) collective-permute-start(bf16[128,1536]{1,0:T(8,128)(2,1)} %get-tuple-element.85), channel_id=1, source_target_pairs={{0,1},{1,0},{2,3},{3,2},{4,5},{5,4},{6,7},{7,6},{8,9},{9,8},{10,11... | collective-permute-start | bytes 1179656 | tf_op jit(solution)/shard_map/y_vg/ppermute | solution.py:851
  46.7 29.7 %all-to-all-start.1 = ((bf16[16,2,128,128]{3,2,1,0:T(8,128)(2,1)}), bf16[16,2,128,128]{3,2,1,0:T(8,128)(2,1)}, u32[]{:S(2)}, u32[]{:S(2)}) async-start(bf16[16,2,128,128]{3,2,1,0:T(8,128)(2,1)} %values_grads.1), calls=%async_computation.1 | async-start | bytes 2097152 | tf_op jit(solution)/shard_map/all_to_all | solution.py:972
  53.1 13.7 %collective-permute-start.5 = (bf16[128,2048]{1,0:T(8,128)(2,1)}, bf16[128,2048]{1,0:T(8,128)(2,1)}, u32[]{:S(2)}, u32[]{:S(2)}) collective-permute-start(bf16[128,2048]{1,0:T(8,128)(2,1)} %get-tuple-element.96), channel_id=1, source_target_pairs={{0,1},{1,0},{2,3},{3,2},{4,5},{5,4},{6,7},{7,6},{8,9},{9,8},{10,11... | collective-permute-start | bytes 1572872 | tf_op jit(solution)/shard_map/y_u/ppermute | solution.py:851
  54.6 17.8 %collective-permute-start.6 = (bf16[256,512]{1,0:T(8,128)(2,1)}, bf16[256,512]{1,0:T(8,128)(2,1)}, u32[]{:S(2)}, u32[]{:S(2)}) collective-permute-start(bf16[256,512]{1,0:T(8,128)(2,1)} %get-tuple-element.97), channel_id=1, source_target_pairs={{0,1},{1,0},{2,3},{3,2},{4,5},{5,4},{6,7},{7,6},{8,9},{9,8},{10,11... | collective-permute-start | bytes 786440 | tf_op jit(solution)/shard_map/y_early/ppermute | solution.py:851
  66.9 21.9 %collective-permute-start.7 = (bf16[128,2048]{1,0:T(8,128)(2,1)}, bf16[128,2048]{1,0:T(8,128)(2,1)}, u32[]{:S(2)}, u32[]{:S(2)}) collective-permute-start(bf16[128,2048]{1,0:T(8,128)(2,1)} %collective-permute-done.5.refs_9_), channel_id=1, source_target_pairs={{0,4},{2,6},{4,0},{6,2},{8,12},{10,14},{12,8},{14,10},{16,20},{18,... | collective-permute-start | bytes 1572872 | tf_op jit(solution)/shard_map/x_u/ppermute | solution.py:855
  68.0 24.3 %collective-permute-start.8 = (bf16[304,1536]{1,0:T(8,128)(2,1)}, bf16[304,1536]{1,0:T(8,128)(2,1)}, u32[]{:S(2)}, u32[]{:S(2)}) collective-permute-start(bf16[304,1536]{1,0:T(8,128)(2,1)} %get-tuple-element.103), channel_id=1, source_target_pairs={{0,1},{1,0},{2,3},{3,2},{4,5},{5,4},{6,7},{7,6},{8,9},{9,8},{10,11... | collective-permute-start | bytes 2801672 | tf_op jit(solution)/shard_map/y_late/ppermute | solution.py:851
  92.3 30.1 %all-to-all-start.2 = ((bf16[16,128,256]{2,1,0:T(8,128)(2,1)}), bf16[16,128,256]{2,1,0:T(8,128)(2,1)}, u32[]{:S(2)}, u32[]{:S(2)}) async-start(bf16[16,128,256]{2,1,0:T(8,128)(2,1)} %bitcast.17), calls=%async_computation.2 | async-start | bytes 2097152 | tf_op jit(solution)/shard_map/all_to_all | solution.py:972
  99.1 19.4 %collective-permute-start.13 = (bf16[128,3072]{1,0:T(8,128)(2,1)}, bf16[128,3072]{1,0:T(8,128)(2,1)}, u32[]{:S(2)}, u32[]{:S(2)}) collective-permute-start(bf16[128,3072]{1,0:T(8,128)(2,1)} %get-tuple-element.125), channel_id=1, source_target_pairs={{0,1},{1,0},{2,3},{3,2},{4,5},{5,4},{6,7},{7,6},{8,9},{9,8},{10,11... | collective-permute-start | bytes 2359304 | tf_op jit(solution)/shard_map/y_v/ppermute | solution.py:851
  101.1 2.6 %collective-permute-start.10 = (bf16[128,2048]{1,0:T(8,128)(2,1)}, bf16[128,2048]{1,0:T(8,128)(2,1)}, u32[]{:S(2)}, u32[]{:S(2)}) collective-permute-start(bf16[128,2048]{1,0:T(8,128)(2,1)} %collective-permute-done.7.refs_10_), channel_id=1, source_target_pairs={{0,2},{2,0},{4,6},{6,4},{8,10},{10,8},{12,14},{14,12},{16,18},{18,... | collective-permute-start | bytes 1572872 | tf_op jit(solution)/shard_map/c_ux/ppermute | solution.py:859
  118.5 24.3 %collective-permute-start.14 = (bf16[128,3072]{1,0:T(8,128)(2,1)}, bf16[128,3072]{1,0:T(8,128)(2,1)}, u32[]{:S(2)}, u32[]{:S(2)}) collective-permute-start(bf16[128,3072]{1,0:T(8,128)(2,1)} %collective-permute-done.13.refs_11_), channel_id=1, source_target_pairs={{0,4},{2,6},{4,0},{6,2},{8,12},{10,14},{12,8},{14,10},{16,20},{18,... | collective-permute-start | bytes 2359304 | tf_op jit(solution)/shard_map/x_v/ppermute | solution.py:855
  119.6 10.2 %collective-permute-start.11 = (bf16[208,1024]{1,0:T(8,128)(2,1)}, bf16[208,1024]{1,0:T(8,128)(2,1)}, u32[]{:S(2)}, u32[]{:S(2)}) collective-permute-start(bf16[208,1024]{1,0:T(8,128)(2,1)} %get-tuple-element.113), channel_id=1, source_target_pairs={{0,1},{1,0},{2,3},{3,2},{4,5},{5,4},{6,7},{7,6},{8,9},{9,8},{10,11... | collective-permute-start | bytes 1277960 | tf_op jit(solution)/shard_map/y_pack/ppermute | solution.py:851
  121.1 14.3 %collective-permute-start.17 = (bf16[128,1024]{1,0:T(8,128)(2,1)}, bf16[128,1024]{1,0:T(8,128)(2,1)}, u32[]{:S(2)}, u32[]{:S(2)}) collective-permute-start(bf16[128,1024]{1,0:T(8,128)(2,1)} %get-tuple-element.132), channel_id=1, source_target_pairs={{0,1},{1,0},{2,3},{3,2},{4,5},{5,4},{6,7},{7,6},{8,9},{9,8},{10,11... | collective-permute-start | bytes 786440 | tf_op jit(solution)/shard_map/y_w/ppermute | solution.py:851
  135.4 22.9 %all-to-all-start.3 = ((bf16[32,16,512]{2,1,0:T(8,128)(2,1)}), bf16[32,16,512]{2,1,0:T(8,128)(2,1)}, u32[]{:S(2)}, u32[]{:S(2)}) async-start(bf16[32,16,512]{2,1,0:T(8,128)(2,1)} %get-tuple-element.139), calls=%async_computation.3 | async-start | bytes 1048576 | tf_op jit(solution)/shard_map/all_to_all | solution.py:1085
  142.4 3.2 %collective-permute-start.15 = (bf16[128,3072]{1,0:T(8,128)(2,1)}, bf16[128,3072]{1,0:T(8,128)(2,1)}, u32[]{:S(2)}, u32[]{:S(2)}) collective-permute-start(bf16[128,3072]{1,0:T(8,128)(2,1)} %collective-permute-done.13.refs_11_), channel_id=1, source_target_pairs={{0,2},{2,0},{4,6},{6,4},{8,10},{10,8},{12,14},{14,12},{16,18},{18,... | collective-permute-start | bytes 2359304 | tf_op jit(solution)/shard_map/c_vy/ppermute | solution.py:859
  142.8 3.4 %collective-permute-start.16 = (bf16[128,3072]{1,0:T(8,128)(2,1)}, bf16[128,3072]{1,0:T(8,128)(2,1)}, u32[]{:S(2)}, u32[]{:S(2)}) collective-permute-start(bf16[128,3072]{1,0:T(8,128)(2,1)} %collective-permute-done.14.refs_12_), channel_id=1, source_target_pairs={{0,2},{2,0},{4,6},{6,4},{8,10},{10,8},{12,14},{14,12},{16,18},{18,... | collective-permute-start | bytes 2359304 | tf_op jit(solution)/shard_map/c_vx/ppermute | solution.py:859
  143.0 12.5 %collective-permute-start.12 = (bf16[128,1024]{1,0:T(8,128)(2,1)}, bf16[128,1024]{1,0:T(8,128)(2,1)}, u32[]{:S(2)}, u32[]{:S(2)}) collective-permute-start(bf16[128,1024]{1,0:T(8,128)(2,1)} %get-tuple-element.118), channel_id=1, source_target_pairs={{0,1},{1,0},{2,3},{3,2},{4,5},{5,4},{6,7},{7,6},{8,9},{9,8},{10,11... | collective-permute-start | bytes 786440 | tf_op jit(solution)/shard_map/y_rest/ppermute | solution.py:851
  144.4 11.1 %collective-permute-start.18 = (bf16[128,1024]{1,0:T(8,128)(2,1)}, bf16[128,1024]{1,0:T(8,128)(2,1)}, u32[]{:S(2)}, u32[]{:S(2)}) collective-permute-start(bf16[128,1024]{1,0:T(8,128)(2,1)} %collective-permute-done.17.refs_9_), channel_id=1, source_target_pairs={{0,4},{2,6},{4,0},{6,2},{8,12},{10,14},{12,8},{14,10},{16,20},{18,... | collective-permute-start | bytes 786440 | tf_op jit(solution)/shard_map/x_w/ppermute | solution.py:855
  155.5 5.7 %collective-permute-start.19 = (bf16[128,1024]{1,0:T(8,128)(2,1)}, bf16[128,1024]{1,0:T(8,128)(2,1)}, u32[]{:S(2)}, u32[]{:S(2)}) collective-permute-start(bf16[128,1024]{1,0:T(8,128)(2,1)} %collective-permute-done.17.refs_9_), channel_id=1, source_target_pairs={{0,2},{2,0},{4,6},{6,4},{8,10},{10,8},{12,14},{14,12},{16,18},{18,... | collective-permute-start | bytes 786440 | tf_op jit(solution)/shard_map/c_wy/ppermute | solution.py:859
  156.7 4.5 %collective-permute-start.20 = (bf16[128,1024]{1,0:T(8,128)(2,1)}, bf16[128,1024]{1,0:T(8,128)(2,1)}, u32[]{:S(2)}, u32[]{:S(2)}) collective-permute-start(bf16[128,1024]{1,0:T(8,128)(2,1)} %collective-permute-done.18.refs_10_), channel_id=1, source_target_pairs={{0,2},{2,0},{4,6},{6,4},{8,10},{10,8},{12,14},{14,12},{16,18},{18,... | collective-permute-start | bytes 786440 | tf_op jit(solution)/shard_map/c_wx/ppermute | solution.py:859
  (1 other events, 2.3 us)

commit v5 on v4

--- a/solution.py
+++ b/solution.py
@@ -560,13 +560,13 @@
         else:
             out.late[:, cut(j - HALF - 1, CB)] = part.astype(bf16)
             if j == 2 * HALF - 1:
-                stage.store(out.late, into=pl.ds(0, part.shape[0]))
+                stage.store(out.late)
     stage.store(out.kept)
 
 
-def share_at(kind, j, rank, rows):
+def share_at(kind, j, rank):
     down, right = divmod(kind * HALF + j, HALF - 1)
-    return pl.ds(rows + down * rank, rank), cut(right, CB)
+    return cut(down, rank), cut(right, CB)
 
 
 def mlp_share(stage, sems):
@@ -580,16 +580,16 @@
     ]
     for copy in copies:
         copy.start()
-    share, low, mask = out.late, stage.low, stage.mask_t[...]
+    share, low, mask = out.share, stage.low, stage.mask_t[...]
     rank, rows = mask.shape
     for j in range(HALF):
-        share[share_at(0, j, rank, 0)] = adapter_block(low, A_DOWN, HALF + j)
-        share[share_at(1, j, rank, 0)] = adapter_block(low, B_UP, HALF + j)
+        share[share_at(0, j, rank)] = adapter_block(low, A_DOWN, HALF + j)
+        share[share_at(1, j, rank)] = adapter_block(low, B_UP, HALF + j)
     inner = (dot_nt(low[A_UP], stage.h[...]) * mask).astype(bf16)
     back = (adapter_scale * dot_nt(low[B_DOWN], stage.grad[...]) * mask).astype(bf16)
     zero = jnp.zeros((rank, CB - 2 * rows), bf16)
-    share[share_at(2, 0, rank, 0)] = jnp.concatenate([inner, back, zero], axis=1)
-    stage.store(share, into=pl.ds(2 * rows, 3 * rank))
+    share[share_at(2, 0, rank)] = jnp.concatenate([inner, back, zero], axis=1)
+    stage.store(share)
     out.products[...] = jnp.concatenate([inner, back], axis=1)
     stage.store(out.products)
     for copy in copies:
@@ -614,17 +614,17 @@
     )
     grads = jnp.concatenate([stage.grad[...], stage.grad_given[...]], axis=0)
     rows = grads.shape[0] // 2
-    products, late = stage.products[...], stage.late
+    products, given = stage.products[...], stage.given
     rank = products.shape[0]
-    other = late[share_at(2, 0, rank, 2 * rows)]
+    other = given[share_at(2, 0, rank)]
     inner, back = (diagonal(products[:, cut(i, rows)], other[:, cut(i, rows)]) for i in range(2))
     sums = None
     grad_ups = []
     for j in range(HALF):
         at = cut(j, CB)
-        a_both = jnp.concatenate([adapter_block(low, A_DOWN, j), late[share_at(0, j, rank, 2 * rows)]], axis=0)
-        b_both = jnp.concatenate([adapter_block(low, B_UP, j), late[share_at(1, j, rank, 2 * rows)]], axis=0)
-        part = stage.early[...] if j == 0 else late[: 2 * rows, cut(j - 1, CB)]
+        a_both = jnp.concatenate([adapter_block(low, A_DOWN, j), given[share_at(0, j, rank)]], axis=0)
+        b_both = jnp.concatenate([adapter_block(low, B_UP, j), given[share_at(1, j, rank)]], axis=0)
+        part = stage.early[...] if j == 0 else stage.late[:, cut(j - 1, CB)]
         shift = pl.multiple_of(4 * D + hidden_block(j) * CB, CB)
         up = stage.kept[j] + swapped(part.astype(f32)) + stage.bias[:, pl.ds(shift, CB)]
         up = up + adapter_scale * dot_tn(inner, b_both)
@@ -923,11 +923,10 @@
         dict(h=tie(h_mlp, both.give), given=given),
         dict(
             early=shape((2 * tok_dev, CB)),
-            late=shape((2 * tok_dev + 3 * rank, (HALF - 1) * CB)),
+            late=shape((2 * tok_dev, (HALF - 1) * CB)),
             kept=shape((HALF, 2 * tok_dev, CB), f32),
         ),
         raws=dict(up=up_weight),
-        inside=dict(late=(2 * tok_dev, (HALF - 1) * CB)),
         scratch=[pltpu.VMEM((2 * HALF, D // 2, CB), bf16), pltpu.SemaphoreType.DMA((2 * HALF,))],
         micros=0.1,
     )
@@ -975,14 +974,12 @@
         mlp_share,
         dict(h=h_mlp, grad=grad, low=low, mask_t=mask_t),
         dict(
-            late=shape(up.late.shape),
+            share=shape((3 * rank, (HALF - 1) * CB)),
             products=shape((rank, 2 * tok_dev)),
             first=shape((D // 8, D + W_CUT)),
             second=shape((D // 8, 3 * D - W_CUT)),
         ),
-        raws=dict(late=up.late, qkv=qkv_weight, out=out_weight),
-        inside=dict(late=(3 * rank, (HALF - 1) * CB)),
-        alias=dict(late="late"),
+        raws=dict(qkv=qkv_weight, out=out_weight),
         scratch=[pltpu.SemaphoreType.DMA((3,))],
     )
 
@@ -992,8 +989,9 @@
     u_y = to_y(table.up, "u")
     early_given = to_y(up.early, "early")
     u_x = to_x(tie(u_y, shared.products), "u")
-    late_given = to_y(shared.late, "late")
-    arrived = tie(exchange(made.send), u_y, early_given)
+    late_given = to_y(up.late, "late")
+    share_given = to_y(shared.share, "share")
+    arrived = tie(exchange(tie(made.send, early_given)), u_y)
     if parts == 1 and ndoc == 1:
         done = attention_one_document(block_order, arrived)
     else:
@@ -1002,7 +1000,7 @@
         )
         far = None if parts == 1 else [[g * HEADS + i for g in range(parts)] for i in range(HEADS)]
         done = attention_documents(arrived, all_pos, all_doc, far, ctx // HEADS * HEADS * tok_dev)
-    back = exchange(tie(done.reshape(HEADS, tok_dev, 4 * HEAD_DIM), u_x, late_given))
+    back = exchange(tie(done.reshape(HEADS, tok_dev, 4 * HEAD_DIM), u_x, late_given, share_given))
     v_y = to_y(tie(shared.first, done), "v")
     middle = staged(
         mlp_middle,
@@ -1010,6 +1008,7 @@
             kept=up.kept,
             early=tie(early_given, done),
             late=late_given,
+            given=share_given,
             grad=grad,
             grad_given=grad_given,
             low=low,

time: 167 us -> 167 us (level)
  waiting for transfers between devices: 41 us -> 39.1 us
    ppermute x12 -> x13, waiting for transfers between devices: 31 us -> 26.2 us  [to_y(): return lax.ppermute(a, 'wsh', [(0, 1), (1, 0)])]
    all_to_all x2, waiting for transfers between devices: 5.11 us -> 8.09 us  [exchange(): return lax.all_to_all(a, 'ctx', 0, 0, tiled=True, axis_index_groups=near)]
    ppermute x12 -> x13, starting transfers between devices: 13.1 us -> 14.6 us  [to_y(): return lax.ppermute(a, 'wsh', [(0, 1), (1, 0)])]
  transfers between devices with their start and end apart: 25 -> 26, of which waited for: 15 -> 14; matrix products, arithmetic and copies ran while one was open for 0% -> 0% of each run, Pallas kernels for 41% -> 43%
where the time goes in v5:
time: 167 us; the launch traced here: 166 us
  Pallas kernels  77.1 us (46%)
  starting transfers between devices  47.8 us (29%)
  waiting for transfers between devices  39.1 us (23%)
  between operations  1.69 us (1%)
    pallas_call x17, Pallas kernels, staged(): pl.pallas_call(kernel, out_shape=tuple(results.values()), in_specs=[HBM]...  77.1 us
    ppermute x13, waiting for transfers between devices, to_y(): return lax.ppermute(a, 'wsh', [(0, 1), (1, 0)])  26.2 us
    ppermute x13, starting transfers between devices, to_y(): return lax.ppermute(a, 'wsh', [(0, 1), (1, 0)])  14.6 us
    all_to_all x2, starting transfers between devices, exchange(): return lax.all_to_all(a, 'ctx', 0, 0, tiled=True, axis_index_groups=near)  13.2 us
    all_to_all x2, waiting for transfers between devices, exchange(): return lax.all_to_all(a, 'ctx', 0, 0, tiled=True, axis_index_groups=near)  8.09 us
    all_to_all x1, starting transfers between devices, on_device(): low = lax.all_to_all(chosen_rows, 'ctx', 0, 0, tiled=True)  7.28 us
    all_to_all x1, starting transfers between devices, on_device(): shares = lax.all_to_all(tie(flat, w_y), ('ctx', 'wsh'), 0, 0, tiled=True)  6.96 us
    ppermute x3, starting transfers between devices, to_x(): return lax.ppermute(a, 'ctx', [(i, i ^ 2) for i in range(n_ctx)])  3.52 us
  transfers between devices with their start and end apart: 26, of which 14 were waited for; matrix products, arithmetic and copies ran while one was open for 0% of the time, Pallas kernels for 43%

profile of v5, /device:TPU:1, one launch (start us, length us, event | category | flops | bytes accessed | tf_op | source)
XLA Modules:
  0.0 165.7 jit_solution(12565396065158443680)
XLA Ops:
  10.3 7.3 %all-to-all-start = ((bf16[16,16,1024]{2,1,0:T(8,128)(2,1)}), bf16[16,16,1024]{2,1,0:T(8,128)(2,1)}, u32[]{:S(2)}, u32[]{:S(2)}) async-start(bf16[16,16,1024]{2,1,0:T(8,128)(2,1)} %choose_adapters.1), calls=%async_computation | async-start | bytes 1048576 | tf_op jit(solution)/shard_map/all_to_all | solution.py:884
  17.6 4.0 %partial_qk.1 = (bf16[128,2048]{1,0:T(8,128)(2,1)}, f32[4,128,512]{2,1,0:T(8,128)}) custom-call(bf16[128,1024]{1,0:T(8,128)(2,1)} %get-tuple-element.89.refs_0_.refs_4_, bf16[128,1024]{1,0:T(8,128)(2,1)} %collective-permute-done.refs_1_, bf16[512,3072]{1,0:T(8,128)(2,1)} %refs_8_.1), custom_call_target="tpu_custom_call" | custom-call | flops 3449999872 | bytes 1024 | tf_op jit(solution)/shard_map/partial_qk/pallas_call | solution.py:135
  23.4 3.4 %partial_vg.1 = (bf16[128,1536]{1,0:T(8,128)(2,1)}, f32[3,128,512]{2,1,0:T(8,128)}) custom-call(bf16[128,1024]{1,0:T(8,128)(2,1)} %get-tuple-element.89.refs_0_.refs_4_, bf16[128,1024]{1,0:T(8,128)(2,1)} %collective-permute-done.refs_1_, bf16[128,1024]{1,0:T(8,128)(2,1)} %bitcast.7, bf16[128,1024]{1,0:T(8,128)(2,1)} %collective-permute-done.2.refs_3_.refs_5_, ...), custom_call_target="tpu_custom_call" | custom-call | flops 3449999872 | bytes 1024 | tf_op jit(solution)/shard_map/partial_vg/pallas_call | solution.py:135
  27.5 6.1 %mlp_up.1 = (bf16[256,512]{1,0:T(8,128)(2,1)}, bf16[256,1536]{1,0:T(8,128)(2,1)}, f32[4,256,512]{2,1,0:T(8,128)}) custom-call(bf16[128,1024]{1,0:T(8,128)(2,1)} %get-tuple-element.87.refs_0_.refs_4_, bf16[128,1024]{1,0:T(8,128)(2,1)} %collective-permute-done.refs_1_, bf16[512,4096]{1,0:T(8,128)(2,1)} %refs_14_.1), custom_call_target="tpu_custom_call" | custom-call | flops 115000000 | bytes 1024 | tf_op jit(solution)/shard_map/mlp_up/pallas_call | solution.py:135
  35.1 2.7 %tables.1 = (f32[3,128,128]{2,1,0:T(8,128)}, f32[128,16]{1,0:T(8,128)}, f32[16,128]{1,0:T(8,128)}, bf16[128,2048]{1,0:T(8,128)(2,1)}) custom-call(s32[1,32]{1,0:T(1,128)} %refs_0_.7, s32[1,1]{1,0:T(1,128)S(6)} %copy.26.refs_1_, bf16[512,4096]{1,0:T(8,128)(2,1)} %refs_14_.1), custom_call_target="tpu_custom_call" | custom-call | flops 115000000 | bytes 1024 | tf_op jit(solution)/shard_map/tables/pallas_call | solution.py:135
  37.9 4.6 %queries_keys.1 = (bf16[128,16]{1,0:T(8,128)(2,1)}, bf16[128,16]{1,0:T(8,128)(2,1)}, bf16[16,2,128,128]{3,2,1,0:T(8,128)(2,1)}, f32[4,128,512]{2,1,0:T(8,128)}) custom-call(bf16[128,1024]{1,0:T(8,128)(2,1)} %get-tuple-element.89.refs_0_.refs_4_, bf16[128,1024]{1,0:T(8,128)(2,1)} %bitcast.8, bf16[16,16,1024]{2,1,0:T(8,128)(2,1)} %all-to-all-done.refs_2_.refs_6_.refs_5_, ...), custom_call_target="tpu_custom_call" | custom-call | flops 115000000 | bytes 1024 | tf_op jit(solution)/shard_map/queries_keys/pallas_call | solution.py:135
  44.3 2.4 %values_grads.1 = bf16[16,2,128,128]{3,2,1,0:T(8,128)(2,1)} custom-call(f32[4,128,512]{2,1,0:T(8,128)} %get-tuple-element.95.refs_0_, bf16[128,1536]{1,0:T(8,128)(2,1)} %collective-permute-done.4.refs_1_, bf16[16,2,128,128]{3,2,1,0:T(8,128)(2,1)} %get-tuple-element.96.refs_2_), custom_call_target="tpu_custom_call", output_to_operand_aliasing={{}: (2, {})} | custom-call | flops 3449999872 | bytes 1024 | tf_op jit(solution)/shard_map/values_grads/pallas_call | solution.py:135
  46.7 3.2 %collective-permute-done.5.refs_1_ = bf16[256,512]{1,0:T(8,128)(2,1)} collective-permute-done((bf16[256,512]{1,0:T(8,128)(2,1)}, bf16[256,512]{1,0:T(8,128)(2,1)}, u32[]{:S(2)}, u32[]{:S(2)}) %collective-permute-start.5) | collective-permute-done | bytes 262176 | tf_op jit(solution)/shard_map/y_early/ppermute | solution.py:851
  49.9 6.4 %all-to-all-start.1 = ((bf16[16,2,128,128]{3,2,1,0:T(8,128)(2,1)}), bf16[16,2,128,128]{3,2,1,0:T(8,128)(2,1)}, u32[]{:S(2)}, u32[]{:S(2)}) async-start(bf16[16,2,128,128]{3,2,1,0:T(8,128)(2,1)} %values_grads.1), calls=%async_computation.1 | async-start | bytes 2097152 | tf_op jit(solution)/shard_map/all_to_all | solution.py:971
  57.9 2.8 %mlp_share.1 = (bf16[48,1536]{1,0:T(8,128)(2,1)}, bf16[16,256]{1,0:T(8,128)(2,1)}, bf16[128,3072]{1,0:T(8,128)(2,1)}, bf16[128,1024]{1,0:T(8,128)(2,1)}) custom-call(bf16[128,1024]{1,0:T(8,128)(2,1)} %get-tuple-element.87.refs_0_.refs_4_, bf16[128,1024]{1,0:T(8,128)(2,1)} %bitcast.9, bf16[16,16,1024]{2,1,0:T(8,128)(2,1)} %all-to-all-done.refs_2_.refs_6_.refs_5_, ...), custom_call_target="tpu_custom_call" | custom-call | flops 2300000000 | bytes 1024 | tf_op jit(solution)/shard_map/mlp_share/pallas_call | solution.py:135
  60.7 9.3 %collective-permute-done.6.refs_10_ = bf16[128,2048]{1,0:T(8,128)(2,1)} collective-permute-done((bf16[128,2048]{1,0:T(8,128)(2,1)}, bf16[128,2048]{1,0:T(8,128)(2,1)}, u32[]{:S(2)}, u32[]{:S(2)}) %collective-permute-start.6) | collective-permute-done | bytes 524320 | tf_op jit(solution)/shard_map/y_u/ppermute | solution.py:851
  72.6 6.9 %all-to-all-done.1.refs_1_ = bf16[16,2,128,128]{3,2,1,0:T(8,128)(2,1)} async-done(((bf16[16,2,128,128]{3,2,1,0:T(8,128)(2,1)}), bf16[16,2,128,128]{3,2,1,0:T(8,128)(2,1)}, u32[]{:S(2)}, u32[]{:S(2)}) %all-to-all-start.1) | async-done | bytes 1048608 | tf_op jit(solution)/shard_map/all_to_all | solution.py:971
  79.5 12.4 %attention.1 = bf16[2048,256]{1,0:T(8,128)(2,1)} custom-call(s32[1,32]{1,0:T(1,128)} %refs_0_.7, bf16[16,2,128,128]{3,2,1,0:T(8,128)(2,1)} %all-to-all-done.1.refs_1_), custom_call_target="tpu_custom_call" | custom-call | flops 19549999104 | bytes 1024 | tf_op jit(solution)/shard_map/attention/pallas_call | solution.py:135
  91.9 6.8 %all-to-all-start.2 = ((bf16[16,128,256]{2,1,0:T(8,128)(2,1)}), bf16[16,128,256]{2,1,0:T(8,128)(2,1)}, u32[]{:S(2)}, u32[]{:S(2)}) async-start(bf16[16,128,256]{2,1,0:T(8,128)(2,1)} %bitcast.17), calls=%async_computation.2 | async-start | bytes 2097152 | tf_op jit(solution)/shard_map/all_to_all | solution.py:971
  103.3 10.7 %mlp_middle.1 = (bf16[208,1024]{1,0:T(8,128)(2,1)}, f32[2,16,128]{2,1,0:T(8,128)}, bf16[8,16,512]{2,1,0:T(8,128)(2,1)}, f32[128,1024]{1,0:T(8,128)}, bf16[128,1024]{1,0:T(8,128)(2,1)}, /*index=5*/f32[128,1024]{1,0:T(8,128)}) custom-call(f32[4,256,512]{2,1,0:T(8,128)} %get-tuple-element.88.refs_0_, bf16[256,512]{1,0:T(8,128)(2,1)} %collective-permute-done.5.refs_1_, ...), custom_call_target="tpu_custom_call" | custom-call | flops 115000000 | bytes 1024 | tf_op jit(solution)/shard_map/mlp_middle/pallas_call | solution.py:135
  114.1 4.0 %collective-permute-done.14.refs_11_ = bf16[128,3072]{1,0:T(8,128)(2,1)} collective-permute-done((bf16[128,3072]{1,0:T(8,128)(2,1)}, bf16[128,3072]{1,0:T(8,128)(2,1)}, u32[]{:S(2)}, u32[]{:S(2)}) %collective-permute-start.14) | collective-permute-done | bytes 786464 | tf_op jit(solution)/shard_map/y_v/ppermute | solution.py:851
  121.9 4.4 %adapter_gradients.1 = (bf16[128,1024]{1,0:T(8,128)(2,1)}, bf16[128,3072]{1,0:T(8,128)(2,1)}, bf16[128,16]{1,0:T(8,128)(2,1)}, bf16[128,16]{1,0:T(8,128)(2,1)}, bf16[32,16,512]{2,1,0:T(8,128)(2,1)}) custom-call(bf16[16,128,256]{2,1,0:T(8,128)(2,1)} %all-to-all-done.2.refs_0_, f32[3,128,128]{2,1,0:T(8,128)} %get-tuple-element.92.refs_5_.refs_1_, ...), custom_call_target="tpu_custom_call" | custom-call | flops 115000000 | bytes 1024 | tf_op jit(solution)/shard_map/adapter_gradients/pallas_call | solution.py:135
  126.3 3.1 %collective-permute-done.12.refs_2_ = bf16[208,1024]{1,0:T(8,128)(2,1)} collective-permute-done((bf16[208,1024]{1,0:T(8,128)(2,1)}, bf16[208,1024]{1,0:T(8,128)(2,1)}, u32[]{:S(2)}, u32[]{:S(2)}) %collective-permute-start.12) | collective-permute-done | bytes 426016 | tf_op jit(solution)/shard_map/y_pack/ppermute | solution.py:851
  129.4 3.0 %mlp_finish.1 = (bf16[16,128]{1,0:T(8,128)(2,1)}, f32[128,1024]{1,0:T(8,128)}, bf16[32,16,512]{2,1,0:T(8,128)(2,1)}) custom-call(f32[2,16,128]{2,1,0:T(8,128)} %get-tuple-element.113.refs_0_, bf16[8,16,512]{2,1,0:T(8,128)(2,1)} %get-tuple-element.114.refs_1_, bf16[208,1024]{1,0:T(8,128)(2,1)} %collective-permute-done.12.refs_2_, ...), custom_call_target="tpu_custom_call", output_to_operand_aliasing={{2}: (8, {})} | custom-call | flops 115000000 | bytes 1024 | tf_op jit(solution)/shard_map/mlp_finish/pallas_call | solution.py:135
  132.5 2.6 %collective-permute-done.18.refs_9_ = bf16[128,1024]{1,0:T(8,128)(2,1)} collective-permute-done((bf16[128,1024]{1,0:T(8,128)(2,1)}, bf16[128,1024]{1,0:T(8,128)(2,1)}, u32[]{:S(2)}, u32[]{:S(2)}) %collective-permute-start.18) | collective-permute-done | bytes 262176 | tf_op jit(solution)/shard_map/y_w/ppermute | solution.py:851
  135.1 7.0 %all-to-all-start.3 = ((bf16[32,16,512]{2,1,0:T(8,128)(2,1)}), bf16[32,16,512]{2,1,0:T(8,128)(2,1)}, u32[]{:S(2)}, u32[]{:S(2)}) async-start(bf16[32,16,512]{2,1,0:T(8,128)(2,1)} %get-tuple-element.141), calls=%async_computation.3 | async-start | bytes 1048576 | tf_op jit(solution)/shard_map/all_to_all | solution.py:1084
  145.9 7.1 %first_outputs.1 = (f32[128,1024]{1,0:T(8,128)}, f32[128,1024]{1,0:T(8,128)}) custom-call(bf16[128,1024]{1,0:T(8,128)(2,1)} %bitcast.15, bf16[128,1024]{1,0:T(8,128)(2,1)} %get-tuple-element.121.refs_1_, bf16[128,3072]{1,0:T(8,128)(2,1)} %get-tuple-element.109.refs_2_.refs_3_, bf16[128,16]{1,0:T(8,128)(2,1)} %get-tuple-element.122.refs_3_, ...), custom_call_target="tpu_custom_call" | custom-call | flops 115000000 | bytes 1024 | tf_op jit(solution)/shard_map/first_outputs/pallas_call | solution.py:135
  157.9 2.9 %adamw.1 = (f32[8,16,512]{2,1,0:T(8,128)}, f32[8,16,512]{2,1,0:T(8,128)}, f32[8,16,512]{2,1,0:T(8,128)}, f32[8,16,512]{2,1,0:T(8,128)}, bf16[8,16,512]{2,1,0:T(8,128)(2,1)}) custom-call(s32[1,1,8]{2,1,0:T(1,128)} %refs_0_.8, f32[8,16,512]{2,1,0:T(8,128)} %refs_1_.8, f32[8,16,512]{2,1,0:T(8,128)} %refs_2_.11, f32[8,16,512]{2,1,0:T(8,128)} %refs_3_.1, ...), custom_call_target="tpu_custom_call" | custom-call | flops 2300000000 | bytes 1024 | tf_op jit(solution)/shard_map/adamw/pallas_call | solution.py:135
  160.8 4.7 %last_outputs.1 = (bf16[128,1024]{1,0:T(8,128)(2,1)}, f32[128,1024]{1,0:T(8,128)}) custom-call(bf16[128,1024]{1,0:T(8,128)(2,1)} %bitcast.16, bf16[128,1024]{1,0:T(8,128)(2,1)} %bitcast.13, f32[2,1024]{1,0:T(2,128)} %refs_2_.10, bf16[128,3072]{1,0:T(8,128)(2,1)} %get-tuple-element.109.refs_2_.refs_3_, f32[128,1024]{1,0:T(8,128)} %get-tuple-element.118.refs_4_, ...), custom_call_target="tpu_custom_call" | custom-call | flops 115000000 | bytes 1024 | tf_op jit(solution)/shard_map/last_outputs/pallas_call | solution.py:135
  (45 shorter events, 36.3 us)
Async XLA Ops:
  2.3 6.0 %collective-permute-start.1 = (bf16[144,512]{1,0:T(8,128)(2,1)}, bf16[144,512]{1,0:T(8,128)(2,1)}, u32[]{:S(2)}, u32[]{:S(2)}) collective-permute-start(bf16[144,512]{1,0:T(8,128)(2,1)} %give_adapters.1), channel_id=1, source_target_pairs={{0,1},{1,0},{2,3},{3,2},{4,5},{5,4},{6,7},{7,6},{8,9},{9,8},{10,11... | collective-permute-start | bytes 442376 | tf_op jit(solution)/shard_map/y_adapters/ppermute | solution.py:851
  6.7 10.9 %collective-permute-start = (bf16[128,1024]{1,0:T(8,128)(2,1)}, bf16[128,1024]{1,0:T(8,128)(2,1)}, u32[]{:S(2)}, u32[]{:S(2)}) collective-permute-start(bf16[128,1024]{1,0:T(8,128)(2,1)} %get-tuple-element.80), channel_id=1, source_target_pairs={{0,1},{1,0},{2,3},{3,2},{4,5},{5,4},{6,7},{7,6},{8,9},{9,8},{10,11... | collective-permute-start | bytes 786440 | tf_op jit(solution)/shard_map/y_h/ppermute | solution.py:851
  6.8 16.6 %collective-permute-start.2 = (bf16[128,1024]{1,0:T(8,128)(2,1)}, bf16[128,1024]{1,0:T(8,128)(2,1)}, u32[]{:S(2)}, u32[]{:S(2)}) collective-permute-start(bf16[128,1024]{1,0:T(8,128)(2,1)} %bitcast.6), channel_id=1, source_target_pairs={{0,1},{1,0},{2,3},{3,2},{4,5},{5,4},{6,7},{7,6},{8,9},{9,8},{10,11... | collective-permute-start | bytes 786440 | tf_op jit(solution)/shard_map/y_grad/ppermute | solution.py:851
  10.3 27.6 %all-to-all-start = ((bf16[16,16,1024]{2,1,0:T(8,128)(2,1)}), bf16[16,16,1024]{2,1,0:T(8,128)(2,1)}, u32[]{:S(2)}, u32[]{:S(2)}) async-start(bf16[16,16,1024]{2,1,0:T(8,128)(2,1)} %choose_adapters.1), calls=%async_computation | async-start | bytes 1048576 | tf_op jit(solution)/shard_map/all_to_all | solution.py:884
  21.5 16.4 %collective-permute-start.3 = (bf16[128,2048]{1,0:T(8,128)(2,1)}, bf16[128,2048]{1,0:T(8,128)(2,1)}, u32[]{:S(2)}, u32[]{:S(2)}) collective-permute-start(bf16[128,2048]{1,0:T(8,128)(2,1)} %get-tuple-element.83), channel_id=1, source_target_pairs={{0,1},{1,0},{2,3},{3,2},{4,5},{5,4},{6,7},{7,6},{8,9},{9,8},{10,11... | collective-permute-start | bytes 1572872 | tf_op jit(solution)/shard_map/y_qk/ppermute | solution.py:851
  26.8 17.5 %collective-permute-start.4 = (bf16[128,1536]{1,0:T(8,128)(2,1)}, bf16[128,1536]{1,0:T(8,128)(2,1)}, u32[]{:S(2)}, u32[]{:S(2)}) collective-permute-start(bf16[128,1536]{1,0:T(8,128)(2,1)} %get-tuple-element.86), channel_id=1, source_target_pairs={{0,1},{1,0},{2,3},{3,2},{4,5},{5,4},{6,7},{7,6},{8,9},{9,8},{10,11... | collective-permute-start | bytes 1179656 | tf_op jit(solution)/shard_map/y_vg/ppermute | solution.py:851
  33.6 16.2 %collective-permute-start.5 = (bf16[256,512]{1,0:T(8,128)(2,1)}, bf16[256,512]{1,0:T(8,128)(2,1)}, u32[]{:S(2)}, u32[]{:S(2)}) collective-permute-start(bf16[256,512]{1,0:T(8,128)(2,1)} %get-tuple-element.97), channel_id=1, source_target_pairs={{0,1},{1,0},{2,3},{3,2},{4,5},{5,4},{6,7},{7,6},{8,9},{9,8},{10,11... | collective-permute-start | bytes 786440 | tf_op jit(solution)/shard_map/y_early/ppermute | solution.py:851
  49.9 29.6 %all-to-all-start.1 = ((bf16[16,2,128,128]{3,2,1,0:T(8,128)(2,1)}), bf16[16,2,128,128]{3,2,1,0:T(8,128)(2,1)}, u32[]{:S(2)}, u32[]{:S(2)}) async-start(bf16[16,2,128,128]{3,2,1,0:T(8,128)(2,1)} %values_grads.1), calls=%async_computation.1 | async-start | bytes 2097152 | tf_op jit(solution)/shard_map/all_to_all | solution.py:971
  56.3 13.7 %collective-permute-start.6 = (bf16[128,2048]{1,0:T(8,128)(2,1)}, bf16[128,2048]{1,0:T(8,128)(2,1)}, u32[]{:S(2)}, u32[]{:S(2)}) collective-permute-start(bf16[128,2048]{1,0:T(8,128)(2,1)} %get-tuple-element.99), channel_id=1, source_target_pairs={{0,1},{1,0},{2,3},{3,2},{4,5},{5,4},{6,7},{7,6},{8,9},{9,8},{10,11... | collective-permute-start | bytes 1572872 | tf_op jit(solution)/shard_map/y_u/ppermute | solution.py:851
  57.8 34.1 %collective-permute-start.8 = (bf16[256,1536]{1,0:T(8,128)(2,1)}, bf16[256,1536]{1,0:T(8,128)(2,1)}, u32[]{:S(2)}, u32[]{:S(2)}) collective-permute-start(bf16[256,1536]{1,0:T(8,128)(2,1)} %get-tuple-element.104), channel_id=1, source_target_pairs={{0,1},{1,0},{2,3},{3,2},{4,5},{5,4},{6,7},{7,6},{8,9},{9,8},{10,11... | collective-permute-start | bytes 2359304 | tf_op jit(solution)/shard_map/y_late/ppermute | solution.py:851
  70.0 21.9 %collective-permute-start.7 = (bf16[128,2048]{1,0:T(8,128)(2,1)}, bf16[128,2048]{1,0:T(8,128)(2,1)}, u32[]{:S(2)}, u32[]{:S(2)}) collective-permute-start(bf16[128,2048]{1,0:T(8,128)(2,1)} %collective-permute-done.6.refs_10_), channel_id=1, source_target_pairs={{0,4},{2,6},{4,0},{6,2},{8,12},{10,14},{12,8},{14,10},{16,20},{18,... | collective-permute-start | bytes 1572872 | tf_op jit(solution)/shard_map/x_u/ppermute | solution.py:855
  71.2 20.7 %collective-permute-start.9 = (bf16[48,1536]{1,0:T(8,128)(2,1)}, bf16[48,1536]{1,0:T(8,128)(2,1)}, u32[]{:S(2)}, u32[]{:S(2)}) collective-permute-start(bf16[48,1536]{1,0:T(8,128)(2,1)} %get-tuple-element.105), channel_id=1, source_target_pairs={{0,1},{1,0},{2,3},{3,2},{4,5},{5,4},{6,7},{7,6},{8,9},{9,8},{10,11... | collective-permute-start | bytes 442376 | tf_op jit(solution)/shard_map/y_share/ppermute | solution.py:851
  91.9 30.0 %all-to-all-start.2 = ((bf16[16,128,256]{2,1,0:T(8,128)(2,1)}), bf16[16,128,256]{2,1,0:T(8,128)(2,1)}, u32[]{:S(2)}, u32[]{:S(2)}) async-start(bf16[16,128,256]{2,1,0:T(8,128)(2,1)} %bitcast.17), calls=%async_computation.2 | async-start | bytes 2097152 | tf_op jit(solution)/shard_map/all_to_all | solution.py:971
  98.7 19.4 %collective-permute-start.14 = (bf16[128,3072]{1,0:T(8,128)(2,1)}, bf16[128,3072]{1,0:T(8,128)(2,1)}, u32[]{:S(2)}, u32[]{:S(2)}) collective-permute-start(bf16[128,3072]{1,0:T(8,128)(2,1)} %get-tuple-element.127), channel_id=1, source_target_pairs={{0,1},{1,0},{2,3},{3,2},{4,5},{5,4},{6,7},{7,6},{8,9},{9,8},{10,11... | collective-permute-start | bytes 2359304 | tf_op jit(solution)/shard_map/y_v/ppermute | solution.py:851
  118.1 23.9 %collective-permute-start.15 = (bf16[128,3072]{1,0:T(8,128)(2,1)}, bf16[128,3072]{1,0:T(8,128)(2,1)}, u32[]{:S(2)}, u32[]{:S(2)}) collective-permute-start(bf16[128,3072]{1,0:T(8,128)(2,1)} %collective-permute-done.14.refs_11_), channel_id=1, source_target_pairs={{0,4},{2,6},{4,0},{6,2},{8,12},{10,14},{12,8},{14,10},{16,20},{18,... | collective-permute-start | bytes 2359304 | tf_op jit(solution)/shard_map/x_v/ppermute | solution.py:855
  119.3 10.2 %collective-permute-start.12 = (bf16[208,1024]{1,0:T(8,128)(2,1)}, bf16[208,1024]{1,0:T(8,128)(2,1)}, u32[]{:S(2)}, u32[]{:S(2)}) collective-permute-start(bf16[208,1024]{1,0:T(8,128)(2,1)} %get-tuple-element.115), channel_id=1, source_target_pairs={{0,1},{1,0},{2,3},{3,2},{4,5},{5,4},{6,7},{7,6},{8,9},{9,8},{10,11... | collective-permute-start | bytes 1277960 | tf_op jit(solution)/shard_map/y_pack/ppermute | solution.py:851
  120.7 14.3 %collective-permute-start.18 = (bf16[128,1024]{1,0:T(8,128)(2,1)}, bf16[128,1024]{1,0:T(8,128)(2,1)}, u32[]{:S(2)}, u32[]{:S(2)}) collective-permute-start(bf16[128,1024]{1,0:T(8,128)(2,1)} %get-tuple-element.134), channel_id=1, source_target_pairs={{0,1},{1,0},{2,3},{3,2},{4,5},{5,4},{6,7},{7,6},{8,9},{9,8},{10,11... | collective-permute-start | bytes 786440 | tf_op jit(solution)/shard_map/y_w/ppermute | solution.py:851
  135.1 22.8 %all-to-all-start.3 = ((bf16[32,16,512]{2,1,0:T(8,128)(2,1)}), bf16[32,16,512]{2,1,0:T(8,128)(2,1)}, u32[]{:S(2)}, u32[]{:S(2)}) async-start(bf16[32,16,512]{2,1,0:T(8,128)(2,1)} %get-tuple-element.141), calls=%async_computation.3 | async-start | bytes 1048576 | tf_op jit(solution)/shard_map/all_to_all | solution.py:1084
  142.0 3.1 %collective-permute-start.17 = (bf16[128,3072]{1,0:T(8,128)(2,1)}, bf16[128,3072]{1,0:T(8,128)(2,1)}, u32[]{:S(2)}, u32[]{:S(2)}) collective-permute-start(bf16[128,3072]{1,0:T(8,128)(2,1)} %collective-permute-done.15.refs_12_), channel_id=1, source_target_pairs={{0,2},{2,0},{4,6},{6,4},{8,10},{10,8},{12,14},{14,12},{16,18},{18,... | collective-permute-start | bytes 2359304 | tf_op jit(solution)/shard_map/c_vx/ppermute | solution.py:859
  142.4 3.4 %collective-permute-start.16 = (bf16[128,3072]{1,0:T(8,128)(2,1)}, bf16[128,3072]{1,0:T(8,128)(2,1)}, u32[]{:S(2)}, u32[]{:S(2)}) collective-permute-start(bf16[128,3072]{1,0:T(8,128)(2,1)} %collective-permute-done.14.refs_11_), channel_id=1, source_target_pairs={{0,2},{2,0},{4,6},{6,4},{8,10},{10,8},{12,14},{14,12},{16,18},{18,... | collective-permute-start | bytes 2359304 | tf_op jit(solution)/shard_map/c_vy/ppermute | solution.py:859
  142.6 12.5 %collective-permute-start.13 = (bf16[128,1024]{1,0:T(8,128)(2,1)}, bf16[128,1024]{1,0:T(8,128)(2,1)}, u32[]{:S(2)}, u32[]{:S(2)}) collective-permute-start(bf16[128,1024]{1,0:T(8,128)(2,1)} %get-tuple-element.120), channel_id=1, source_target_pairs={{0,1},{1,0},{2,3},{3,2},{4,5},{5,4},{6,7},{7,6},{8,9},{9,8},{10,11... | collective-permute-start | bytes 786440 | tf_op jit(solution)/shard_map/y_rest/ppermute | solution.py:851
  144.0 11.1 %collective-permute-start.19 = (bf16[128,1024]{1,0:T(8,128)(2,1)}, bf16[128,1024]{1,0:T(8,128)(2,1)}, u32[]{:S(2)}, u32[]{:S(2)}) collective-permute-start(bf16[128,1024]{1,0:T(8,128)(2,1)} %collective-permute-done.18.refs_9_), channel_id=1, source_target_pairs={{0,4},{2,6},{4,0},{6,2},{8,12},{10,14},{12,8},{14,10},{16,20},{18,... | collective-permute-start | bytes 786440 | tf_op jit(solution)/shard_map/x_w/ppermute | solution.py:855
  155.1 5.7 %collective-permute-start.21 = (bf16[128,1024]{1,0:T(8,128)(2,1)}, bf16[128,1024]{1,0:T(8,128)(2,1)}, u32[]{:S(2)}, u32[]{:S(2)}) collective-permute-start(bf16[128,1024]{1,0:T(8,128)(2,1)} %collective-permute-done.19.refs_10_), channel_id=1, source_target_pairs={{0,2},{2,0},{4,6},{6,4},{8,10},{10,8},{12,14},{14,12},{16,18},{18,... | collective-permute-start | bytes 786440 | tf_op jit(solution)/shard_map/c_wx/ppermute | solution.py:859
  156.3 4.5 %collective-permute-start.20 = (bf16[128,1024]{1,0:T(8,128)(2,1)}, bf16[128,1024]{1,0:T(8,128)(2,1)}, u32[]{:S(2)}, u32[]{:S(2)}) collective-permute-start(bf16[128,1024]{1,0:T(8,128)(2,1)} %collective-permute-done.18.refs_9_), channel_id=1, source_target_pairs={{0,2},{2,0},{4,6},{6,4},{8,10},{10,8},{12,14},{14,12},{16,18},{18,... | collective-permute-start | bytes 786440 | tf_op jit(solution)/shard_map/c_wy/ppermute | solution.py:859
  (2 other events, 5.0 us)

commit v6 on v4

--- a/solution.py
+++ b/solution.py
@@ -323,10 +323,11 @@
     for n, copy in enumerate(copies):
         copy.wait()
         part = dot_nn(both, weights[n])
-        stage.out.give[:, cut(n, WIDE)] = part[rows:].astype(bf16)
+        at = (slice(None), cut(n, WIDE))
+        stage.out.give[at] = part[rows:].astype(bf16)
+        stage.store(stage.out.give, at=at, into=at, sem=n)
         stage.out.kept[n] = part[:rows]
-    stage.store(stage.out.give)
-    stage.store(stage.out.kept)
+        stage.store(stage.out.kept, n)
 
 
 def partial_vg(stage, weights, out_rows, sems):
@@ -338,15 +339,19 @@
     for n, copy in enumerate(copies):
         copy.wait()
         part = dot_nn(both, weights[n])
-        stage.out.give[:, cut(n, WIDE)] = part[rows:].astype(bf16)
+        at = (slice(None), cut(n, WIDE))
+        stage.out.give[at] = part[rows:].astype(bf16)
+        stage.store(stage.out.give, at=at, into=at, sem=n)
         stage.out.kept[n] = part[:rows]
+        stage.store(stage.out.kept, n)
     grads = jnp.concatenate([stage.grad[...], stage.grad_given[...]], axis=0)
     out_copy.wait()
     part = dot_nt(grads, out_rows[...])
-    stage.out.give[:, D:] = part[rows:].astype(bf16)
-    stage.store(stage.out.give)
+    at = (slice(None), slice(D, D + WIDE))
+    stage.out.give[at] = part[rows:].astype(bf16)
+    stage.store(stage.out.give, at=at, into=at, sem=D // WIDE)
     stage.out.kept[D // WIDE] = part[:rows]
-    stage.store(stage.out.kept)
+    stage.store(stage.out.kept, D // WIDE)
 
 
 def queries_keys(stage):
@@ -390,7 +395,8 @@
             head = n * WIDE // HEAD_DIM + 2 * pair
             for i, both in enumerate(swap_halves(value[:, cut(pair, 128)], grad[:, cut(pair, 128)])):
                 stage.out.send[head + i] = both.astype(bf16)
-    stage.store(stage.out.send, into=(slice(None), 1))
+        heads = pl.ds(n * WIDE // HEAD_DIM, WIDE // HEAD_DIM)
+        stage.store(stage.out.send, at=heads, into=(heads, 1), sem=n)
 
 
 def attention(stage, xt, dks, dvs, ks, vs, aq, s_scr, e_scr):
@@ -891,6 +897,7 @@
         dict(give=shape((tok_dev, 2 * D)), kept=shape((2 * D // WIDE, tok_dev, WIDE), f32)),
         raws=dict(qkv=qkv_weight),
         scratch=[pltpu.VMEM((2 * D // WIDE, D // 2, WIDE), bf16), pltpu.SemaphoreType.DMA((2 * D // WIDE,))],
+        parts=dict(give=2 * D // WIDE, kept=2 * D // WIDE),
         micros=3,
     )
     kept_qk, give_qk = both.kept, both.give
@@ -905,6 +912,7 @@
             pltpu.VMEM((D // 2, D), bf16),
             pltpu.SemaphoreType.DMA((D // WIDE + 1,)),
         ],
+        parts=dict(give=D // WIDE + 1, kept=D // WIDE + 1),
         micros=3,
     )
     given_vg = to_y(both.give, "vg")
@@ -963,6 +971,7 @@
         raws=dict(send=made.send),
         inside=dict(send=one),
         alias=dict(send="send"),
+        parts=dict(send=D // WIDE),
         micros=3,
     )
     parts = n_ctx // HEADS

time: 167 us -> 167 us (level)
  no operation moved by 1% of the time
where the time goes in v6:
time: 167 us; the launch traced here: 166 us
  Pallas kernels  76.4 us (46%)
  starting transfers between devices  46.4 us (28%)
  waiting for transfers between devices  41.2 us (25%)
    pallas_call x17, Pallas kernels, staged(): pl.pallas_call(kernel, out_shape=tuple(results.values()), in_specs=[HBM]...  76.4 us
    ppermute x12, waiting for transfers between devices, to_y(): return lax.ppermute(a, 'wsh', [(0, 1), (1, 0)])  31.3 us
    all_to_all x2, starting transfers between devices, exchange(): return lax.all_to_all(a, 'ctx', 0, 0, tiled=True, axis_index_groups=near)  13.2 us
    ppermute x12, starting transfers between devices, to_y(): return lax.ppermute(a, 'wsh', [(0, 1), (1, 0)])  13.1 us
    all_to_all x1, starting transfers between devices, on_device(): low = lax.all_to_all(chosen_rows, 'ctx', 0, 0, tiled=True)  7.28 us
    all_to_all x1, starting transfers between devices, on_device(): shares = lax.all_to_all(tie(flat, w_y), ('ctx', 'wsh'), 0, 0, tiled=True)  6.99 us
    all_to_all x2, waiting for transfers between devices, exchange(): return lax.all_to_all(a, 'ctx', 0, 0, tiled=True, axis_index_groups=near)  5.11 us
    ppermute x3, starting transfers between devices, to_x(): return lax.ppermute(a, 'ctx', [(i, i ^ 2) for i in range(n_ctx)])  3.52 us
  transfers between devices with their start and end apart: 25, of which 15 were waited for; matrix products, arithmetic and copies ran while one was open for 0% of the time, Pallas kernels for 41%

profile of v6, /device:TPU:1, one launch (start us, length us, event | category | flops | bytes accessed | tf_op | source)
XLA Modules:
  0.0 165.7 jit_solution(1028752452955406724)
XLA Ops:
  10.3 7.3 %all-to-all-start = ((bf16[16,16,1024]{2,1,0:T(8,128)(2,1)}), bf16[16,16,1024]{2,1,0:T(8,128)(2,1)}, u32[]{:S(2)}, u32[]{:S(2)}) async-start(bf16[16,16,1024]{2,1,0:T(8,128)(2,1)} %choose_adapters.1), calls=%async_computation | async-start | bytes 1048576 | tf_op jit(solution)/shard_map/all_to_all | solution.py:890
  17.6 3.6 %partial_qk.1 = (bf16[128,2048]{1,0:T(8,128)(2,1)}, f32[4,128,512]{2,1,0:T(8,128)}) custom-call(bf16[128,1024]{1,0:T(8,128)(2,1)} %get-tuple-element.88.refs_0_.refs_4_, bf16[128,1024]{1,0:T(8,128)(2,1)} %collective-permute-done.refs_1_, bf16[512,3072]{1,0:T(8,128)(2,1)} %refs_8_.3), custom_call_target="tpu_custom_call" | custom-call | flops 3449999872 | bytes 1024 | tf_op jit(solution)/shard_map/partial_qk/pallas_call | solution.py:135
  23.1 3.2 %partial_vg.1 = (bf16[128,1536]{1,0:T(8,128)(2,1)}, f32[3,128,512]{2,1,0:T(8,128)}) custom-call(bf16[128,1024]{1,0:T(8,128)(2,1)} %get-tuple-element.88.refs_0_.refs_4_, bf16[128,1024]{1,0:T(8,128)(2,1)} %collective-permute-done.refs_1_, bf16[128,1024]{1,0:T(8,128)(2,1)} %bitcast.7, bf16[128,1024]{1,0:T(8,128)(2,1)} %collective-permute-done.2.refs_3_.refs_4_, ...), custom_call_target="tpu_custom_call" | custom-call | flops 3449999872 | bytes 1024 | tf_op jit(solution)/shard_map/partial_vg/pallas_call | solution.py:135
  27.0 6.1 %mlp_up.1 = (bf16[256,512]{1,0:T(8,128)(2,1)}, bf16[304,1536]{1,0:T(8,128)(2,1)}, f32[4,256,512]{2,1,0:T(8,128)}) custom-call(bf16[128,1024]{1,0:T(8,128)(2,1)} %get-tuple-element.86.refs_0_.refs_4_, bf16[128,1024]{1,0:T(8,128)(2,1)} %collective-permute-done.refs_1_, bf16[512,4096]{1,0:T(8,128)(2,1)} %refs_13_.1), custom_call_target="tpu_custom_call" | custom-call | flops 115000000 | bytes 1024 | tf_op jit(solution)/shard_map/mlp_up/pallas_call | solution.py:135
  33.1 2.7 %tables.1 = (f32[3,128,128]{2,1,0:T(8,128)}, f32[128,16]{1,0:T(8,128)}, f32[16,128]{1,0:T(8,128)}, bf16[128,2048]{1,0:T(8,128)(2,1)}) custom-call(s32[1,32]{1,0:T(1,128)} %refs_0_.7, s32[1,1]{1,0:T(1,128)S(6)} %copy.28.refs_1_, bf16[512,4096]{1,0:T(8,128)(2,1)} %refs_13_.1), custom_call_target="tpu_custom_call" | custom-call | flops 115000000 | bytes 1024 | tf_op jit(solution)/shard_map/tables/pallas_call | solution.py:135
  35.8 4.6 %queries_keys.1 = (bf16[128,16]{1,0:T(8,128)(2,1)}, bf16[128,16]{1,0:T(8,128)(2,1)}, bf16[16,2,128,128]{3,2,1,0:T(8,128)(2,1)}, f32[4,128,512]{2,1,0:T(8,128)}) custom-call(bf16[128,1024]{1,0:T(8,128)(2,1)} %get-tuple-element.88.refs_0_.refs_4_, bf16[128,1024]{1,0:T(8,128)(2,1)} %bitcast.8, bf16[16,16,1024]{2,1,0:T(8,128)(2,1)} %all-to-all-done.refs_2_.refs_5_.refs_6_, ...), custom_call_target="tpu_custom_call" | custom-call | flops 115000000 | bytes 1024 | tf_op jit(solution)/shard_map/queries_keys/pallas_call | solution.py:135
  40.4 3.5 %collective-permute-done.4.refs_1_ = bf16[128,1536]{1,0:T(8,128)(2,1)} collective-permute-done((bf16[128,1536]{1,0:T(8,128)(2,1)}, bf16[128,1536]{1,0:T(8,128)(2,1)}, u32[]{:S(2)}, u32[]{:S(2)}) %collective-permute-start.4) | collective-permute-done | bytes 393248 | tf_op jit(solution)/shard_map/y_vg/ppermute | solution.py:857
  46.3 6.4 %all-to-all-start.1 = ((bf16[16,2,128,128]{3,2,1,0:T(8,128)(2,1)}), bf16[16,2,128,128]{3,2,1,0:T(8,128)(2,1)}, u32[]{:S(2)}, u32[]{:S(2)}) async-start(bf16[16,2,128,128]{3,2,1,0:T(8,128)(2,1)} %values_grads.1), calls=%async_computation.1 | async-start | bytes 2097152 | tf_op jit(solution)/shard_map/all_to_all | solution.py:981
  54.3 2.8 %mlp_share.1 = (bf16[304,1536]{1,0:T(8,128)(2,1)}, bf16[16,256]{1,0:T(8,128)(2,1)}, bf16[128,3072]{1,0:T(8,128)(2,1)}, bf16[128,1024]{1,0:T(8,128)(2,1)}) custom-call(bf16[128,1024]{1,0:T(8,128)(2,1)} %get-tuple-element.86.refs_0_.refs_4_, bf16[128,1024]{1,0:T(8,128)(2,1)} %bitcast.9, ...), custom_call_target="tpu_custom_call", output_to_operand_aliasing={{0}: (4, {})} | custom-call | flops 2300000000 | bytes 1024 | tf_op jit(solution)/shard_map/mlp_share/pallas_call | solution.py:135
  57.2 9.3 %collective-permute-done.5.refs_9_ = bf16[128,2048]{1,0:T(8,128)(2,1)} collective-permute-done((bf16[128,2048]{1,0:T(8,128)(2,1)}, bf16[128,2048]{1,0:T(8,128)(2,1)}, u32[]{:S(2)}, u32[]{:S(2)}) %collective-permute-start.5) | collective-permute-done | bytes 524320 | tf_op jit(solution)/shard_map/y_u/ppermute | solution.py:857
  69.1 3.0 %collective-permute-done.6.refs_1_ = bf16[256,512]{1,0:T(8,128)(2,1)} collective-permute-done((bf16[256,512]{1,0:T(8,128)(2,1)}, bf16[256,512]{1,0:T(8,128)(2,1)}, u32[]{:S(2)}, u32[]{:S(2)}) %collective-permute-start.6) | collective-permute-done | bytes 262176 | tf_op jit(solution)/shard_map/y_early/ppermute | solution.py:857
  72.1 3.9 %all-to-all-done.1.refs_1_ = bf16[16,2,128,128]{3,2,1,0:T(8,128)(2,1)} async-done(((bf16[16,2,128,128]{3,2,1,0:T(8,128)(2,1)}), bf16[16,2,128,128]{3,2,1,0:T(8,128)(2,1)}, u32[]{:S(2)}, u32[]{:S(2)}) %all-to-all-start.1) | async-done | bytes 1048608 | tf_op jit(solution)/shard_map/all_to_all | solution.py:981
  76.0 12.4 %attention.1 = bf16[2048,256]{1,0:T(8,128)(2,1)} custom-call(s32[1,32]{1,0:T(1,128)} %refs_0_.7, bf16[16,2,128,128]{3,2,1,0:T(8,128)(2,1)} %all-to-all-done.1.refs_1_), custom_call_target="tpu_custom_call" | custom-call | flops 19549999104 | bytes 1024 | tf_op jit(solution)/shard_map/attention/pallas_call | solution.py:135
  88.4 3.5 %collective-permute-done.8.refs_2_ = bf16[304,1536]{1,0:T(8,128)(2,1)} collective-permute-done((bf16[304,1536]{1,0:T(8,128)(2,1)}, bf16[304,1536]{1,0:T(8,128)(2,1)}, u32[]{:S(2)}, u32[]{:S(2)}) %collective-permute-start.8) | collective-permute-done | bytes 933920 | tf_op jit(solution)/shard_map/y_late/ppermute | solution.py:857
  91.9 6.8 %all-to-all-start.2 = ((bf16[16,128,256]{2,1,0:T(8,128)(2,1)}), bf16[16,128,256]{2,1,0:T(8,128)(2,1)}, u32[]{:S(2)}, u32[]{:S(2)}) async-start(bf16[16,128,256]{2,1,0:T(8,128)(2,1)} %bitcast.17), calls=%async_computation.2 | async-start | bytes 2097152 | tf_op jit(solution)/shard_map/all_to_all | solution.py:981
  103.3 10.6 %mlp_middle.1 = (bf16[208,1024]{1,0:T(8,128)(2,1)}, f32[2,16,128]{2,1,0:T(8,128)}, bf16[8,16,512]{2,1,0:T(8,128)(2,1)}, f32[128,1024]{1,0:T(8,128)}, bf16[128,1024]{1,0:T(8,128)(2,1)}, /*index=5*/f32[128,1024]{1,0:T(8,128)}) custom-call(f32[4,256,512]{2,1,0:T(8,128)} %get-tuple-element.87.refs_0_, bf16[256,512]{1,0:T(8,128)(2,1)} %collective-permute-done.6.refs_1_, ...), custom_call_target="tpu_custom_call" | custom-call | flops 115000000 | bytes 1024 | tf_op jit(solution)/shard_map/mlp_middle/pallas_call | solution.py:135
  114.0 4.1 %collective-permute-done.13.refs_11_ = bf16[128,3072]{1,0:T(8,128)(2,1)} collective-permute-done((bf16[128,3072]{1,0:T(8,128)(2,1)}, bf16[128,3072]{1,0:T(8,128)(2,1)}, u32[]{:S(2)}, u32[]{:S(2)}) %collective-permute-start.13) | collective-permute-done | bytes 786464 | tf_op jit(solution)/shard_map/y_v/ppermute | solution.py:857
  122.0 4.4 %adapter_gradients.1 = (bf16[128,1024]{1,0:T(8,128)(2,1)}, bf16[128,3072]{1,0:T(8,128)(2,1)}, bf16[128,16]{1,0:T(8,128)(2,1)}, bf16[128,16]{1,0:T(8,128)(2,1)}, bf16[32,16,512]{2,1,0:T(8,128)(2,1)}) custom-call(bf16[16,128,256]{2,1,0:T(8,128)(2,1)} %all-to-all-done.2.refs_0_, f32[3,128,128]{2,1,0:T(8,128)} %get-tuple-element.91.refs_5_.refs_1_, ...), custom_call_target="tpu_custom_call" | custom-call | flops 115000000 | bytes 1024 | tf_op jit(solution)/shard_map/adapter_gradients/pallas_call | solution.py:135
  126.4 3.0 %collective-permute-done.11.refs_2_ = bf16[208,1024]{1,0:T(8,128)(2,1)} collective-permute-done((bf16[208,1024]{1,0:T(8,128)(2,1)}, bf16[208,1024]{1,0:T(8,128)(2,1)}, u32[]{:S(2)}, u32[]{:S(2)}) %collective-permute-start.11) | collective-permute-done | bytes 426016 | tf_op jit(solution)/shard_map/y_pack/ppermute | solution.py:857
  129.4 3.0 %mlp_finish.1 = (bf16[16,128]{1,0:T(8,128)(2,1)}, f32[128,1024]{1,0:T(8,128)}, bf16[32,16,512]{2,1,0:T(8,128)(2,1)}) custom-call(f32[2,16,128]{2,1,0:T(8,128)} %get-tuple-element.111.refs_0_, bf16[8,16,512]{2,1,0:T(8,128)(2,1)} %get-tuple-element.112.refs_1_, bf16[208,1024]{1,0:T(8,128)(2,1)} %collective-permute-done.11.refs_2_, ...), custom_call_target="tpu_custom_call", output_to_operand_aliasing={{2}: (8, {})} | custom-call | flops 115000000 | bytes 1024 | tf_op jit(solution)/shard_map/mlp_finish/pallas_call | solution.py:135
  135.0 7.0 %all-to-all-start.3 = ((bf16[32,16,512]{2,1,0:T(8,128)(2,1)}), bf16[32,16,512]{2,1,0:T(8,128)(2,1)}, u32[]{:S(2)}, u32[]{:S(2)}) async-start(bf16[32,16,512]{2,1,0:T(8,128)(2,1)} %get-tuple-element.139), calls=%async_computation.3 | async-start | bytes 1048576 | tf_op jit(solution)/shard_map/all_to_all | solution.py:1094
  145.8 7.1 %first_outputs.1 = (f32[128,1024]{1,0:T(8,128)}, f32[128,1024]{1,0:T(8,128)}) custom-call(bf16[128,1024]{1,0:T(8,128)(2,1)} %bitcast.15, bf16[128,1024]{1,0:T(8,128)(2,1)} %get-tuple-element.119.refs_1_, bf16[128,3072]{1,0:T(8,128)(2,1)} %get-tuple-element.107.refs_2_.refs_3_, bf16[128,16]{1,0:T(8,128)(2,1)} %get-tuple-element.120.refs_3_, ...), custom_call_target="tpu_custom_call" | custom-call | flops 115000000 | bytes 1024 | tf_op jit(solution)/shard_map/first_outputs/pallas_call | solution.py:135
  157.9 2.9 %adamw.1 = (f32[8,16,512]{2,1,0:T(8,128)}, f32[8,16,512]{2,1,0:T(8,128)}, f32[8,16,512]{2,1,0:T(8,128)}, f32[8,16,512]{2,1,0:T(8,128)}, bf16[8,16,512]{2,1,0:T(8,128)(2,1)}) custom-call(s32[1,1,8]{2,1,0:T(1,128)} %refs_0_.8, f32[8,16,512]{2,1,0:T(8,128)} %refs_1_.8, f32[8,16,512]{2,1,0:T(8,128)} %refs_2_.11, f32[8,16,512]{2,1,0:T(8,128)} %refs_3_.1, ...), custom_call_target="tpu_custom_call" | custom-call | flops 2300000000 | bytes 1024 | tf_op jit(solution)/shard_map/adamw/pallas_call | solution.py:135
  160.8 4.7 %last_outputs.1 = (bf16[128,1024]{1,0:T(8,128)(2,1)}, f32[128,1024]{1,0:T(8,128)}) custom-call(bf16[128,1024]{1,0:T(8,128)(2,1)} %bitcast.16, bf16[128,1024]{1,0:T(8,128)(2,1)} %bitcast.13, f32[2,1024]{1,0:T(2,128)} %refs_2_.10, bf16[128,3072]{1,0:T(8,128)(2,1)} %get-tuple-element.107.refs_2_.refs_3_, f32[128,1024]{1,0:T(8,128)} %get-tuple-element.116.refs_4_, ...), custom_call_target="tpu_custom_call" | custom-call | flops 115000000 | bytes 1024 | tf_op jit(solution)/shard_map/last_outputs/pallas_call | solution.py:135
  (43 shorter events, 38.0 us)
Async XLA Ops:
  2.3 6.0 %collective-permute-start.1 = (bf16[144,512]{1,0:T(8,128)(2,1)}, bf16[144,512]{1,0:T(8,128)(2,1)}, u32[]{:S(2)}, u32[]{:S(2)}) collective-permute-start(bf16[144,512]{1,0:T(8,128)(2,1)} %give_adapters.1), channel_id=1, source_target_pairs={{0,1},{1,0},{2,3},{3,2},{4,5},{5,4},{6,7},{7,6},{8,9},{9,8},{10,11... | collective-permute-start | bytes 442376 | tf_op jit(solution)/shard_map/y_adapters/ppermute | solution.py:857
  6.7 10.9 %collective-permute-start = (bf16[128,1024]{1,0:T(8,128)(2,1)}, bf16[128,1024]{1,0:T(8,128)(2,1)}, u32[]{:S(2)}, u32[]{:S(2)}) collective-permute-start(bf16[128,1024]{1,0:T(8,128)(2,1)} %get-tuple-element.79), channel_id=1, source_target_pairs={{0,1},{1,0},{2,3},{3,2},{4,5},{5,4},{6,7},{7,6},{8,9},{9,8},{10,11... | collective-permute-start | bytes 786440 | tf_op jit(solution)/shard_map/y_h/ppermute | solution.py:857
  6.8 16.3 %collective-permute-start.2 = (bf16[128,1024]{1,0:T(8,128)(2,1)}, bf16[128,1024]{1,0:T(8,128)(2,1)}, u32[]{:S(2)}, u32[]{:S(2)}) collective-permute-start(bf16[128,1024]{1,0:T(8,128)(2,1)} %bitcast.6), channel_id=1, source_target_pairs={{0,1},{1,0},{2,3},{3,2},{4,5},{5,4},{6,7},{7,6},{8,9},{9,8},{10,11... | collective-permute-start | bytes 786440 | tf_op jit(solution)/shard_map/y_grad/ppermute | solution.py:857
  10.3 25.5 %all-to-all-start = ((bf16[16,16,1024]{2,1,0:T(8,128)(2,1)}), bf16[16,16,1024]{2,1,0:T(8,128)(2,1)}, u32[]{:S(2)}, u32[]{:S(2)}) async-start(bf16[16,16,1024]{2,1,0:T(8,128)(2,1)} %choose_adapters.1), calls=%async_computation | async-start | bytes 1048576 | tf_op jit(solution)/shard_map/all_to_all | solution.py:890
  21.2 14.6 %collective-permute-start.3 = (bf16[128,2048]{1,0:T(8,128)(2,1)}, bf16[128,2048]{1,0:T(8,128)(2,1)}, u32[]{:S(2)}, u32[]{:S(2)}) collective-permute-start(bf16[128,2048]{1,0:T(8,128)(2,1)} %get-tuple-element.82), channel_id=1, source_target_pairs={{0,1},{1,0},{2,3},{3,2},{4,5},{5,4},{6,7},{7,6},{8,9},{9,8},{10,11... | collective-permute-start | bytes 1572872 | tf_op jit(solution)/shard_map/y_qk/ppermute | solution.py:857
  26.3 17.7 %collective-permute-start.4 = (bf16[128,1536]{1,0:T(8,128)(2,1)}, bf16[128,1536]{1,0:T(8,128)(2,1)}, u32[]{:S(2)}, u32[]{:S(2)}) collective-permute-start(bf16[128,1536]{1,0:T(8,128)(2,1)} %get-tuple-element.85), channel_id=1, source_target_pairs={{0,1},{1,0},{2,3},{3,2},{4,5},{5,4},{6,7},{7,6},{8,9},{9,8},{10,11... | collective-permute-start | bytes 1179656 | tf_op jit(solution)/shard_map/y_vg/ppermute | solution.py:857
  46.3 29.7 %all-to-all-start.1 = ((bf16[16,2,128,128]{3,2,1,0:T(8,128)(2,1)}), bf16[16,2,128,128]{3,2,1,0:T(8,128)(2,1)}, u32[]{:S(2)}, u32[]{:S(2)}) async-start(bf16[16,2,128,128]{3,2,1,0:T(8,128)(2,1)} %values_grads.1), calls=%async_computation.1 | async-start | bytes 2097152 | tf_op jit(solution)/shard_map/all_to_all | solution.py:981
  52.7 13.7 %collective-permute-start.5 = (bf16[128,2048]{1,0:T(8,128)(2,1)}, bf16[128,2048]{1,0:T(8,128)(2,1)}, u32[]{:S(2)}, u32[]{:S(2)}) collective-permute-start(bf16[128,2048]{1,0:T(8,128)(2,1)} %get-tuple-element.96), channel_id=1, source_target_pairs={{0,1},{1,0},{2,3},{3,2},{4,5},{5,4},{6,7},{7,6},{8,9},{9,8},{10,11... | collective-permute-start | bytes 1572872 | tf_op jit(solution)/shard_map/y_u/ppermute | solution.py:857
  54.2 17.8 %collective-permute-start.6 = (bf16[256,512]{1,0:T(8,128)(2,1)}, bf16[256,512]{1,0:T(8,128)(2,1)}, u32[]{:S(2)}, u32[]{:S(2)}) collective-permute-start(bf16[256,512]{1,0:T(8,128)(2,1)} %get-tuple-element.97), channel_id=1, source_target_pairs={{0,1},{1,0},{2,3},{3,2},{4,5},{5,4},{6,7},{7,6},{8,9},{9,8},{10,11... | collective-permute-start | bytes 786440 | tf_op jit(solution)/shard_map/y_early/ppermute | solution.py:857
  66.5 21.9 %collective-permute-start.7 = (bf16[128,2048]{1,0:T(8,128)(2,1)}, bf16[128,2048]{1,0:T(8,128)(2,1)}, u32[]{:S(2)}, u32[]{:S(2)}) collective-permute-start(bf16[128,2048]{1,0:T(8,128)(2,1)} %collective-permute-done.5.refs_9_), channel_id=1, source_target_pairs={{0,4},{2,6},{4,0},{6,2},{8,12},{10,14},{12,8},{14,10},{16,20},{18,... | collective-permute-start | bytes 1572872 | tf_op jit(solution)/shard_map/x_u/ppermute | solution.py:861
  67.6 24.3 %collective-permute-start.8 = (bf16[304,1536]{1,0:T(8,128)(2,1)}, bf16[304,1536]{1,0:T(8,128)(2,1)}, u32[]{:S(2)}, u32[]{:S(2)}) collective-permute-start(bf16[304,1536]{1,0:T(8,128)(2,1)} %get-tuple-element.103), channel_id=1, source_target_pairs={{0,1},{1,0},{2,3},{3,2},{4,5},{5,4},{6,7},{7,6},{8,9},{9,8},{10,11... | collective-permute-start | bytes 2801672 | tf_op jit(solution)/shard_map/y_late/ppermute | solution.py:857
  91.9 30.1 %all-to-all-start.2 = ((bf16[16,128,256]{2,1,0:T(8,128)(2,1)}), bf16[16,128,256]{2,1,0:T(8,128)(2,1)}, u32[]{:S(2)}, u32[]{:S(2)}) async-start(bf16[16,128,256]{2,1,0:T(8,128)(2,1)} %bitcast.17), calls=%async_computation.2 | async-start | bytes 2097152 | tf_op jit(solution)/shard_map/all_to_all | solution.py:981
  98.7 19.4 %collective-permute-start.13 = (bf16[128,3072]{1,0:T(8,128)(2,1)}, bf16[128,3072]{1,0:T(8,128)(2,1)}, u32[]{:S(2)}, u32[]{:S(2)}) collective-permute-start(bf16[128,3072]{1,0:T(8,128)(2,1)} %get-tuple-element.125), channel_id=1, source_target_pairs={{0,1},{1,0},{2,3},{3,2},{4,5},{5,4},{6,7},{7,6},{8,9},{9,8},{10,11... | collective-permute-start | bytes 2359304 | tf_op jit(solution)/shard_map/y_v/ppermute | solution.py:857
  100.7 2.6 %collective-permute-start.10 = (bf16[128,2048]{1,0:T(8,128)(2,1)}, bf16[128,2048]{1,0:T(8,128)(2,1)}, u32[]{:S(2)}, u32[]{:S(2)}) collective-permute-start(bf16[128,2048]{1,0:T(8,128)(2,1)} %collective-permute-done.7.refs_10_), channel_id=1, source_target_pairs={{0,2},{2,0},{4,6},{6,4},{8,10},{10,8},{12,14},{14,12},{16,18},{18,... | collective-permute-start | bytes 1572872 | tf_op jit(solution)/shard_map/c_ux/ppermute | solution.py:865
  118.1 24.3 %collective-permute-start.14 = (bf16[128,3072]{1,0:T(8,128)(2,1)}, bf16[128,3072]{1,0:T(8,128)(2,1)}, u32[]{:S(2)}, u32[]{:S(2)}) collective-permute-start(bf16[128,3072]{1,0:T(8,128)(2,1)} %collective-permute-done.13.refs_11_), channel_id=1, source_target_pairs={{0,4},{2,6},{4,0},{6,2},{8,12},{10,14},{12,8},{14,10},{16,20},{18,... | collective-permute-start | bytes 2359304 | tf_op jit(solution)/shard_map/x_v/ppermute | solution.py:861
  119.2 10.2 %collective-permute-start.11 = (bf16[208,1024]{1,0:T(8,128)(2,1)}, bf16[208,1024]{1,0:T(8,128)(2,1)}, u32[]{:S(2)}, u32[]{:S(2)}) collective-permute-start(bf16[208,1024]{1,0:T(8,128)(2,1)} %get-tuple-element.113), channel_id=1, source_target_pairs={{0,1},{1,0},{2,3},{3,2},{4,5},{5,4},{6,7},{7,6},{8,9},{9,8},{10,11... | collective-permute-start | bytes 1277960 | tf_op jit(solution)/shard_map/y_pack/ppermute | solution.py:857
  120.7 14.3 %collective-permute-start.17 = (bf16[128,1024]{1,0:T(8,128)(2,1)}, bf16[128,1024]{1,0:T(8,128)(2,1)}, u32[]{:S(2)}, u32[]{:S(2)}) collective-permute-start(bf16[128,1024]{1,0:T(8,128)(2,1)} %get-tuple-element.132), channel_id=1, source_target_pairs={{0,1},{1,0},{2,3},{3,2},{4,5},{5,4},{6,7},{7,6},{8,9},{9,8},{10,11... | collective-permute-start | bytes 786440 | tf_op jit(solution)/shard_map/y_w/ppermute | solution.py:857
  135.0 22.9 %all-to-all-start.3 = ((bf16[32,16,512]{2,1,0:T(8,128)(2,1)}), bf16[32,16,512]{2,1,0:T(8,128)(2,1)}, u32[]{:S(2)}, u32[]{:S(2)}) async-start(bf16[32,16,512]{2,1,0:T(8,128)(2,1)} %get-tuple-element.139), calls=%async_computation.3 | async-start | bytes 1048576 | tf_op jit(solution)/shard_map/all_to_all | solution.py:1094
  142.0 3.2 %collective-permute-start.15 = (bf16[128,3072]{1,0:T(8,128)(2,1)}, bf16[128,3072]{1,0:T(8,128)(2,1)}, u32[]{:S(2)}, u32[]{:S(2)}) collective-permute-start(bf16[128,3072]{1,0:T(8,128)(2,1)} %collective-permute-done.13.refs_11_), channel_id=1, source_target_pairs={{0,2},{2,0},{4,6},{6,4},{8,10},{10,8},{12,14},{14,12},{16,18},{18,... | collective-permute-start | bytes 2359304 | tf_op jit(solution)/shard_map/c_vy/ppermute | solution.py:865
  142.4 3.4 %collective-permute-start.16 = (bf16[128,3072]{1,0:T(8,128)(2,1)}, bf16[128,3072]{1,0:T(8,128)(2,1)}, u32[]{:S(2)}, u32[]{:S(2)}) collective-permute-start(bf16[128,3072]{1,0:T(8,128)(2,1)} %collective-permute-done.14.refs_12_), channel_id=1, source_target_pairs={{0,2},{2,0},{4,6},{6,4},{8,10},{10,8},{12,14},{14,12},{16,18},{18,... | collective-permute-start | bytes 2359304 | tf_op jit(solution)/shard_map/c_vx/ppermute | solution.py:865
  142.6 12.5 %collective-permute-start.12 = (bf16[128,1024]{1,0:T(8,128)(2,1)}, bf16[128,1024]{1,0:T(8,128)(2,1)}, u32[]{:S(2)}, u32[]{:S(2)}) collective-permute-start(bf16[128,1024]{1,0:T(8,128)(2,1)} %get-tuple-element.118), channel_id=1, source_target_pairs={{0,1},{1,0},{2,3},{3,2},{4,5},{5,4},{6,7},{7,6},{8,9},{9,8},{10,11... | collective-permute-start | bytes 786440 | tf_op jit(solution)/shard_map/y_rest/ppermute | solution.py:857
  144.0 11.1 %collective-permute-start.18 = (bf16[128,1024]{1,0:T(8,128)(2,1)}, bf16[128,1024]{1,0:T(8,128)(2,1)}, u32[]{:S(2)}, u32[]{:S(2)}) collective-permute-start(bf16[128,1024]{1,0:T(8,128)(2,1)} %collective-permute-done.17.refs_9_), channel_id=1, source_target_pairs={{0,4},{2,6},{4,0},{6,2},{8,12},{10,14},{12,8},{14,10},{16,20},{18,... | collective-permute-start | bytes 786440 | tf_op jit(solution)/shard_map/x_w/ppermute | solution.py:861
  155.1 5.7 %collective-permute-start.19 = (bf16[128,1024]{1,0:T(8,128)(2,1)}, bf16[128,1024]{1,0:T(8,128)(2,1)}, u32[]{:S(2)}, u32[]{:S(2)}) collective-permute-start(bf16[128,1024]{1,0:T(8,128)(2,1)} %collective-permute-done.17.refs_9_), channel_id=1, source_target_pairs={{0,2},{2,0},{4,6},{6,4},{8,10},{10,8},{12,14},{14,12},{16,18},{18,... | collective-permute-start | bytes 786440 | tf_op jit(solution)/shard_map/c_wy/ppermute | solution.py:865
  156.3 4.5 %collective-permute-start.20 = (bf16[128,1024]{1,0:T(8,128)(2,1)}, bf16[128,1024]{1,0:T(8,128)(2,1)}, u32[]{:S(2)}, u32[]{:S(2)}) collective-permute-start(bf16[128,1024]{1,0:T(8,128)(2,1)} %collective-permute-done.18.refs_10_), channel_id=1, source_target_pairs={{0,2},{2,0},{4,6},{6,4},{8,10},{10,8},{12,14},{14,12},{16,18},{18,... | collective-permute-start | bytes 786440 | tf_op jit(solution)/shard_map/c_wx/ppermute | solution.py:865
  (1 other events, 2.3 us)
